TPU v7x, 32 devices: a whole 2x2x4 slice. The times are simulated.
32 devices in a mesh: groups: 2 (over y), lon: 4 (over z), chan: 4 (over x, core).
Axes of the slice: x: 2, y: 2, z: 4, core: 2. Of those that a mesh axis runs over, the one named last changes fastest.
Arguments:
- inputs: bfloat16 [2, 16, 8, 512], P(None, None, 'groups', 'lon'), parts along dimension 2, may hold values from -6 to 6
- hidden_init: bfloat16 [256, 8, 512], P('chan', 'groups', 'lon'), parts along dimension 1, may hold values from -0.8984375 to 0.8984375
- cell_init: float32 [256, 8, 512], P('chan', 'groups', 'lon'), parts along dimension 1, may hold values from -6 to 6
- w_input: bfloat16 [5, 5, 1024, 16], P(None, None, 'chan'), may hold values from -0.3125 to 0.3125
- w_hidden: bfloat16 [5, 5, 1024, 256], P(None, None, 'chan'), may hold values from -0.078125 to 0.078125
- gate_bias: float32 [1024], P('chan'), may hold values from -1 to 1
Outputs:
- hidden_out: bfloat16 [256, 8, 512], P('chan', 'groups', 'lon'), parts along dimension 1
- cell_out: float32 [256, 8, 512], P('chan', 'groups', 'lon'), parts along dimension 1
There are 2 independent parts, one for each index of `groups`. A program takes and returns all parts, laid end to end along the dimension named above; an argument that names none is the same for every part. Nothing has to cross between parts.
All inputs are finite; a program needn't handle non-finite values.
Results may differ from a plain program's by a relative error of at most 0.0019.
Values may be sent and summed in bfloat16 or wider, within the bound.
No kernel may reach another device: no remote copies, remote signals or barrier semaphores. Data moves between devices by JAX's collectives and lax.ppermute only.
A program may use at most 64 MiB of HBM per device.

v0:
```python
import jax
import jax.numpy as jnp
from jax import lax
from jax.sharding import PartitionSpec as P

STEPS = 2


def with_halo(cells, sides, width):
    for axis, dim in sides:
        count = lax.axis_size(axis)
        head = lax.slice_in_dim(cells, 0, width, axis=dim)
        tail = lax.slice_in_dim(cells, cells.shape[dim] - width, cells.shape[dim], axis=dim)
        cells = jnp.concatenate(
            [
                lax.ppermute(tail, axis, [(i, (i + 1) % count) for i in range(count)]),
                cells,
                lax.ppermute(head, axis, [((i + 1) % count, i) for i in range(count)]),
            ],
            axis=dim,
        )
    return cells


def pad_rows(field):
    return jnp.pad(field, ((0, 0), (2, 2), (0, 0)))


def conv_taps(padded, weights):
    depth = padded.shape[0]
    rows = padded.shape[1] - 4
    cols = padded.shape[2] - 4
    outputs = weights.shape[2]
    if depth < 128:
        windows = [
            padded[:, row_tap : row_tap + rows, col_tap : col_tap + cols].reshape(
                depth, rows * cols
            )
            for row_tap in range(5)
            for col_tap in range(5)
        ]
        stacked = jnp.concatenate(windows, axis=0)
        flat_weights = jnp.transpose(weights, (2, 0, 1, 3)).reshape(outputs, 25 * depth)
        total = jnp.dot(flat_weights, stacked, preferred_element_type=jnp.float32)
        return total.reshape(outputs, rows, cols)
    total = jnp.zeros((outputs, rows * cols), jnp.float32)
    for row_tap in range(5):
        for col_tap in range(5):
            window = padded[:, row_tap : row_tap + rows, col_tap : col_tap + cols].reshape(
                depth, rows * cols
            )
            total = total + jnp.dot(
                weights[row_tap, col_tap], window, preferred_element_type=jnp.float32
            )
    return total.reshape(outputs, rows, cols)


def shards(inputs, hidden_init, cell_init, w_input, w_hidden, gate_bias):
    hidden = hidden_init
    cell = cell_init
    for step in range(STEPS):
        step_input = with_halo(inputs[step], (("lon", 2),), 2)
        pre = conv_taps(pad_rows(step_input), w_input)
        whole = lax.all_gather(hidden, "chan", axis=0, tiled=True)
        rimmed = with_halo(whole, (("lon", 2),), 2)
        pre = pre + conv_taps(pad_rows(rimmed), w_hidden)
        pre = pre + gate_bias[:, None, None]
        pre = pre.reshape(-1, 4, pre.shape[1], pre.shape[2])
        in_gate = jax.nn.sigmoid(pre[:, 0])
        forget = jax.nn.sigmoid(pre[:, 1])
        update = jnp.tanh(pre[:, 2])
        out_gate = jax.nn.sigmoid(pre[:, 3])
        cell = forget * cell + in_gate * update
        hidden = (out_gate * jnp.tanh(cell)).astype(jnp.bfloat16)
    return (hidden, cell)


def solution(mesh):
    in_specs = (
        P(None, None, "groups", "lon"),
        P("chan", "groups", "lon"),
        P("chan", "groups", "lon"),
        P(None, None, "chan", None),
        P(None, None, "chan", None),
        P("chan"),
    )
    out_specs = (P("chan", "groups", "lon"), P("chan", "groups", "lon"))
    return jax.shard_map(shards, mesh=mesh, in_specs=in_specs, out_specs=out_specs, check_vma=False)
```

profile of v0, /device:TPU:0, one launch (start us, length us, event | category | flops | bytes accessed | tf_op | source)
XLA Modules:
  0.0 89.4 jit_solution(3993381534454433626)
XLA Ops:
  0.6 0.8 fusion.284
  1.5 3.0 %collective-permute-start.2 = (bf16[16,4,2]{2,1,0:T(4,128)(2,1)S(1)}, bf16[16,4,2]{2,1,0:T(4,128)(2,1)S(1)}, u32[]{:S(2)}, u32[]{:S(2)}) collective-permute-start(bf16[16,4,2]{2,1,0:T(4,128)(2,1)S(1)} %get-tuple-element.116), channel_id=1, source_target_pairs={{0,4},{4,8},{8,12},{12,0},{1,5},{5,9},{9,13},{13,1},{2,6},{6,10},{... | collective-permute-start | bytes 776 | tf_op jit(solution)/shard_map/ppermute | solution.py:16
  4.5 2.1 %collective-permute-start.3 = (bf16[16,4,2]{2,1,0:T(4,128)(2,1)S(1)}, bf16[16,4,2]{2,1,0:T(4,128)(2,1)S(1)}, u32[]{:S(2)}, u32[]{:S(2)}) collective-permute-start(bf16[16,4,2]{2,1,0:T(4,128)(2,1)S(1)} %get-tuple-element.117), channel_id=1, source_target_pairs={{4,0},{8,4},{12,8},{0,12},{5,1},{9,5},{13,9},{1,13},{6,2},{10,6},{... | collective-permute-start | bytes 776 | tf_op jit(solution)/shard_map/ppermute | solution.py:18
  6.6 6.1 %all_gather.6 = bf16[256,4,128]{2,1,0:T(4,128)(2,1)S(1)} all-gather(bf16[64,4,128]{2,1,0:T(4,128)(2,1)} %param.7), channel_id=1, replica_groups=mesh['groups'=2,'lon'=4,'chan'=4] {'chan'}, dimensions={0}, use_global_device_ids=true | all-gather | bytes 327680 | tf_op jit(solution)/shard_map/all_gather | solution.py:64
  13.1 3.8 %collective-permute-start.5 = (bf16[256,4,2]{2,1,0:T(4,128)(2,1)S(1)}, bf16[256,4,2]{2,1,0:T(4,128)(2,1)S(1)}, u32[]{:S(2)}, u32[]{:S(2)}) collective-permute-start(bf16[256,4,2]{2,1,0:T(4,128)(2,1)S(1)} %get-tuple-element.59), channel_id=1, source_target_pairs={{4,0},{8,4},{12,8},{0,12},{5,1},{9,5},{13,9},{1,13},{6,2},{10,6},{... | collective-permute-start | bytes 12296 | tf_op jit(solution)/shard_map/ppermute | solution.py:18
  17.0 0.8 add.253
  17.8 3.8 %collective-permute-start.1 = (bf16[16,4,2]{2,1,0:T(4,128)(2,1)S(1)}, bf16[16,4,2]{2,1,0:T(4,128)(2,1)S(1)}, u32[]{:S(2)}, u32[]{:S(2)}) collective-permute-start(bf16[16,4,2]{2,1,0:T(4,128)(2,1)S(1)} %get-tuple-element.113), channel_id=1, source_target_pairs={{4,0},{8,4},{12,8},{0,12},{5,1},{9,5},{13,9},{1,13},{6,2},{10,6},{... | collective-permute-start | bytes 776 | tf_op jit(solution)/shard_map/ppermute | solution.py:18
  22.0 7.6 %collective-permute-done = bf16[16,4,2]{2,1,0:T(4,128)(2,1)S(1)} collective-permute-done((bf16[16,4,2]{2,1,0:T(4,128)(2,1)S(1)}, bf16[16,4,2]{2,1,0:T(4,128)(2,1)S(1)}, u32[]{:S(2)}, u32[]{:S(2)}) %collective-permute-start) | collective-permute-done | bytes 288 | tf_op jit(solution)/shard_map/ppermute | solution.py:16
  30.9 0.7 copy-done.9
  31.7 0.7 copy-done.4
  32.3 0.7 copy-done.6
  33.0 1.1 %fusion.29 = bf16[256,8,132]{2,1,0:T(8,128)(2,1)S(1)} fusion(bf16[256,4,2]{2,1,0:T(4,128)(2,1)S(1)} %collective-permute-done.5, bf16[256,4,128]{2,1,0:T(4,128)(2,1)S(1)} %all_gather.6, bf16[256,4,2]{2,1,0:T(4,128)(2,1)S(1)} %collective-permute-done.4), kind=kLoop, calls=%fused_computation.83 | loop fusion | flops 3244032 | bytes 811008 | tf_op jit(solution)/shard_map/concatenate | solution.py:14
  34.2 2.7 %fusion.277 = (bf16[256,4,128]{2,1,0:T(4,128)(2,1)S(1)}, bf16[256,4,128]{2,1,0:T(4,128)(2,1)S(1)}, bf16[256,4,128]{2,1,0:T(4,128)(2,1)S(1)}, bf16[256,4,128]{2,1...) fusion(bf16[256,8,132]{2,1,0:T(8,128)(2,1)S(1)} %fusion.29), kind=kLoop, calls=%fused_computation.419 | loop fusion | bytes 9961472 | tf_op jit(solution)/shard_map/slice | solution.py:49
  39.8 0.7 pad_maximum_fusion.1
  44.8 0.5 fusion.13
  45.5 1.2 %fusion.2 = f32[256,512]{0,1:T(8,128)} fusion(f32[256,512]{0,1:T(8,128)S(1)} %fusion.14, bf16[400,512]{1,0:T(8,128)(2,1)S(1)} %constant_dynamic-update-slice_fusion.25, bf16[256,400]{0,1:T(8,128)(2,1)S(1)} %bitcast.617), kind=kOutput, calls=%fused_computation.26 | convolution fusion | flops 104988672 | bytes 1662976 | tf_op jit(solution)/shard_map/dot_general | solution.py:44
  46.7 2.0 %copy.32 = f32[256,512]{1,0:T(8,128)} copy(f32[256,512]{0,1:T(8,128)} %fusion.2) | data formatting | bytes 1048576 | tf_op jit(solution)/shard_map/add | solution.py:66
  48.7 2.0 %add.252 = f32[64,4,4,128]{3,2,1,0:T(4,128)} reshape(f32[256,512]{1,0:T(8,128)} %copy.32) | data formatting | bytes 1048576 | tf_op jit(solution)/shard_map/add | solution.py:66
  50.8 1.3 %copy_add_fusion.1 = f32[64,4,4,128]{3,0,2,1:T(8,128)S(1)} fusion(f32[64,4,4,128]{3,2,1,0:T(4,128)} %add.252, f32[64,4]{0,1:T(4,128)S(1)} %copy.33), kind=kLoop, calls=%fused_computation.89 | loop fusion | flops 131072 | bytes 1049600 | tf_op jit(solution)/shard_map/add | solution.py:67
  52.0 1.7 %fusion.216 = (bf16[64,4,128]{2,0,1:T(8,128)(2,1)S(1)}, f32[64,4,128]{2,0,1:T(8,128)}) fusion(f32[64,4,4,128]{3,0,2,1:T(8,128)S(1)} %copy_add_fusion.1, f32[64,4,128]{2,1,0:T(4,128)} %param.8), kind=kLoop, calls=%fused_computation.288 | loop fusion | flops 458752 | bytes 851968 | tf_op jit(solution)/shard_map/convert_element_type | solution.py:74
  53.8 5.8 %all_gather.7 = bf16[256,4,128]{2,1,0:T(4,128)(2,1)S(1)} all-gather(bf16[64,4,128]{2,1,0:T(4,128)(2,1)S(1)} %copy.36), channel_id=1, replica_groups=mesh['groups'=2,'lon'=4,'chan'=4] {'chan'}, dimensions={0}, use_global_device_ids=true | all-gather | bytes 327680 | tf_op jit(solution)/shard_map/all_gather | solution.py:64
  59.9 3.8 %collective-permute-start.7 = (bf16[256,4,2]{2,1,0:T(4,128)(2,1)S(1)}, bf16[256,4,2]{2,1,0:T(4,128)(2,1)S(1)}, u32[]{:S(2)}, u32[]{:S(2)}) collective-permute-start(bf16[256,4,2]{2,1,0:T(4,128)(2,1)S(1)} %get-tuple-element.56), channel_id=1, source_target_pairs={{4,0},{8,4},{12,8},{0,12},{5,1},{9,5},{13,9},{1,13},{6,2},{10,6},{... | collective-permute-start | bytes 12296 | tf_op jit(solution)/shard_map/ppermute | solution.py:18
  63.7 7.1 %collective-permute-done.6 = bf16[256,4,2]{2,1,0:T(4,128)(2,1)S(1)} collective-permute-done((bf16[256,4,2]{2,1,0:T(4,128)(2,1)S(1)}, bf16[256,4,2]{2,1,0:T(4,128)(2,1)S(1)}, u32[]{:S(2)}, u32[]{:S(2)}) %collective-permute-start.6) | collective-permute-done | bytes 4128 | tf_op jit(solution)/shard_map/ppermute | solution.py:16
  70.9 3.5 %collective-permute-done.7 = bf16[256,4,2]{2,1,0:T(4,128)(2,1)S(1)} collective-permute-done((bf16[256,4,2]{2,1,0:T(4,128)(2,1)S(1)}, bf16[256,4,2]{2,1,0:T(4,128)(2,1)S(1)}, u32[]{:S(2)}, u32[]{:S(2)}) %collective-permute-start.7) | collective-permute-done | bytes 4128 | tf_op jit(solution)/shard_map/ppermute | solution.py:18
  74.3 1.1 %select_maximum_fusion = bf16[256,8,132]{2,1,0:T(8,128)(2,1)S(1)} fusion(bf16[256,4,2]{2,1,0:T(4,128)(2,1)S(1)} %collective-permute-done.7, bf16[256,4,128]{2,1,0:T(4,128)(2,1)S(1)} %all_gather.7, bf16[256,4,2]{2,1,0:T(4,128)(2,1)S(1)} %collective-permute-done.6), kind=kLoop, calls=%fused_computation.77 | loop fusion | flops 3244032 | bytes 811008 | tf_op jit(solution)/shard_map/concatenate | solution.py:14
  75.4 2.6 %fusion.276 = (bf16[256,4,128]{2,1,0:T(4,128)(2,1)S(1)}, bf16[256,4,128]{2,1,0:T(4,128)(2,1)S(1)}, bf16[256,4,128]{2,1,0:T(4,128)(2,1)S(1)}, bf16[256,4,128]{2,1...) fusion(bf16[256,8,132]{2,1,0:T(8,128)(2,1)S(1)} %select_maximum, ...), kind=kLoop, calls=%fused_computation.418 | loop fusion | bytes 9961472 | tf_op jit(solution)/shard_map/slice | solution.py:49
  78.4 0.7 pad_maximum_fusion
  79.3 0.4 fusion.278
  86.5 0.4 fusion.22
  86.9 0.4 fusion.1
  88.0 0.7 copy.40
  88.8 0.7 copy.39
  (148 shorter events, 17.3 us)
Async XLA Ops:
  0.6 44.9 %copy-start = (bf16[5,5,256,16]{2,3,1,0:T(8,128)(2,1)S(1)}, bf16[5,5,256,16]{2,3,1,0:T(8,128)(2,1)}, u32[]{:S(2)}) copy-start(bf16[5,5,256,16]{2,3,1,0:T(8,128)(2,1)} %param.9) | copy-start | bytes 614404
  1.5 16.3 %collective-permute-start.2 = (bf16[16,4,2]{2,1,0:T(4,128)(2,1)S(1)}, bf16[16,4,2]{2,1,0:T(4,128)(2,1)S(1)}, u32[]{:S(2)}, u32[]{:S(2)}) collective-permute-start(bf16[16,4,2]{2,1,0:T(4,128)(2,1)S(1)} %get-tuple-element.116), channel_id=1, source_target_pairs={{0,4},{4,8},{8,12},{12,0},{1,5},{5,9},{9,13},{13,1},{2,6},{6,10},{... | collective-permute-start | bytes 776 | tf_op jit(solution)/shard_map/ppermute | solution.py:16
  4.5 17.1 %collective-permute-start.3 = (bf16[16,4,2]{2,1,0:T(4,128)(2,1)S(1)}, bf16[16,4,2]{2,1,0:T(4,128)(2,1)S(1)}, u32[]{:S(2)}, u32[]{:S(2)}) collective-permute-start(bf16[16,4,2]{2,1,0:T(4,128)(2,1)S(1)} %get-tuple-element.117), channel_id=1, source_target_pairs={{4,0},{8,4},{12,8},{0,12},{5,1},{9,5},{13,9},{1,13},{6,2},{10,6},{... | collective-permute-start | bytes 776 | tf_op jit(solution)/shard_map/ppermute | solution.py:18
  12.7 18.9 %copy-start.2 = (bf16[256,4,128]{2,1,0:T(4,128)(2,1)}, bf16[256,4,128]{2,1,0:T(4,128)(2,1)S(1)}, u32[]{:S(2)}) copy-start(bf16[256,4,128]{2,1,0:T(4,128)(2,1)S(1)} %all_gather.6) | copy-start | bytes 786436
  13.0 17.9 %collective-permute-start.4 = (bf16[256,4,2]{2,1,0:T(4,128)(2,1)S(1)}, bf16[256,4,2]{2,1,0:T(4,128)(2,1)S(1)}, u32[]{:S(2)}, u32[]{:S(2)}) collective-permute-start(bf16[256,4,2]{2,1,0:T(4,128)(2,1)S(1)} %get-tuple-element.58), channel_id=1, source_target_pairs={{0,4},{4,8},{8,12},{12,0},{1,5},{5,9},{9,13},{13,1},{2,6},{6,10},{... | collective-permute-start | bytes 12296 | tf_op jit(solution)/shard_map/ppermute | solution.py:16
  13.1 18.6 %collective-permute-start.5 = (bf16[256,4,2]{2,1,0:T(4,128)(2,1)S(1)}, bf16[256,4,2]{2,1,0:T(4,128)(2,1)S(1)}, u32[]{:S(2)}, u32[]{:S(2)}) collective-permute-start(bf16[256,4,2]{2,1,0:T(4,128)(2,1)S(1)} %get-tuple-element.59), channel_id=1, source_target_pairs={{4,0},{8,4},{12,8},{0,12},{5,1},{9,5},{13,9},{1,13},{6,2},{10,6},{... | collective-permute-start | bytes 12296 | tf_op jit(solution)/shard_map/ppermute | solution.py:18
  17.0 12.6 %collective-permute-start = (bf16[16,4,2]{2,1,0:T(4,128)(2,1)S(1)}, bf16[16,4,2]{2,1,0:T(4,128)(2,1)S(1)}, u32[]{:S(2)}, u32[]{:S(2)}) collective-permute-start(bf16[16,4,2]{2,1,0:T(4,128)(2,1)S(1)} %get-tuple-element.112), channel_id=1, source_target_pairs={{0,4},{4,8},{8,12},{12,0},{1,5},{5,9},{9,13},{13,1},{2,6},{6,10},{... | collective-permute-start | bytes 776 | tf_op jit(solution)/shard_map/ppermute | solution.py:16
  17.8 11.8 %collective-permute-start.1 = (bf16[16,4,2]{2,1,0:T(4,128)(2,1)S(1)}, bf16[16,4,2]{2,1,0:T(4,128)(2,1)S(1)}, u32[]{:S(2)}, u32[]{:S(2)}) collective-permute-start(bf16[16,4,2]{2,1,0:T(4,128)(2,1)S(1)} %get-tuple-element.113), channel_id=1, source_target_pairs={{4,0},{8,4},{12,8},{0,12},{5,1},{9,5},{13,9},{1,13},{6,2},{10,6},{... | collective-permute-start | bytes 776 | tf_op jit(solution)/shard_map/ppermute | solution.py:18
  30.9 0.8 copy-start.9
  31.6 0.7 copy-start.4
  32.3 0.7 copy-start.6
  34.1 2.8 %copy-start.1 = (bf16[5,5,256,256]{3,2,1,0:T(8,128)(2,1)S(1)}, bf16[5,5,256,256]{3,2,1,0:T(8,128)(2,1)}, u32[]{:S(2)}) copy-start(bf16[5,5,256,256]{3,2,1,0:T(8,128)(2,1)} %param.10) | copy-start | bytes 9830404
  37.8 2.0 %copy-start.3 = (bf16[256,4,128]{2,1,0:T(4,128)(2,1)S(1)}, bf16[256,4,128]{2,1,0:T(4,128)(2,1)}, u32[]{:S(2)}) copy-start(bf16[256,4,128]{2,1,0:T(4,128)(2,1)} %copy-done.2) | copy-start | bytes 786436
  37.8 2.0 %copy-start.5 = (bf16[256,4,2]{2,1,0:T(4,128)(2,1)S(1)}, bf16[256,4,2]{2,1,0:T(4,128)(2,1)}, u32[]{:S(2)}) copy-start(bf16[256,4,2]{2,1,0:T(4,128)(2,1)} %copy-done.4) | copy-start | bytes 12292
  38.1 2.5 %copy-start.7 = (bf16[256,4,2]{2,1,0:T(4,128)(2,1)S(1)}, bf16[256,4,2]{2,1,0:T(4,128)(2,1)}, u32[]{:S(2)}) copy-start(bf16[256,4,2]{2,1,0:T(4,128)(2,1)} %copy-done.6) | copy-start | bytes 12292
  50.8 13.0 %copy-start.10 = (bf16[400,512]{1,0:T(8,128)(2,1)S(1)}, bf16[400,512]{1,0:T(8,128)(2,1)}, u32[]{:S(2)}) copy-start(bf16[400,512]{1,0:T(8,128)(2,1)} %copy-done.9) | copy-start | bytes 1228804
  59.9 11.0 %collective-permute-start.6 = (bf16[256,4,2]{2,1,0:T(4,128)(2,1)S(1)}, bf16[256,4,2]{2,1,0:T(4,128)(2,1)S(1)}, u32[]{:S(2)}, u32[]{:S(2)}) collective-permute-start(bf16[256,4,2]{2,1,0:T(4,128)(2,1)S(1)} %get-tuple-element.55), channel_id=1, source_target_pairs={{0,4},{4,8},{8,12},{12,0},{1,5},{5,9},{9,13},{13,1},{2,6},{6,10},{... | collective-permute-start | bytes 12296 | tf_op jit(solution)/shard_map/ppermute | solution.py:16
  59.9 14.4 %collective-permute-start.7 = (bf16[256,4,2]{2,1,0:T(4,128)(2,1)S(1)}, bf16[256,4,2]{2,1,0:T(4,128)(2,1)S(1)}, u32[]{:S(2)}, u32[]{:S(2)}) collective-permute-start(bf16[256,4,2]{2,1,0:T(4,128)(2,1)S(1)} %get-tuple-element.56), channel_id=1, source_target_pairs={{4,0},{8,4},{12,8},{0,12},{5,1},{9,5},{13,9},{1,13},{6,2},{10,6},{... | collective-permute-start | bytes 12296 | tf_op jit(solution)/shard_map/ppermute | solution.py:18
  86.9 1.0 %copy-start.8 = (f32[64,4,128]{2,0,1:T(8,128)S(1)}, f32[64,4,128]{2,0,1:T(8,128)}, u32[]{:S(2)}) copy-start(f32[64,4,128]{2,0,1:T(8,128)} %get-tuple-element.7) | copy-start | bytes 393220
where the time goes:
time: 89.7 us; the launch traced here: 89.4 us
  waiting for transfers between devices  18.2 us (20%)
  local copies, waits for them, and re-layouts  17.9 us (20%)
  starting transfers between devices  16.7 us (19%)
  matrix products  15.6 us (17%)
  blocking collectives  11.9 us (13%)
  other arithmetic  7.48 us (8%)
  between operations  1.65 us (2%)
    ppermute x4, waiting for transfers between devices, with_halo(): lax.ppermute(tail, axis, [(i, (i + 1) % count) for i in range(count)])  14.7 us
    dot_general x50, matrix products, conv_taps(): jnp.dot(weights[row_tap, col_tap], window, preferred_element_type=jnp.flo...  14.1 us
    ppermute x4, starting transfers between devices, with_halo(): lax.ppermute(head, axis, [((i + 1) % count, i) for i in range(count)])  13.5 us
    all_gather x2, blocking collectives, shards(): whole = lax.all_gather(hidden, 'chan', axis=0, tiled=True)  11.9 us
    slice x10, local copies, waits for them, and re-layouts, conv_taps(): padded[:, row_tap:row_tap + rows, col_tap:col_tap + cols]  6.91 us
    add x4, local copies, waits for them, and re-layouts, shards(): pre = pre + conv_taps(pad_rows(rimmed), w_hidden)  4.42 us
    concatenate x8, other arithmetic, with_halo(): jnp.concatenate([lax.ppermute(tail, axis, [(i, (i + 1) % count) for i in...  4.15 us
    unnamed x72, local copies, waits for them, and re-layouts  3.86 us
  transfers between devices with their start and end apart: 8, of which 3 were waited for; matrix products, arithmetic and copies ran while one was open for 3% of the time, Pallas kernels for 0%

commit v1 on v0

v1 whole, which is shorter than its diff:
```python
import functools

import jax
import jax.numpy as jnp
from jax import lax
from jax.experimental import pallas as pl
from jax.experimental.pallas import tpu as pltpu
from jax.sharding import PartitionSpec as P

STEPS = 2
FOLD = 16
F32, BF16 = jnp.float32, jnp.bfloat16


def lanes(rows):
    return lax.broadcasted_iota(jnp.int32, (rows, 128), 1)


def roll(x, by):
    by = by % 128
    return pltpu.roll(x, by, 1) if by else x


def unfold(block, channels):
    return jnp.concatenate(
        [roll(block[8 * (i // 4) : 8 * (i // 4) + 8], -32 * (i % 4)) for i in range(channels // 8)], axis=0
    )


def fold(field):
    lane = lanes(8)
    parts = [jnp.zeros((8, 128), F32) for _ in range(FOLD // 8)]
    for i in range(field.shape[0] // 8):
        base = 32 * (i % 4)
        here = (lane >= base) & (lane < base + 32)
        parts[i // 4] = jnp.where(here, roll(field[8 * i : 8 * i + 8], base), parts[i // 4])
    return jnp.concatenate(parts, axis=0)


def edges_of(rows, groups, vectors):
    lane = lanes(8)
    left = [jnp.zeros((8, 128), F32) for _ in range(vectors)]
    right = [jnp.zeros((8, 128), F32) for _ in range(vectors)]
    for i in range(groups):
        for y in range(4):
            base = 32 * (i % 4) + 8 * y
            moved = roll(rows(i, y), base + 4)
            left[i // 4] = jnp.where((lane >= base + 4) & (lane < base + 8), moved, left[i // 4])
            right[i // 4] = jnp.where((lane >= base) & (lane < base + 4), moved, right[i // 4])
    return jnp.concatenate(left, axis=0), jnp.concatenate(right, axis=0)


def pack_kernel(hid, cell, inp, to_left, to_right, main, hid32, inp32):
    ch = hid.shape[0] // 4
    hid32[...] = hid[...].astype(F32)
    inp32[...] = inp[...].astype(F32)
    hl, hr = edges_of(lambda i, y: hid32[pl.ds(32 * i + y, 8, stride=4), :], ch // 8, 2)
    cl, cr = edges_of(lambda i, y: cell[pl.ds(32 * i + y, 8, stride=4), :], ch // 8, 2)
    il, ir = edges_of(lambda i, y: inp32[pl.ds(32 * i + y, 8, stride=4), :], inp.shape[0] // 32, 1)
    to_left[0:FOLD] = hl + roll(cl, -4)
    to_left[FOLD:] = il
    to_right[0:FOLD] = hr + roll(cr, 4)
    to_right[FOLD:] = ir
    for y in range(4):
        main[y * ch : (y + 1) * ch, :] = hid32[pl.ds(y, ch, stride=4), :].astype(BF16)


def join_kernel(main, from_left, from_right, out):
    n = main.shape[0]
    out[0:n] = main[...]
    low = (lanes(FOLD) & 7) < 4
    out[n : n + FOLD] = jnp.where(low, from_left[0:FOLD], from_right[0:FOLD]).astype(BF16)


def windows(row, halo, y):
    lane = lanes(row.shape[0])
    ring = roll(halo, -(8 * y + 4))
    out = []
    for d in range(-2, 3):
        if d == 0:
            out.append(row)
        else:
            other = lane >= 128 + d if d < 0 else lane < d
            out.append(roll(jnp.where(other, ring, row), -d))
    return out


def strips(rows, halo):
    lane = lanes(halo.shape[0])
    low, left = (lane & 7) < 4, lane < 64
    own = jnp.zeros_like(halo)
    for y in range(4):
        here = (lane >= 8 * y + 16) & (lane < 8 * y + 24)
        own = jnp.where(here, roll(rows[y], 8 * y + 20), own)
    rim = jnp.where(lane < 32, halo, jnp.zeros_like(halo))
    return jnp.where(
        left, jnp.where(low, roll(rim, 16), own), jnp.where(low, roll(own, 64), roll(rim, 80))
    )


def sigmoid(x):
    return 0.5 * jnp.tanh(0.5 * x) + 0.5


def gates(pre, ch, at, cell):
    part = [pre[at, pl.ds(g, ch, stride=4), :] for g in range(4)]
    cell = sigmoid(part[1]) * cell + sigmoid(part[0]) * jnp.tanh(part[2])
    return sigmoid(part[3]) * jnp.tanh(cell), cell


def step_kernel(step, *refs):
    last = step == STEPS - 1
    gathered, from_left, from_right, inp, cell, w, wx, bias = refs[:8]
    hid_out, cell_out, xs, xi, wxb, pre, inp32 = refs[8:15]
    shards, ch = gathered.shape[0], (gathered.shape[1] - FOLD) // 4
    depth, cin = shards * ch, inp.shape[0] // (4 * STEPS)
    taps = 25 * cin
    rows = [
        jnp.concatenate([gathered[c, y * ch : (y + 1) * ch, :] for c in range(shards)], axis=0) for y in range(4)
    ]
    halo = jnp.concatenate(
        [unfold(gathered[c, 4 * ch : 4 * ch + FOLD, :].astype(F32), ch) for c in range(shards)], axis=0
    ).astype(BF16)
    for b in range(5):
        xs[b, :, 0:128] = jnp.zeros((depth, 128), BF16)
        xs[b, :, 640:768] = jnp.zeros((depth, 128), BF16)
    for y in range(4):
        for b, window in enumerate(windows(rows[y], halo, y)):
            xs[b, :, 128 * (y + 1) : 128 * (y + 2)] = window
    inp32[...] = inp[...].astype(F32)
    irows = [inp32[pl.ds(4 * cin * step + y, cin, stride=4), :].astype(BF16) for y in range(4)]
    low = (lanes(8) & 7) < 4
    iblock = jnp.where(low, from_left[FOLD:], from_right[FOLD:])
    first = step * cin // 8
    ihalo = jnp.concatenate([roll(iblock, -32 * i) for i in range(first, first + cin // 8)], axis=0).astype(BF16)
    iwin = [windows(irows[y], ihalo, y) for y in range(4)]
    for a in range(5):
        for b in range(5):
            at = cin * (5 * a + b)
            for y in range(4):
                r = y + a - 2
                xi[at : at + cin, 128 * y : 128 * (y + 1)] = (
                    iwin[r][b] if 0 <= r < 4 else jnp.zeros((cin, 128), BF16)
                )
    count = xi.shape[1]
    ones = lax.broadcasted_iota(jnp.int32, (16, count), 0) < 3
    xi[taps : taps + 16, :] = jnp.where(ones, 1.0, 0.0).astype(BF16)
    wxb[0:taps, :] = wx[...]
    b0 = bias[...]
    b1 = b0.astype(BF16).astype(F32)
    b2 = (b0 - b1).astype(BF16).astype(F32)
    b3 = b0 - b1 - b2
    sub = lax.broadcasted_iota(jnp.int32, (16, wxb.shape[1]), 0)
    wxb[taps : taps + 16, :] = jnp.where(
        sub == 0, b1, jnp.where(sub == 1, b2, jnp.where(sub == 2, b3, 0.0))
    ).astype(BF16)
    if not last:
        istrip = strips(irows, ihalo)
        for a in range(5):
            for b in range(5):
                at = cin * (5 * a + b)
                xi[at : at + cin, 512:640] = roll(istrip, -(8 * (a - 2) + b - 2))
    drive = (((0,), (0,)), ((), ()))
    for pair in range(2):
        terms = [(a, b, 2 * pair + a - 2) for a in range(5) for b in range(5) if -2 < 2 * pair + a - 2 < 4]
        left = jnp.concatenate([w[a, b] for a, b, _ in terms], axis=1)
        right = jnp.concatenate([xs[b, :, 128 * (lo + 1) : 128 * (lo + 3)] for _, b, lo in terms], axis=0)
        at = 256 * pair
        total = jnp.dot(left, right, preferred_element_type=F32) + lax.dot_general(
            wxb[...], xi[:, at : at + 256], drive, preferred_element_type=F32
        )
        pre[2 * pair] = total[:, 0:128]
        pre[2 * pair + 1] = total[:, 128:256]
    for y in range(4):
        before = cell[pl.ds(y, ch, stride=4), :] if step == 0 else cell[y * ch : (y + 1) * ch, :]
        h, c = gates(pre, ch, y, before)
        if last:
            cell_out[pl.ds(y, ch, stride=4), :] = c
            refs[15][pl.ds(y, ch, stride=4), :] = h
        else:
            cell_out[y * ch : (y + 1) * ch, :] = c
            hid_out[y * ch : (y + 1) * ch, :] = h.astype(BF16)
    if last:
        hid_out[...] = refs[15][...].astype(BF16)
        return
    strip = strips(rows, halo)
    stack = jnp.concatenate([roll(strip, -8 * (a - 2)) for a in range(5)], axis=0)
    total = lax.dot_general(wxb[...], xi[:, 512:640], drive, preferred_element_type=F32)
    for b in range(5):
        left = jnp.concatenate([w[a, b] for a in range(5)], axis=1)
        total = total + roll(jnp.dot(left, stack, preferred_element_type=F32), -(b - 2))
    pre[4] = total
    lane = lanes(ch)
    near = lane < 64
    cells = unfold(jnp.where((lanes(FOLD) & 7) < 4, from_right[0:FOLD], from_left[0:FOLD]), ch)
    h, _ = gates(pre, ch, 4, jnp.where(near, roll(cells, 12), roll(cells, 84)))
    h = jnp.where((lane & 7) < 4, roll(h, -16), roll(h, -80))
    hid_out[4 * ch : 4 * ch + FOLD, :] = fold(h).astype(BF16)


def call(kernel, outs, scratch, *args):
    return pl.pallas_call(
        kernel,
        out_shape=[jax.ShapeDtypeStruct(s, d) for s, d in outs],
        in_specs=[pl.BlockSpec(memory_space=pltpu.VMEM)] * len(args),
        out_specs=[pl.BlockSpec(memory_space=pltpu.VMEM)] * len(outs),
        scratch_shapes=[pltpu.VMEM(s, d) for s, d in scratch],
        compiler_params=pltpu.CompilerParams(vmem_limit_bytes=24 << 20),
    )(*args)


def shards(inputs, hidden_init, cell_init, w_input, w_hidden, gate_bias):
    ch, rows, cols = hidden_init.shape
    gate = 4 * ch
    depth = w_hidden.shape[3]
    cin = w_input.shape[3]
    hid = hidden_init.reshape(ch * rows, cols)
    cell = cell_init.reshape(ch * rows, cols)
    inp = inputs.reshape(-1, cols)
    wx = jnp.transpose(w_input, (0, 1, 3, 2)).reshape(25 * cin, gate)
    bias = gate_bias.reshape(1, gate)
    to_left, to_right, main = call(
        pack_kernel,
        [((FOLD + 8, 128), F32), ((FOLD + 8, 128), F32), ((4 * ch, 128), BF16)],
        [((4 * ch, 128), F32), (inp.shape, F32)],
        hid, cell, inp,
    )
    n = lax.axis_size("lon")
    from_right = lax.ppermute(to_left, "lon", [((i + 1) % n, i) for i in range(n)])
    from_left = lax.ppermute(to_right, "lon", [(i, (i + 1) % n) for i in range(n)])
    (field,) = call(join_kernel, [((4 * ch + FOLD, 128), BF16)], [], main, from_left, from_right)
    for step in range(STEPS):
        last = step == STEPS - 1
        gathered = lax.all_gather(field, "chan", axis=0)
        wide = 512 if last else 640
        scratch = [
            ((5, depth, 768), BF16),
            ((25 * cin + 16, wide), BF16),
            ((25 * cin + 16, gate), BF16),
            ((wide // 128, gate, 128), F32),
            (inp.shape, F32),
        ]
        if last:
            scratch.append(((4 * ch, 128), F32))
        field, cell = call(
            functools.partial(step_kernel, step),
            [((4 * ch + (0 if last else FOLD), 128), BF16), ((4 * ch, 128), F32)],
            scratch,
            gathered, from_left, from_right, inp, cell, w_hidden, wx, bias,
        )
    return field.reshape(ch, rows, cols), cell.reshape(ch, rows, cols)


def solution(mesh):
    in_specs = (
        P(None, None, "groups", "lon"),
        P("chan", "groups", "lon"),
        P("chan", "groups", "lon"),
        P(None, None, "chan", None),
        P(None, None, "chan", None),
        P("chan"),
    )
    out_specs = (P("chan", "groups", "lon"), P("chan", "groups", "lon"))
    return jax.shard_map(shards, mesh=mesh, in_specs=in_specs, out_specs=out_specs, check_vma=False)
```

time: 89.7 us -> 34 us (0.38)
  waiting for transfers between devices: 18.2 us -> 1.73 us
  matrix products: 15.6 us -> 0 us
  starting transfers between devices: 16.7 us -> 5.13 us
  local copies, waits for them, and re-layouts: 17.9 us -> 7.74 us
  other arithmetic: 7.48 us -> 0 us
  Pallas kernels: 0 us -> 6.44 us
  between operations: 1.65 us -> 0.66 us
    ppermute x8 -> x2, waiting for transfers between devices: 18.2 us -> 1.73 us  [the longest x1 1.71 us: shards(): lax.ppermute(to_right, 'lon', [(i, (i + 1) % n) for i in range(n)])]
    dot_general x52 -> x0, matrix products: 15.6 us -> none  [the longest x50 14.1 us: conv_taps(): jnp.dot(weights[row_tap, col_tap], window, preferred_element_type=jnp.flo...]
    ppermute x8 -> x2, starting transfers between devices: 16.7 us -> 5.13 us  [the longest x1 3.04 us: shards(): lax.ppermute(to_right, 'lon', [(i, (i + 1) % n) for i in range(n)])]
    slice x15 -> x0, local copies, waits for them, and re-layouts: 8.36 us -> none  [the longest x10 6.91 us: conv_taps(): padded[:, row_tap:row_tap + rows, col_tap:col_tap + cols]]
    pallas_call x0 -> x4, Pallas kernels: none -> 6.44 us  [call(): pl.pallas_call(kernel, out_shape=[jax.ShapeDtypeStruct(s, d) for s, d in...]
    add x6 -> x0, local copies, waits for them, and re-layouts: 5.27 us -> none  [the longest x4 4.42 us: shards(): pre = pre + conv_taps(pad_rows(rimmed), w_hidden)]
    concatenate x8 -> x0, other arithmetic: 4.15 us -> none  [with_halo(): jnp.concatenate([lax.ppermute(tail, axis, [(i, (i + 1) % count) for i in...]
    unnamed x72 -> x22, local copies, waits for them, and re-layouts: 3.86 us -> 7.74 us
  transfers between devices with their start and end apart: 8 -> 2, of which waited for: 3 -> 1; matrix products, arithmetic and copies ran while one was open for 3% -> 0% of each run, Pallas kernels for 0% -> 0%
where the time goes in v1:
time: 34 us; the launch traced here: 33.6 us
  blocking collectives  11.9 us (35%)
  local copies, waits for them, and re-layouts  7.74 us (23%)
  Pallas kernels  6.44 us (19%)
  starting transfers between devices  5.13 us (15%)
  waiting for transfers between devices  1.73 us (5%)
  between operations  0.66 us (2%)
    all_gather x2, blocking collectives, shards(): gathered = lax.all_gather(field, 'chan', axis=0)  11.9 us
    unnamed x22, local copies, waits for them, and re-layouts  7.74 us
    pallas_call x4, Pallas kernels, call(): pl.pallas_call(kernel, out_shape=[jax.ShapeDtypeStruct(s, d) for s, d in...  6.44 us
    ppermute x1, starting transfers between devices, shards(): lax.ppermute(to_right, 'lon', [(i, (i + 1) % n) for i in range(n)])  3.04 us
    ppermute x1, starting transfers between devices, shards(): lax.ppermute(to_left, 'lon', [((i + 1) % n, i) for i in range(n)])  2.09 us
    ppermute x1, waiting for transfers between devices, shards(): lax.ppermute(to_right, 'lon', [(i, (i + 1) % n) for i in range(n)])  1.71 us
  transfers between devices with their start and end apart: 2, of which 1 were waited for; matrix products, arithmetic and copies ran while one was open for 0% of the time, Pallas kernels for 0%

profile of v1, /device:TPU:0, one launch (start us, length us, event | category | flops | bytes accessed | tf_op | source)
XLA Modules:
  0.0 33.6 jit_solution(16340316578206245970)
XLA Ops:
  0.6 0.0 copy-start.3
  0.6 0.0 copy-start.4
  0.7 0.9 %copy-done.4 = f32[64,4,128]{2,1,0:T(4,128)S(1)} copy-done((f32[64,4,128]{2,1,0:T(4,128)S(1)}, f32[64,4,128]{2,1,0:T(4,128)}, u32[]{:S(2)}) %copy-start.4) | copy-done | bytes 131096
  1.6 0.0 copy-start.6
  1.6 0.8 %copy-done.6 = bf16[2,16,4,128]{3,2,1,0:T(4,128)(2,1)S(1)} copy-done((bf16[2,16,4,128]{3,2,1,0:T(4,128)(2,1)S(1)}, bf16[2,16,4,128]{3,2,1,0:T(4,128)(2,1)}, u32[]{:S(2)}) %copy-start.6) | copy-done | bytes 32792
  2.3 0.0 copy-start.8
  2.3 0.8 %copy-done.8 = bf16[64,4,128]{2,1,0:T(4,128)(2,1)S(1)} copy-done((bf16[64,4,128]{2,1,0:T(4,128)(2,1)S(1)}, bf16[64,4,128]{2,1,0:T(4,128)(2,1)}, u32[]{:S(2)}) %copy-start.8) | copy-done | bytes 65560
  3.2 0.0 copy-start.10
  3.2 0.2 shard_map.77
  3.4 3.0 %collective-permute-start = (f32[24,128]{1,0:T(8,128)S(1)}, f32[24,128]{1,0:T(8,128)S(1)}, u32[]{:S(2)}, u32[]{:S(2)}) collective-permute-start(f32[24,128]{1,0:T(8,128)S(1)} %get-tuple-element.10), channel_id=1, source_target_pairs={{0,4},{4,8},{8,12},{12,0},{1,5},{5,9},{9,13},{13,1},{2,6},{6,10},{... | collective-permute-start | bytes 36872 | tf_op jit(solution)/shard_map/ppermute | solution.py:230
  6.4 2.1 %collective-permute-start.1 = (f32[24,128]{1,0:T(8,128)S(1)}, f32[24,128]{1,0:T(8,128)S(1)}, u32[]{:S(2)}, u32[]{:S(2)}) collective-permute-start(f32[24,128]{1,0:T(8,128)S(1)} %get-tuple-element.11), channel_id=1, source_target_pairs={{4,0},{8,4},{12,8},{0,12},{5,1},{9,5},{13,9},{1,13},{6,2},{10,6},{... | collective-permute-start | bytes 36872 | tf_op jit(solution)/shard_map/ppermute | solution.py:229
  8.5 1.7 %collective-permute-done.from_left.refs_1_ = f32[24,128]{1,0:T(8,128)S(1)} collective-permute-done((f32[24,128]{1,0:T(8,128)S(1)}, f32[24,128]{1,0:T(8,128)S(1)}, u32[]{:S(2)}, u32[]{:S(2)}) %collective-permute-start) | collective-permute-done | bytes 12320 | tf_op jit(solution)/shard_map/ppermute | solution.py:230
  10.2 0.0 collective-permute-done.1.from_right.refs_2_
  10.3 5.9 %all-gather = bf16[1088,128]{1,0:T(8,128)(2,1)S(1)} all-gather(bf16[272,128]{1,0:T(8,128)(2,1)S(1)} %shard_map.78), channel_id=2, replica_groups=mesh['groups'=2,'lon'=4,'chan'=4] {'chan'}, dimensions={0}, use_global_device_ids=true | all-gather | bytes 348160 | tf_op jit(solution)/shard_map/all_gather | solution.py:234
  16.2 0.0 copy-start
  16.2 1.9 %copy-done = bf16[5,5,256,256]{3,2,1,0:T(8,128)(2,1)S(1)} copy-done((bf16[5,5,256,256]{3,2,1,0:T(8,128)(2,1)S(1)}, bf16[5,5,256,256]{3,2,1,0:T(8,128)(2,1)}, u32[]{:S(2)}) %copy-start) | copy-done | bytes 3276824
  18.1 0.0 copy-start.2
  18.1 0.9 %copy-done.2 = bf16[5,5,256,16]{2,3,1,0:T(8,128)(2,1)S(1)} copy-done((bf16[5,5,256,16]{2,3,1,0:T(8,128)(2,1)S(1)}, bf16[5,5,256,16]{2,3,1,0:T(8,128)(2,1)}, u32[]{:S(2)}) %copy-start.2) | copy-done | bytes 204824
  19.0 0.0 copy-start.5
  19.1 0.9 %copy-done.5 = f32[64,4,128]{2,1,0:T(4,128)S(1)} copy-done((f32[64,4,128]{2,1,0:T(4,128)S(1)}, f32[64,4,128]{2,1,0:T(4,128)}, u32[]{:S(2)}) %copy-start.5) | copy-done | bytes 131096
  20.0 0.0 copy-start.7
  20.0 0.8 %copy-done.7 = bf16[2,16,4,128]{3,2,1,0:T(4,128)(2,1)S(1)} copy-done((bf16[2,16,4,128]{3,2,1,0:T(4,128)(2,1)S(1)}, bf16[2,16,4,128]{3,2,1,0:T(4,128)(2,1)}, u32[]{:S(2)}) %copy-start.7) | copy-done | bytes 32792
  20.7 0.0 copy-start.9
  20.7 0.7 %copy-done.9 = f32[256]{0:T(256)S(1)} copy-done((f32[256]{0:T(256)S(1)}, f32[256]{0:T(256)}, u32[]{:S(2)}) %copy-start.9) | copy-done | bytes 1048
  21.4 0.0 copy-start.1
  21.4 3.3 %shard_map.79 = (bf16[272,128]{1,0:T(8,128)(2,1)S(1)}, f32[256,128]{1,0:T(8,128)S(1)}) custom-call(bf16[4,272,128]{2,1,0:T(8,128)(2,1)S(1)} %bitcast.12, f32[24,128]{1,0:T(8,128)S(1)} %collective-permute-done.from_left.refs_1_, f32[24,128]{1,0:T(8,128)S(1)} %collective-permute-done.1.from_right.refs_2_, bf16[128,128]{1,0:T(8,128)(2,1)S(1)} %bitcast.18, ...), custom_call_target="tpu_custom_call" | custom-call | tf_op jit(solution)/shard_map/pallas_call | solution.py:202
  24.7 5.9 %all-gather.1 = bf16[1088,128]{1,0:T(8,128)(2,1)S(1)} all-gather(bf16[272,128]{1,0:T(8,128)(2,1)S(1)} %get-tuple-element.12), channel_id=3, replica_groups=mesh['groups'=2,'lon'=4,'chan'=4] {'chan'}, dimensions={0}, use_global_device_ids=true | all-gather | bytes 348160 | tf_op jit(solution)/shard_map/all_gather | solution.py:234
  30.7 0.0 copy-done.3
  30.7 0.0 copy-done.10
  30.7 0.0 copy-done.1
  30.7 2.9 %shard_map.80 = (bf16[256,128]{1,0:T(8,128)(2,1)}, f32[256,128]{1,0:T(8,128)}) custom-call(bf16[4,272,128]{2,1,0:T(8,128)(2,1)S(1)} %bitcast.11, f32[24,128]{1,0:T(8,128)S(1)} %collective-permute-done.from_left.refs_1_, f32[24,128]{1,0:T(8,128)S(1)} %collective-permute-done.1.from_right.refs_2_, bf16[128,128]{1,0:T(8,128)(2,1)S(1)} %bitcast.19, ...), custom_call_target="tpu_custom_call" | custom-call | tf_op jit(solution)/shard_map/pallas_call | solution.py:202
  (1 shorter events, 0.0 us)
Async XLA Ops:
  0.6 30.1 %copy-start.3 = (bf16[5,5,256,16]{2,3,1,0:T(8,128)(2,1)S(1)}, bf16[5,5,256,16]{2,3,1,0:T(8,128)(2,1)}, u32[]{:S(2)}) copy-start(bf16[5,5,256,16]{2,3,1,0:T(8,128)(2,1)} %param.9) | copy-start | bytes 614404
  0.6 0.9 %copy-start.4 = (f32[64,4,128]{2,1,0:T(4,128)S(1)}, f32[64,4,128]{2,1,0:T(4,128)}, u32[]{:S(2)}) copy-start(f32[64,4,128]{2,1,0:T(4,128)} %param.8) | copy-start | bytes 393220
  1.6 0.8 %copy-start.6 = (bf16[2,16,4,128]{3,2,1,0:T(4,128)(2,1)S(1)}, bf16[2,16,4,128]{3,2,1,0:T(4,128)(2,1)}, u32[]{:S(2)}) copy-start(bf16[2,16,4,128]{3,2,1,0:T(4,128)(2,1)} %param.6) | copy-start | bytes 98308
  2.3 0.8 %copy-start.8 = (bf16[64,4,128]{2,1,0:T(4,128)(2,1)S(1)}, bf16[64,4,128]{2,1,0:T(4,128)(2,1)}, u32[]{:S(2)}) copy-start(bf16[64,4,128]{2,1,0:T(4,128)(2,1)} %param.7) | copy-start | bytes 196612
  3.2 27.5 %copy-start.10 = (f32[256]{0:T(256)S(1)}, f32[256]{0:T(256)}, u32[]{:S(2)}) copy-start(f32[256]{0:T(256)} %param.11) | copy-start | bytes 3076
  3.4 6.8 %collective-permute-start = (f32[24,128]{1,0:T(8,128)S(1)}, f32[24,128]{1,0:T(8,128)S(1)}, u32[]{:S(2)}, u32[]{:S(2)}) collective-permute-start(f32[24,128]{1,0:T(8,128)S(1)} %get-tuple-element.10), channel_id=1, source_target_pairs={{0,4},{4,8},{8,12},{12,0},{1,5},{5,9},{9,13},{13,1},{2,6},{6,10},{... | collective-permute-start | bytes 36872 | tf_op jit(solution)/shard_map/ppermute | solution.py:230
  6.4 3.8 %collective-permute-start.1 = (f32[24,128]{1,0:T(8,128)S(1)}, f32[24,128]{1,0:T(8,128)S(1)}, u32[]{:S(2)}, u32[]{:S(2)}) collective-permute-start(f32[24,128]{1,0:T(8,128)S(1)} %get-tuple-element.11), channel_id=1, source_target_pairs={{4,0},{8,4},{12,8},{0,12},{5,1},{9,5},{13,9},{1,13},{6,2},{10,6},{... | collective-permute-start | bytes 36872 | tf_op jit(solution)/shard_map/ppermute | solution.py:229
  16.2 1.9 %copy-start = (bf16[5,5,256,256]{3,2,1,0:T(8,128)(2,1)S(1)}, bf16[5,5,256,256]{3,2,1,0:T(8,128)(2,1)}, u32[]{:S(2)}) copy-start(bf16[5,5,256,256]{3,2,1,0:T(8,128)(2,1)} %refs_5_.3) | copy-start | bytes 9830404
  18.1 0.9 %copy-start.2 = (bf16[5,5,256,16]{2,3,1,0:T(8,128)(2,1)S(1)}, bf16[5,5,256,16]{2,3,1,0:T(8,128)(2,1)}, u32[]{:S(2)}) copy-start(bf16[5,5,256,16]{2,3,1,0:T(8,128)(2,1)} %param.9) | copy-start | bytes 614404
  19.0 0.9 %copy-start.5 = (f32[64,4,128]{2,1,0:T(4,128)S(1)}, f32[64,4,128]{2,1,0:T(4,128)}, u32[]{:S(2)}) copy-start(f32[64,4,128]{2,1,0:T(4,128)} %param.8) | copy-start | bytes 393220
  20.0 0.8 %copy-start.7 = (bf16[2,16,4,128]{3,2,1,0:T(4,128)(2,1)S(1)}, bf16[2,16,4,128]{3,2,1,0:T(4,128)(2,1)}, u32[]{:S(2)}) copy-start(bf16[2,16,4,128]{3,2,1,0:T(4,128)(2,1)} %param.6) | copy-start | bytes 98308
  20.7 0.7 %copy-start.9 = (f32[256]{0:T(256)S(1)}, f32[256]{0:T(256)}, u32[]{:S(2)}) copy-start(f32[256]{0:T(256)} %param.11) | copy-start | bytes 3076
  21.4 9.3 %copy-start.1 = (bf16[5,5,256,256]{3,2,1,0:T(8,128)(2,1)S(1)}, bf16[5,5,256,256]{3,2,1,0:T(8,128)(2,1)}, u32[]{:S(2)}) copy-start(bf16[5,5,256,256]{3,2,1,0:T(8,128)(2,1)} %refs_5_.3) | copy-start | bytes 9830404

commit v2 on v1

--- a/solution.py
+++ b/solution.py
@@ -50,8 +50,14 @@
     return jnp.concatenate(left, axis=0), jnp.concatenate(right, axis=0)
 
 
-def pack_kernel(hid, cell, inp, to_left, to_right, main, hid32, inp32):
+def pack_kernel(hid_far, cell_far, inp_far, to_left, to_right, main, hid, cell, inp, hid32, inp32, arrived):
     ch = hid.shape[0] // 4
+    pairs = ((hid_far, hid), (cell_far, cell), (inp_far, inp))
+    copies = [pltpu.make_async_copy(a, b, arrived.at[i]) for i, (a, b) in enumerate(pairs)]
+    for copy in copies:
+        copy.start()
+    for copy in copies:
+        copy.wait()
     hid32[...] = hid[...].astype(F32)
     inp32[...] = inp[...].astype(F32)
     hl, hr = edges_of(lambda i, y: hid32[pl.ds(32 * i + y, 8, stride=4), :], ch // 8, 2)
@@ -198,15 +204,17 @@
     hid_out[4 * ch : 4 * ch + FOLD, :] = fold(h).astype(BF16)
 
 
-def call(kernel, outs, scratch, *args):
+def call(kernel, outs, scratch, *args, far=0, us=1):
     return pl.pallas_call(
         kernel,
         out_shape=[jax.ShapeDtypeStruct(s, d) for s, d in outs],
-        in_specs=[pl.BlockSpec(memory_space=pltpu.VMEM)] * len(args),
+        in_specs=[pl.BlockSpec(memory_space=pltpu.HBM)] * far
+        + [pl.BlockSpec(memory_space=pltpu.VMEM)] * (len(args) - far),
         out_specs=[pl.BlockSpec(memory_space=pltpu.VMEM)] * len(outs),
-        scratch_shapes=[pltpu.VMEM(s, d) for s, d in scratch],
+        scratch_shapes=[pltpu.VMEM(s, d) for s, d in scratch] + ([pltpu.SemaphoreType.DMA((far,))] if far else []),
+        cost_estimate=pl.CostEstimate(flops=int(us * 1e9), bytes_accessed=0, transcendentals=0),
         compiler_params=pltpu.CompilerParams(vmem_limit_bytes=24 << 20),
-    )(*args)
+    )(*[pltpu.with_memory_space_constraint(a, pltpu.HBM) if i < far else a for i, a in enumerate(args)])
 
 
 def shards(inputs, hidden_init, cell_init, w_input, w_hidden, gate_bias):
@@ -222,8 +230,8 @@
     to_left, to_right, main = call(
         pack_kernel,
         [((FOLD + 8, 128), F32), ((FOLD + 8, 128), F32), ((4 * ch, 128), BF16)],
-        [((4 * ch, 128), F32), (inp.shape, F32)],
-        hid, cell, inp,
+        [(hid.shape, BF16), (cell.shape, F32), (inp.shape, BF16), (hid.shape, F32), (inp.shape, F32)],
+        hid, cell, inp, far=3, us=1,
     )
     n = lax.axis_size("lon")
     from_right = lax.ppermute(to_left, "lon", [((i + 1) % n, i) for i in range(n)])
@@ -246,7 +254,7 @@
             functools.partial(step_kernel, step),
             [((4 * ch + (0 if last else FOLD), 128), BF16), ((4 * ch, 128), F32)],
             scratch,
-            gathered, from_left, from_right, inp, cell, w_hidden, wx, bias,
+            gathered, from_left, from_right, inp, cell, w_hidden, wx, bias, us=3,
         )
     return field.reshape(ch, rows, cols), cell.reshape(ch, rows, cols)
 

time: 34 us -> 27.2 us (0.80)
  local copies, waits for them, and re-layouts: 7.74 us -> 0.02 us
  Pallas kernels: 6.44 us -> 7.56 us
    unnamed x22 -> x10, local copies, waits for them, and re-layouts: 7.74 us -> 0.02 us
    pallas_call x4, Pallas kernels: 6.44 us -> 7.56 us  [call(): pl.pallas_call(kernel, out_shape=[jax.ShapeDtypeStruct(s, d) for s, d in...]
where the time goes in v2:
time: 27.2 us; the launch traced here: 27.1 us
  blocking collectives  11.9 us (44%)
  Pallas kernels  7.56 us (28%)
  starting transfers between devices  5.17 us (19%)
  waiting for transfers between devices  1.73 us (6%)
  between operations  0.7 us (3%)
    all_gather x2, blocking collectives, shards(): gathered = lax.all_gather(field, 'chan', axis=0)  11.9 us
    pallas_call x4, Pallas kernels, call(): pl.pallas_call(kernel, out_shape=[jax.ShapeDtypeStruct(s, d) for s, d in...  7.56 us
    ppermute x1, starting transfers between devices, shards(): lax.ppermute(to_right, 'lon', [(i, (i + 1) % n) for i in range(n)])  3.08 us
    ppermute x1, starting transfers between devices, shards(): lax.ppermute(to_left, 'lon', [((i + 1) % n, i) for i in range(n)])  2.09 us
    ppermute x1, waiting for transfers between devices, shards(): lax.ppermute(to_right, 'lon', [(i, (i + 1) % n) for i in range(n)])  1.71 us
  transfers between devices with their start and end apart: 2, of which 1 were waited for; matrix products, arithmetic and copies ran while one was open for 0% of the time, Pallas kernels for 0%

profile of v2, /device:TPU:0, one launch (start us, length us, event | category | flops | bytes accessed | tf_op | source)
XLA Modules:
  0.0 27.1 jit_solution(693986186107352823)
XLA Ops:
  0.6 0.0 copy-start
  0.6 0.0 copy-start.1
  0.7 0.0 copy-start.2
  0.7 0.0 copy-start.3
  0.7 0.0 copy-start.4
  0.7 1.3 %shard_map.77 = (f32[24,128]{1,0:T(8,128)S(1)}, f32[24,128]{1,0:T(8,128)S(1)}, bf16[256,128]{1,0:T(8,128)(2,1)S(1)}) custom-call(bf16[256,128]{1,0:T(8,128)(2,1)} %bitcast.22, f32[256,128]{1,0:T(8,128)} %bitcast.15, bf16[128,128]{1,0:T(8,128)(2,1)} %bitcast.17), custom_call_target="tpu_custom_call" | custom-call | flops 1000000000 | tf_op jit(solution)/shard_map/pallas_call | solution.py:208
  2.0 3.1 %collective-permute-start = (f32[24,128]{1,0:T(8,128)S(1)}, f32[24,128]{1,0:T(8,128)S(1)}, u32[]{:S(2)}, u32[]{:S(2)}) collective-permute-start(f32[24,128]{1,0:T(8,128)S(1)} %get-tuple-element.10), channel_id=1, source_target_pairs={{0,4},{4,8},{8,12},{12,0},{1,5},{5,9},{9,13},{13,1},{2,6},{6,10},{... | collective-permute-start | bytes 36872 | tf_op jit(solution)/shard_map/ppermute | solution.py:238
  5.1 2.1 %collective-permute-start.1 = (f32[24,128]{1,0:T(8,128)S(1)}, f32[24,128]{1,0:T(8,128)S(1)}, u32[]{:S(2)}, u32[]{:S(2)}) collective-permute-start(f32[24,128]{1,0:T(8,128)S(1)} %get-tuple-element.11), channel_id=1, source_target_pairs={{4,0},{8,4},{12,8},{0,12},{5,1},{9,5},{13,9},{1,13},{6,2},{10,6},{... | collective-permute-start | bytes 36872 | tf_op jit(solution)/shard_map/ppermute | solution.py:237
  7.2 1.7 %collective-permute-done.from_left.refs_1_ = f32[24,128]{1,0:T(8,128)S(1)} collective-permute-done((f32[24,128]{1,0:T(8,128)S(1)}, f32[24,128]{1,0:T(8,128)S(1)}, u32[]{:S(2)}, u32[]{:S(2)}) %collective-permute-start) | collective-permute-done | bytes 12320 | tf_op jit(solution)/shard_map/ppermute | solution.py:238
  8.9 0.0 collective-permute-done.1.from_right.refs_2_
  8.9 5.9 %all-gather = bf16[1088,128]{1,0:T(8,128)(2,1)S(1)} all-gather(bf16[272,128]{1,0:T(8,128)(2,1)S(1)} %shard_map.78), channel_id=2, replica_groups=mesh['groups'=2,'lon'=4,'chan'=4] {'chan'}, dimensions={0}, use_global_device_ids=true | all-gather | bytes 348160 | tf_op jit(solution)/shard_map/all_gather | solution.py:242
  14.8 0.0 copy-done
  14.8 0.0 copy-done.1
  14.8 0.0 copy-done.2
  14.9 0.0 copy-done.3
  14.9 0.0 copy-done.4
  14.9 3.4 %shard_map.79 = (bf16[272,128]{1,0:T(8,128)(2,1)S(1)}, f32[256,128]{1,0:T(8,128)S(1)}) custom-call(bf16[4,272,128]{2,1,0:T(8,128)(2,1)S(1)} %bitcast.12, f32[24,128]{1,0:T(8,128)S(1)} %collective-permute-done.from_left.refs_1_, f32[24,128]{1,0:T(8,128)S(1)} %collective-permute-done.1.from_right.refs_2_, bf16[128,128]{1,0:T(8,128)(2,1)S(1)} %bitcast.18, ...), custom_call_target="tpu_custom_call" | custom-call | flops 3000000000 | tf_op jit(solution)/shard_map/pallas_call | solution.py:208
  18.2 5.9 %all-gather.1 = bf16[1088,128]{1,0:T(8,128)(2,1)S(1)} all-gather(bf16[272,128]{1,0:T(8,128)(2,1)S(1)} %get-tuple-element.12), channel_id=3, replica_groups=mesh['groups'=2,'lon'=4,'chan'=4] {'chan'}, dimensions={0}, use_global_device_ids=true | all-gather | bytes 348160 | tf_op jit(solution)/shard_map/all_gather | solution.py:242
  24.2 2.9 %shard_map.80 = (bf16[256,128]{1,0:T(8,128)(2,1)}, f32[256,128]{1,0:T(8,128)}) custom-call(bf16[4,272,128]{2,1,0:T(8,128)(2,1)S(1)} %bitcast.11, f32[24,128]{1,0:T(8,128)S(1)} %collective-permute-done.from_left.refs_1_, f32[24,128]{1,0:T(8,128)S(1)} %collective-permute-done.1.from_right.refs_2_, bf16[128,128]{1,0:T(8,128)(2,1)S(1)} %bitcast.19, ...), custom_call_target="tpu_custom_call" | custom-call | flops 3000000000 | tf_op jit(solution)/shard_map/pallas_call | solution.py:208
  (1 shorter events, 0.0 us)
Async XLA Ops:
  0.6 14.2 %copy-start = (bf16[5,5,256,256]{3,2,1,0:T(8,128)(2,1)S(1)}, bf16[5,5,256,256]{3,2,1,0:T(8,128)(2,1)}, u32[]{:S(2)}) copy-start(bf16[5,5,256,256]{3,2,1,0:T(8,128)(2,1)} %refs_5_.3) | copy-start | bytes 9830404
  0.6 14.2 %copy-start.1 = (bf16[5,5,256,16]{2,3,1,0:T(8,128)(2,1)S(1)}, bf16[5,5,256,16]{2,3,1,0:T(8,128)(2,1)}, u32[]{:S(2)}) copy-start(bf16[5,5,256,16]{2,3,1,0:T(8,128)(2,1)} %param.9) | copy-start | bytes 614404
  0.7 14.2 %copy-start.2 = (f32[64,4,128]{2,1,0:T(4,128)S(1)}, f32[64,4,128]{2,1,0:T(4,128)}, u32[]{:S(2)}) copy-start(f32[64,4,128]{2,1,0:T(4,128)} %param.8) | copy-start | bytes 393220
  0.7 14.2 %copy-start.3 = (bf16[2,16,4,128]{3,2,1,0:T(4,128)(2,1)S(1)}, bf16[2,16,4,128]{3,2,1,0:T(4,128)(2,1)}, u32[]{:S(2)}) copy-start(bf16[2,16,4,128]{3,2,1,0:T(4,128)(2,1)} %param.6) | copy-start | bytes 98308
  0.7 14.2 %copy-start.4 = (f32[256]{0:T(256)S(1)}, f32[256]{0:T(256)}, u32[]{:S(2)}) copy-start(f32[256]{0:T(256)} %param.11) | copy-start | bytes 3076
  2.0 6.9 %collective-permute-start = (f32[24,128]{1,0:T(8,128)S(1)}, f32[24,128]{1,0:T(8,128)S(1)}, u32[]{:S(2)}, u32[]{:S(2)}) collective-permute-start(f32[24,128]{1,0:T(8,128)S(1)} %get-tuple-element.10), channel_id=1, source_target_pairs={{0,4},{4,8},{8,12},{12,0},{1,5},{5,9},{9,13},{13,1},{2,6},{6,10},{... | collective-permute-start | bytes 36872 | tf_op jit(solution)/shard_map/ppermute | solution.py:238
  5.1 3.8 %collective-permute-start.1 = (f32[24,128]{1,0:T(8,128)S(1)}, f32[24,128]{1,0:T(8,128)S(1)}, u32[]{:S(2)}, u32[]{:S(2)}) collective-permute-start(f32[24,128]{1,0:T(8,128)S(1)} %get-tuple-element.11), channel_id=1, source_target_pairs={{4,0},{8,4},{12,8},{0,12},{5,1},{9,5},{13,9},{1,13},{6,2},{10,6},{... | collective-permute-start | bytes 36872 | tf_op jit(solution)/shard_map/ppermute | solution.py:237

commit v3 on v2

--- a/solution.py
+++ b/solution.py
@@ -114,42 +114,76 @@
     return sigmoid(part[3]) * jnp.tanh(cell), cell
 
 
-def step_kernel(step, *refs):
-    last = step == STEPS - 1
-    gathered, from_left, from_right, inp, cell, w, wx, bias = refs[:8]
-    hid_out, cell_out, xs, xi, wxb, pre, inp32 = refs[8:15]
-    shards, ch = gathered.shape[0], (gathered.shape[1] - FOLD) // 4
-    depth, cin = shards * ch, inp.shape[0] // (4 * STEPS)
-    taps = 25 * cin
-    rows = [
-        jnp.concatenate([gathered[c, y * ch : (y + 1) * ch, :] for c in range(shards)], axis=0) for y in range(4)
-    ]
-    halo = jnp.concatenate(
-        [unfold(gathered[c, 4 * ch : 4 * ch + FOLD, :].astype(F32), ch) for c in range(shards)], axis=0
-    ).astype(BF16)
+DRIVE = (((0,), (0,)), ((), ()))
+
+
+def near_far(own, other, ch):
+    even = lax.axis_index("chan") % 2 == 0
+    low, high = jnp.where(even, own, other), jnp.where(even, other, own)
+    return rows_of([low, high], ch)
+
+
+def rows_of(shards, ch):
+    rows = [jnp.concatenate([s[y * ch : (y + 1) * ch] for s in shards], axis=0) for y in range(4)]
+    halo = jnp.concatenate([unfold(s[4 * ch : 4 * ch + FOLD].astype(F32), ch) for s in shards], axis=0)
+    return rows, halo.astype(BF16)
+
+
+def store_windows(xs, rows, halo):
+    depth = halo.shape[0]
     for b in range(5):
         xs[b, :, 0:128] = jnp.zeros((depth, 128), BF16)
         xs[b, :, 640:768] = jnp.zeros((depth, 128), BF16)
     for y in range(4):
         for b, window in enumerate(windows(rows[y], halo, y)):
             xs[b, :, 128 * (y + 1) : 128 * (y + 2)] = window
+
+
+def hidden_rows(w, xs, at, pair):
+    depth = xs.shape[1]
+    terms = [(a, b, 2 * pair + a - 2) for a in range(5) for b in range(5) if -2 < 2 * pair + a - 2 < 4]
+    left = jnp.concatenate([w[a, b, :, pl.ds(at, depth)] for a, b, _ in terms], axis=1)
+    right = jnp.concatenate([xs[b, :, 128 * (lo + 1) : 128 * (lo + 3)] for _, b, lo in terms], axis=0)
+    return jnp.dot(left, right, preferred_element_type=F32)
+
+
+def hidden_rim(w, rows, halo, at):
+    depth = halo.shape[0]
+    strip = strips(rows, halo)
+    stack = jnp.concatenate([roll(strip, -8 * (a - 2)) for a in range(5)], axis=0)
+    total = None
+    for b in range(5):
+        left = jnp.concatenate([w[a, b, :, pl.ds(at, depth)] for a in range(5)], axis=1)
+        part = roll(jnp.dot(left, stack, preferred_element_type=F32), -(b - 2))
+        total = part if total is None else total + part
+    return total
+
+
+def store_inputs(step, xi, wxb, inp32, inp, from_left, from_right, wx, bias):
+    cin = inp.shape[0] // (4 * STEPS)
+    taps = 25 * cin
     inp32[...] = inp[...].astype(F32)
-    irows = [inp32[pl.ds(4 * cin * step + y, cin, stride=4), :].astype(BF16) for y in range(4)]
+    rows = [inp32[pl.ds(4 * cin * step + y, cin, stride=4), :].astype(BF16) for y in range(4)]
     low = (lanes(8) & 7) < 4
-    iblock = jnp.where(low, from_left[FOLD:], from_right[FOLD:])
+    block = jnp.where(low, from_left[FOLD:], from_right[FOLD:])
     first = step * cin // 8
-    ihalo = jnp.concatenate([roll(iblock, -32 * i) for i in range(first, first + cin // 8)], axis=0).astype(BF16)
-    iwin = [windows(irows[y], ihalo, y) for y in range(4)]
+    halo = jnp.concatenate([roll(block, -32 * i) for i in range(first, first + cin // 8)], axis=0).astype(BF16)
+    wins = [windows(rows[y], halo, y) for y in range(4)]
     for a in range(5):
         for b in range(5):
             at = cin * (5 * a + b)
             for y in range(4):
                 r = y + a - 2
                 xi[at : at + cin, 128 * y : 128 * (y + 1)] = (
-                    iwin[r][b] if 0 <= r < 4 else jnp.zeros((cin, 128), BF16)
+                    wins[r][b] if 0 <= r < 4 else jnp.zeros((cin, 128), BF16)
                 )
-    count = xi.shape[1]
-    ones = lax.broadcasted_iota(jnp.int32, (16, count), 0) < 3
+    if xi.shape[1] > 512:
+        strip = strips(rows, halo)
+        for a in range(5):
+            for b in range(5):
+                at = cin * (5 * a + b)
+                xi[at : at + cin, 512:640] = roll(strip, -(8 * (a - 2) + b - 2))
+    ones = lax.broadcasted_iota(jnp.int32, (16, xi.shape[1]), 0) < 3
     xi[taps : taps + 16, :] = jnp.where(ones, 1.0, 0.0).astype(BF16)
     wxb[0:taps, :] = wx[...]
     b0 = bias[...]
@@ -160,48 +194,79 @@
     wxb[taps : taps + 16, :] = jnp.where(
         sub == 0, b1, jnp.where(sub == 1, b2, jnp.where(sub == 2, b3, 0.0))
     ).astype(BF16)
-    if not last:
-        istrip = strips(irows, ihalo)
-        for a in range(5):
-            for b in range(5):
-                at = cin * (5 * a + b)
-                xi[at : at + cin, 512:640] = roll(istrip, -(8 * (a - 2) + b - 2))
-    drive = (((0,), (0,)), ((), ()))
-    for pair in range(2):
-        terms = [(a, b, 2 * pair + a - 2) for a in range(5) for b in range(5) if -2 < 2 * pair + a - 2 < 4]
-        left = jnp.concatenate([w[a, b] for a, b, _ in terms], axis=1)
-        right = jnp.concatenate([xs[b, :, 128 * (lo + 1) : 128 * (lo + 3)] for _, b, lo in terms], axis=0)
-        at = 256 * pair
-        total = jnp.dot(left, right, preferred_element_type=F32) + lax.dot_general(
-            wxb[...], xi[:, at : at + 256], drive, preferred_element_type=F32
-        )
-        pre[2 * pair] = total[:, 0:128]
-        pre[2 * pair + 1] = total[:, 128:256]
+
+
+def input_part(wxb, xi, at, wide):
+    return lax.dot_general(wxb[...], xi[:, at : at + wide], DRIVE, preferred_element_type=F32)
+
+
+def finish(step, pre, cell, from_left, from_right, hid_out, cell_out, hid32):
+    ch = cell.shape[0] // 4
+    last = step == STEPS - 1
     for y in range(4):
         before = cell[pl.ds(y, ch, stride=4), :] if step == 0 else cell[y * ch : (y + 1) * ch, :]
         h, c = gates(pre, ch, y, before)
         if last:
             cell_out[pl.ds(y, ch, stride=4), :] = c
-            refs[15][pl.ds(y, ch, stride=4), :] = h
+            hid32[pl.ds(y, ch, stride=4), :] = h
         else:
             cell_out[y * ch : (y + 1) * ch, :] = c
             hid_out[y * ch : (y + 1) * ch, :] = h.astype(BF16)
     if last:
-        hid_out[...] = refs[15][...].astype(BF16)
+        hid_out[...] = hid32[...].astype(BF16)
         return
-    strip = strips(rows, halo)
-    stack = jnp.concatenate([roll(strip, -8 * (a - 2)) for a in range(5)], axis=0)
-    total = lax.dot_general(wxb[...], xi[:, 512:640], drive, preferred_element_type=F32)
-    for b in range(5):
-        left = jnp.concatenate([w[a, b] for a in range(5)], axis=1)
-        total = total + roll(jnp.dot(left, stack, preferred_element_type=F32), -(b - 2))
-    pre[4] = total
     lane = lanes(ch)
-    near = lane < 64
     cells = unfold(jnp.where((lanes(FOLD) & 7) < 4, from_right[0:FOLD], from_left[0:FOLD]), ch)
-    h, _ = gates(pre, ch, 4, jnp.where(near, roll(cells, 12), roll(cells, 84)))
+    h, _ = gates(pre, ch, 4, jnp.where(lane < 64, roll(cells, 12), roll(cells, 84)))
     h = jnp.where((lane & 7) < 4, roll(h, -16), roll(h, -80))
     hid_out[4 * ch : 4 * ch + FOLD, :] = fold(h).astype(BF16)
+
+
+def whole_kernel(step, gathered, from_left, from_right, inp, cell, w, wx, bias, hid_out, cell_out, xs, xi, wxb, pre, inp32, hid32):
+    shards, ch = gathered.shape[0], cell.shape[0] // 4
+    rows, halo = rows_of([gathered[c] for c in range(shards)], ch)
+    store_windows(xs, rows, halo)
+    store_inputs(step, xi, wxb, inp32, inp, from_left, from_right, wx, bias)
+    for pair in range(2):
+        total = hidden_rows(w, xs, 0, pair) + input_part(wxb, xi, 256 * pair, 256)
+        pre[2 * pair] = total[:, 0:128]
+        pre[2 * pair + 1] = total[:, 128:256]
+    if step < STEPS - 1:
+        pre[4] = hidden_rim(w, rows, halo, 0) + input_part(wxb, xi, 512, 128)
+    finish(step, pre, cell, from_left, from_right, hid_out, cell_out, hid32)
+
+
+def first_channel(depth, remote):
+    mine = lax.axis_index("chan") // 2
+    return pl.multiple_of((1 - mine if remote else mine) * depth, depth)
+
+
+def near_kernel(step, own, other, from_left, from_right, inp, w, wx, bias, part, xs, xi, wxb, inp32):
+    ch = w.shape[2] // 4
+    rows, halo = near_far(own[...], other[...], ch)
+    at = first_channel(2 * ch, False)
+    store_windows(xs, rows, halo)
+    store_inputs(step, xi, wxb, inp32, inp, from_left, from_right, wx, bias)
+    for pair in range(2):
+        total = hidden_rows(w, xs, at, pair) + input_part(wxb, xi, 256 * pair, 256)
+        part[2 * pair] = total[:, 0:128]
+        part[2 * pair + 1] = total[:, 128:256]
+    if step < STEPS - 1:
+        part[4] = hidden_rim(w, rows, halo, at) + input_part(wxb, xi, 512, 128)
+
+
+def far_kernel(step, same, cross, part, from_left, from_right, cell, w, hid_out, cell_out, xs, pre, hid32):
+    ch = cell.shape[0] // 4
+    rows, halo = near_far(same[...], cross[...], ch)
+    at = first_channel(2 * ch, True)
+    store_windows(xs, rows, halo)
+    for pair in range(2):
+        total = hidden_rows(w, xs, at, pair)
+        pre[2 * pair] = part[2 * pair] + total[:, 0:128]
+        pre[2 * pair + 1] = part[2 * pair + 1] + total[:, 128:256]
+    if step < STEPS - 1:
+        pre[4] = part[4] + hidden_rim(w, rows, halo, at)
+    finish(step, pre, cell, from_left, from_right, hid_out, cell_out, hid32)
 
 
 def call(kernel, outs, scratch, *args, far=0, us=1):
@@ -237,25 +302,35 @@
     from_right = lax.ppermute(to_left, "lon", [((i + 1) % n, i) for i in range(n)])
     from_left = lax.ppermute(to_right, "lon", [(i, (i + 1) % n) for i in range(n)])
     (field,) = call(join_kernel, [((4 * ch + FOLD, 128), BF16)], [], main, from_left, from_right)
+    shards = lax.axis_size("chan")
     for step in range(STEPS):
         last = step == STEPS - 1
-        gathered = lax.all_gather(field, "chan", axis=0)
         wide = 512 if last else 640
-        scratch = [
-            ((5, depth, 768), BF16),
-            ((25 * cin + 16, wide), BF16),
-            ((25 * cin + 16, gate), BF16),
-            ((wide // 128, gate, 128), F32),
-            (inp.shape, F32),
-        ]
-        if last:
-            scratch.append(((4 * ch, 128), F32))
-        field, cell = call(
-            functools.partial(step_kernel, step),
-            [((4 * ch + (0 if last else FOLD), 128), BF16), ((4 * ch, 128), F32)],
-            scratch,
-            gathered, from_left, from_right, inp, cell, w_hidden, wx, bias, us=3,
-        )
+        stack = [((25 * cin + 16, wide), BF16), ((25 * cin + 16, gate), BF16)]
+        inp32 = (inp.shape, F32)
+        hid32 = ((4 * ch, 128), F32)
+        pre = ((wide // 128, gate, 128), F32)
+        outs = [((4 * ch + (0 if last else FOLD), 128), BF16), ((4 * ch, 128), F32)]
+        if shards == 4 and 2 * ch == 128:
+            other, same, cross = [
+                lax.ppermute(field, "chan", [(i, i ^ k) for i in range(shards)]) for k in (1, 2, 3)
+            ]
+            windowed = ((5, 2 * ch, 768), BF16)
+            (part,) = call(
+                functools.partial(near_kernel, step), [pre], [windowed, *stack, inp32],
+                field, other, from_left, from_right, inp, w_hidden, wx, bias, us=1.5,
+            )
+            field, cell = call(
+                functools.partial(far_kernel, step), outs, [windowed, pre, hid32],
+                same, cross, part, from_left, from_right, cell, w_hidden, us=2,
+            )
+        else:
+            gathered = lax.all_gather(field, "chan", axis=0)
+            field, cell = call(
+                functools.partial(whole_kernel, step), outs,
+                [((5, depth, 768), BF16), *stack, pre, inp32, hid32],
+                gathered, from_left, from_right, inp, cell, w_hidden, wx, bias, us=3,
+            )
     return field.reshape(ch, rows, cols), cell.reshape(ch, rows, cols)
 
 

time: 27.2 us -> 25 us (0.919)
  blocking collectives: 11.9 us -> 0 us
  waiting for transfers between devices: 1.73 us -> 6.12 us
  starting transfers between devices: 5.17 us -> 9.55 us
  Pallas kernels: 7.56 us -> 8.39 us
    all_gather x2 -> x0, blocking collectives: 11.9 us -> none  [shards(): gathered = lax.all_gather(field, 'chan', axis=0)]
    ppermute x0 -> x6, waiting for transfers between devices: none -> 4.39 us  [shards(): lax.ppermute(field, 'chan', [(i, i ^ k) for i in range(shards)])]
    ppermute x0 -> x6, starting transfers between devices: none -> 4.38 us  [shards(): lax.ppermute(field, 'chan', [(i, i ^ k) for i in range(shards)])]
    pallas_call x4 -> x6, Pallas kernels: 7.56 us -> 8.39 us  [call(): pl.pallas_call(kernel, out_shape=[jax.ShapeDtypeStruct(s, d) for s, d in...]
  transfers between devices with their start and end apart: 2 -> 8, of which waited for: 1 -> 5; matrix products, arithmetic and copies ran while one was open for 0% -> 0% of each run, Pallas kernels for 0% -> 14%
where the time goes in v3:
time: 25 us; the launch traced here: 24.8 us
  starting transfers between devices  9.55 us (38%)
  Pallas kernels  8.39 us (34%)
  waiting for transfers between devices  6.12 us (24%)
  between operations  0.74 us (3%)
    pallas_call x6, Pallas kernels, call(): pl.pallas_call(kernel, out_shape=[jax.ShapeDtypeStruct(s, d) for s, d in...  8.39 us
    ppermute x6, waiting for transfers between devices, shards(): lax.ppermute(field, 'chan', [(i, i ^ k) for i in range(shards)])  4.39 us
    ppermute x6, starting transfers between devices, shards(): lax.ppermute(field, 'chan', [(i, i ^ k) for i in range(shards)])  4.38 us
    ppermute x1, starting transfers between devices, shards(): lax.ppermute(to_right, 'lon', [(i, (i + 1) % n) for i in range(n)])  3.08 us
    ppermute x1, starting transfers between devices, shards(): lax.ppermute(to_left, 'lon', [((i + 1) % n, i) for i in range(n)])  2.09 us
    ppermute x1, waiting for transfers between devices, shards(): lax.ppermute(to_right, 'lon', [(i, (i + 1) % n) for i in range(n)])  1.71 us
  transfers between devices with their start and end apart: 8, of which 5 were waited for; matrix products, arithmetic and copies ran while one was open for 0% of the time, Pallas kernels for 14%

profile of v3, /device:TPU:0, one launch (start us, length us, event | category | flops | bytes accessed | tf_op | source)
XLA Modules:
  0.0 24.8 jit_solution(10615645731705435877)
XLA Ops:
  0.6 0.0 copy-start
  0.6 0.0 copy-start.1
  0.7 0.0 copy-start.3
  0.7 0.0 copy-start.4
  0.7 1.3 %shard_map.77 = (f32[24,128]{1,0:T(8,128)S(1)}, f32[24,128]{1,0:T(8,128)S(1)}, bf16[256,128]{1,0:T(8,128)(2,1)S(1)}) custom-call(bf16[256,128]{1,0:T(8,128)(2,1)} %bitcast.18, f32[256,128]{1,0:T(8,128)} %bitcast.11, bf16[128,128]{1,0:T(8,128)(2,1)} %bitcast.13), custom_call_target="tpu_custom_call" | custom-call | flops 1000000000 | tf_op jit(solution)/shard_map/pallas_call | solution.py:273
  2.0 3.1 %collective-permute-start = (f32[24,128]{1,0:T(8,128)S(1)}, f32[24,128]{1,0:T(8,128)S(1)}, u32[]{:S(2)}, u32[]{:S(2)}) collective-permute-start(f32[24,128]{1,0:T(8,128)S(1)} %get-tuple-element.10), channel_id=1, source_target_pairs={{0,4},{4,8},{8,12},{12,0},{1,5},{5,9},{9,13},{13,1},{2,6},{6,10},{... | collective-permute-start | bytes 36872 | tf_op jit(solution)/shard_map/ppermute | solution.py:303
  5.1 2.1 %collective-permute-start.1 = (f32[24,128]{1,0:T(8,128)S(1)}, f32[24,128]{1,0:T(8,128)S(1)}, u32[]{:S(2)}, u32[]{:S(2)}) collective-permute-start(f32[24,128]{1,0:T(8,128)S(1)} %get-tuple-element.11), channel_id=1, source_target_pairs={{4,0},{8,4},{12,8},{0,12},{5,1},{9,5},{13,9},{1,13},{6,2},{10,6},{... | collective-permute-start | bytes 36872 | tf_op jit(solution)/shard_map/ppermute | solution.py:302
  7.2 1.7 %collective-permute-done.from_left = f32[24,128]{1,0:T(8,128)S(1)} collective-permute-done((f32[24,128]{1,0:T(8,128)S(1)}, f32[24,128]{1,0:T(8,128)S(1)}, u32[]{:S(2)}, u32[]{:S(2)}) %collective-permute-start) | collective-permute-done | bytes 12320 | tf_op jit(solution)/shard_map/ppermute | solution.py:303
  8.9 0.0 collective-permute-done.1.from_right
  8.9 0.0 copy-start.2
  8.9 0.1 collective-permute-start.4
  9.0 1.7 %collective-permute-start.3 = (bf16[272,128]{1,0:T(8,128)(2,1)S(1)}, bf16[272,128]{1,0:T(8,128)(2,1)S(1)}, u32[]{:S(2)}, u32[]{:S(2)}) collective-permute-start(bf16[272,128]{1,0:T(8,128)(2,1)S(1)} %shard_map.78.own), channel_id=1, source_target_pairs={{0,3},{1,2},{2,1},{3,0},{4,7},{5,6},{6,5},{7,4},{8,11},{9,10},{10,... | collective-permute-start | bytes 208904 | tf_op jit(solution)/shard_map/ppermute | solution.py:316
  10.7 0.4 %collective-permute-start.2 = (bf16[272,128]{1,0:T(8,128)(2,1)S(1)}, bf16[272,128]{1,0:T(8,128)(2,1)S(1)}, u32[]{:S(2)}, u32[]{:S(2)}) collective-permute-start(bf16[272,128]{1,0:T(8,128)(2,1)S(1)} %shard_map.78.own), channel_id=1, source_target_pairs={{0,2},{1,3},{2,0},{3,1},{4,6},{5,7},{6,4},{7,5},{8,10},{9,11},{10,... | collective-permute-start | bytes 208904 | tf_op jit(solution)/shard_map/ppermute | solution.py:316
  11.1 0.0 collective-permute-done.4.other
  11.1 0.0 copy-done
  11.1 0.0 copy-done.1
  11.1 0.0 copy-done.3
  11.2 0.0 copy-done.4
  11.2 1.9 %shard_map.79.part = f32[5,256,128]{2,1,0:T(8,128)S(1)} custom-call(bf16[272,128]{1,0:T(8,128)(2,1)S(1)} %shard_map.78.own, bf16[272,128]{1,0:T(8,128)(2,1)S(1)} %collective-permute-done.4.other, f32[24,128]{1,0:T(8,128)S(1)} %collective-permute-done.from_left, f32[24,128]{1,0:T(8,128)S(1)} %collective-permute-done.1.from_right, ...), custom_call_target="tpu_custom_call" | custom-call | flops 1500000000 | tf_op jit(solution)/shard_map/pallas_call | solution.py:273
  13.1 0.1 collective-permute-done.3.cross
  13.2 1.8 %collective-permute-done.2.same = bf16[272,128]{1,0:T(8,128)(2,1)S(1)} collective-permute-done((bf16[272,128]{1,0:T(8,128)(2,1)S(1)}, bf16[272,128]{1,0:T(8,128)(2,1)S(1)}, u32[]{:S(2)}, u32[]{:S(2)}) %collective-permute-start.2) | collective-permute-done | bytes 69664 | tf_op jit(solution)/shard_map/ppermute | solution.py:316
  15.0 0.0 copy-done.2
  15.0 1.8 %shard_map.80 = (bf16[272,128]{1,0:T(8,128)(2,1)S(1)}, f32[256,128]{1,0:T(8,128)S(1)}) custom-call(bf16[272,128]{1,0:T(8,128)(2,1)S(1)} %collective-permute-done.2.same, bf16[272,128]{1,0:T(8,128)(2,1)S(1)} %collective-permute-done.3.cross, f32[5,256,128]{2,1,0:T(8,128)S(1)} %shard_map.79.part, f32[24,128]{1,0:T(8,128)S(1)} %collective-permute-done.from_left, ...), custom_call_target="tpu_custom_call" | custom-call | flops 2000000000 | tf_op jit(solution)/shard_map/pallas_call | solution.py:273
  16.9 0.0 collective-permute-start.7
  16.9 1.7 %collective-permute-start.6 = (bf16[272,128]{1,0:T(8,128)(2,1)S(1)}, bf16[272,128]{1,0:T(8,128)(2,1)S(1)}, u32[]{:S(2)}, u32[]{:S(2)}) collective-permute-start(bf16[272,128]{1,0:T(8,128)(2,1)S(1)} %get-tuple-element.12.own), channel_id=1, source_target_pairs={{0,3},{1,2},{2,1},{3,0},{4,7},{5,6},{6,5},{7,4},{8,11},{9,10},{10,... | collective-permute-start | bytes 208904 | tf_op jit(solution)/shard_map/ppermute | solution.py:316
  18.6 0.5 %collective-permute-start.5 = (bf16[272,128]{1,0:T(8,128)(2,1)S(1)}, bf16[272,128]{1,0:T(8,128)(2,1)S(1)}, u32[]{:S(2)}, u32[]{:S(2)}) collective-permute-start(bf16[272,128]{1,0:T(8,128)(2,1)S(1)} %get-tuple-element.12.own), channel_id=1, source_target_pairs={{0,2},{1,3},{2,0},{3,1},{4,6},{5,7},{6,4},{7,5},{8,10},{9,11},{10,... | collective-permute-start | bytes 208904 | tf_op jit(solution)/shard_map/ppermute | solution.py:316
  19.0 0.0 collective-permute-done.7.other
  19.0 1.4 %shard_map.81.part = f32[4,256,128]{2,1,0:T(8,128)S(1)} custom-call(bf16[272,128]{1,0:T(8,128)(2,1)S(1)} %get-tuple-element.12.own, bf16[272,128]{1,0:T(8,128)(2,1)S(1)} %collective-permute-done.7.other, f32[24,128]{1,0:T(8,128)S(1)} %collective-permute-done.from_left, f32[24,128]{1,0:T(8,128)S(1)} %collective-permute-done.1.from_right, ...), custom_call_target="tpu_custom_call" | custom-call | flops 1500000000 | tf_op jit(solution)/shard_map/pallas_call | solution.py:273
  20.5 0.6 %collective-permute-done.6.cross = bf16[272,128]{1,0:T(8,128)(2,1)S(1)} collective-permute-done((bf16[272,128]{1,0:T(8,128)(2,1)S(1)}, bf16[272,128]{1,0:T(8,128)(2,1)S(1)}, u32[]{:S(2)}, u32[]{:S(2)}) %collective-permute-start.6) | collective-permute-done | bytes 69664 | tf_op jit(solution)/shard_map/ppermute | solution.py:316
  21.1 1.8 %collective-permute-done.5.same = bf16[272,128]{1,0:T(8,128)(2,1)S(1)} collective-permute-done((bf16[272,128]{1,0:T(8,128)(2,1)S(1)}, bf16[272,128]{1,0:T(8,128)(2,1)S(1)}, u32[]{:S(2)}, u32[]{:S(2)}) %collective-permute-start.5) | collective-permute-done | bytes 69664 | tf_op jit(solution)/shard_map/ppermute | solution.py:316
  22.9 1.9 %shard_map.82 = (bf16[256,128]{1,0:T(8,128)(2,1)}, f32[256,128]{1,0:T(8,128)}) custom-call(bf16[272,128]{1,0:T(8,128)(2,1)S(1)} %collective-permute-done.5.same, bf16[272,128]{1,0:T(8,128)(2,1)S(1)} %collective-permute-done.6.cross, f32[4,256,128]{2,1,0:T(8,128)S(1)} %shard_map.81.part, f32[24,128]{1,0:T(8,128)S(1)} %collective-permute-done.from_left, ...), custom_call_target="tpu_custom_call" | custom-call | flops 2000000000 | tf_op jit(solution)/shard_map/pallas_call | solution.py:273
  (1 shorter events, 0.0 us)
Async XLA Ops:
  0.6 10.5 %copy-start = (bf16[5,5,256,256]{3,2,1,0:T(8,128)(2,1)S(1)}, bf16[5,5,256,256]{3,2,1,0:T(8,128)(2,1)}, u32[]{:S(2)}) copy-start(bf16[5,5,256,256]{3,2,1,0:T(8,128)(2,1)} %w.7) | copy-start | bytes 9830404
  0.6 10.5 %copy-start.1 = (bf16[5,5,256,16]{2,3,1,0:T(8,128)(2,1)S(1)}, bf16[5,5,256,16]{2,3,1,0:T(8,128)(2,1)}, u32[]{:S(2)}) copy-start(bf16[5,5,256,16]{2,3,1,0:T(8,128)(2,1)} %param.9) | copy-start | bytes 614404
  0.7 10.5 %copy-start.3 = (bf16[2,16,4,128]{3,2,1,0:T(4,128)(2,1)S(1)}, bf16[2,16,4,128]{3,2,1,0:T(4,128)(2,1)}, u32[]{:S(2)}) copy-start(bf16[2,16,4,128]{3,2,1,0:T(4,128)(2,1)} %param.6) | copy-start | bytes 98308
  0.7 10.5 %copy-start.4 = (f32[256]{0:T(256)S(1)}, f32[256]{0:T(256)}, u32[]{:S(2)}) copy-start(f32[256]{0:T(256)} %param.11) | copy-start | bytes 3076
  2.0 6.9 %collective-permute-start = (f32[24,128]{1,0:T(8,128)S(1)}, f32[24,128]{1,0:T(8,128)S(1)}, u32[]{:S(2)}, u32[]{:S(2)}) collective-permute-start(f32[24,128]{1,0:T(8,128)S(1)} %get-tuple-element.10), channel_id=1, source_target_pairs={{0,4},{4,8},{8,12},{12,0},{1,5},{5,9},{9,13},{13,1},{2,6},{6,10},{... | collective-permute-start | bytes 36872 | tf_op jit(solution)/shard_map/ppermute | solution.py:303
  5.1 3.8 %collective-permute-start.1 = (f32[24,128]{1,0:T(8,128)S(1)}, f32[24,128]{1,0:T(8,128)S(1)}, u32[]{:S(2)}, u32[]{:S(2)}) collective-permute-start(f32[24,128]{1,0:T(8,128)S(1)} %get-tuple-element.11), channel_id=1, source_target_pairs={{4,0},{8,4},{12,8},{0,12},{5,1},{9,5},{13,9},{1,13},{6,2},{10,6},{... | collective-permute-start | bytes 36872 | tf_op jit(solution)/shard_map/ppermute | solution.py:302
  8.9 6.1 %copy-start.2 = (f32[64,4,128]{2,1,0:T(4,128)S(1)}, f32[64,4,128]{2,1,0:T(4,128)}, u32[]{:S(2)}) copy-start(f32[64,4,128]{2,1,0:T(4,128)} %param.8) | copy-start | bytes 393220
  8.9 2.2 %collective-permute-start.4 = (bf16[272,128]{1,0:T(8,128)(2,1)S(1)}, bf16[272,128]{1,0:T(8,128)(2,1)S(1)}, u32[]{:S(2)}, u32[]{:S(2)}) collective-permute-start(bf16[272,128]{1,0:T(8,128)(2,1)S(1)} %shard_map.78.own), channel_id=1, source_target_pairs={{0,1},{1,0},{2,3},{3,2},{4,5},{5,4},{6,7},{7,6},{8,9},{9,8},{10,11... | collective-permute-start | bytes 208904 | tf_op jit(solution)/shard_map/ppermute | solution.py:316
  9.0 4.2 %collective-permute-start.3 = (bf16[272,128]{1,0:T(8,128)(2,1)S(1)}, bf16[272,128]{1,0:T(8,128)(2,1)S(1)}, u32[]{:S(2)}, u32[]{:S(2)}) collective-permute-start(bf16[272,128]{1,0:T(8,128)(2,1)S(1)} %shard_map.78.own), channel_id=1, source_target_pairs={{0,3},{1,2},{2,1},{3,0},{4,7},{5,6},{6,5},{7,4},{8,11},{9,10},{10,... | collective-permute-start | bytes 208904 | tf_op jit(solution)/shard_map/ppermute | solution.py:316
  10.7 4.3 %collective-permute-start.2 = (bf16[272,128]{1,0:T(8,128)(2,1)S(1)}, bf16[272,128]{1,0:T(8,128)(2,1)S(1)}, u32[]{:S(2)}, u32[]{:S(2)}) collective-permute-start(bf16[272,128]{1,0:T(8,128)(2,1)S(1)} %shard_map.78.own), channel_id=1, source_target_pairs={{0,2},{1,3},{2,0},{3,1},{4,6},{5,7},{6,4},{7,5},{8,10},{9,11},{10,... | collective-permute-start | bytes 208904 | tf_op jit(solution)/shard_map/ppermute | solution.py:316
  16.9 2.2 %collective-permute-start.7 = (bf16[272,128]{1,0:T(8,128)(2,1)S(1)}, bf16[272,128]{1,0:T(8,128)(2,1)S(1)}, u32[]{:S(2)}, u32[]{:S(2)}) collective-permute-start(bf16[272,128]{1,0:T(8,128)(2,1)S(1)} %get-tuple-element.12.own), channel_id=1, source_target_pairs={{0,1},{1,0},{2,3},{3,2},{4,5},{5,4},{6,7},{7,6},{8,9},{9,8},{10,11... | collective-permute-start | bytes 208904 | tf_op jit(solution)/shard_map/ppermute | solution.py:316
  16.9 4.2 %collective-permute-start.6 = (bf16[272,128]{1,0:T(8,128)(2,1)S(1)}, bf16[272,128]{1,0:T(8,128)(2,1)S(1)}, u32[]{:S(2)}, u32[]{:S(2)}) collective-permute-start(bf16[272,128]{1,0:T(8,128)(2,1)S(1)} %get-tuple-element.12.own), channel_id=1, source_target_pairs={{0,3},{1,2},{2,1},{3,0},{4,7},{5,6},{6,5},{7,4},{8,11},{9,10},{10,... | collective-permute-start | bytes 208904 | tf_op jit(solution)/shard_map/ppermute | solution.py:316
  18.6 4.4 %collective-permute-start.5 = (bf16[272,128]{1,0:T(8,128)(2,1)S(1)}, bf16[272,128]{1,0:T(8,128)(2,1)S(1)}, u32[]{:S(2)}, u32[]{:S(2)}) collective-permute-start(bf16[272,128]{1,0:T(8,128)(2,1)S(1)} %get-tuple-element.12.own), channel_id=1, source_target_pairs={{0,2},{1,3},{2,0},{3,1},{4,6},{5,7},{6,4},{7,5},{8,10},{9,11},{10,... | collective-permute-start | bytes 208904 | tf_op jit(solution)/shard_map/ppermute | solution.py:316

commit v4 on v3

--- a/solution.py
+++ b/solution.py
@@ -50,7 +50,7 @@
     return jnp.concatenate(left, axis=0), jnp.concatenate(right, axis=0)
 
 
-def pack_kernel(hid_far, cell_far, inp_far, to_left, to_right, main, hid, cell, inp, hid32, inp32, arrived):
+def pack_kernel(hid_far, cell_far, inp_far, to_right, to_left, hid_out, hid, cell, inp, hid32, inp32, arrived):
     ch = hid.shape[0] // 4
     pairs = ((hid_far, hid), (cell_far, cell), (inp_far, inp))
     copies = [pltpu.make_async_copy(a, b, arrived.at[i]) for i, (a, b) in enumerate(pairs)]
@@ -67,18 +67,25 @@
     to_left[FOLD:] = il
     to_right[0:FOLD] = hr + roll(cr, 4)
     to_right[FOLD:] = ir
+    hid_out[...] = hid32[...]
+
+
+def main_kernel(hid, main):
+    ch = hid.shape[0] // 4
     for y in range(4):
-        main[y * ch : (y + 1) * ch, :] = hid32[pl.ds(y, ch, stride=4), :].astype(BF16)
-
-
-def join_kernel(main, from_left, from_right, out):
-    n = main.shape[0]
-    out[0:n] = main[...]
+        main[y * ch : (y + 1) * ch, :] = hid[pl.ds(y, ch, stride=4), :].astype(BF16)
+
+
+def strip_kernel(came_left, came_right, to_right, to_left, from_right, from_left, out):
+    from_left[...], from_right[...] = came_left[...], came_right[...]
     low = (lanes(FOLD) & 7) < 4
-    out[n : n + FOLD] = jnp.where(low, from_left[0:FOLD], from_right[0:FOLD]).astype(BF16)
+    out[0:FOLD] = jnp.where(low, from_left[0:FOLD], from_right[0:FOLD]).astype(BF16)
+    out[FOLD:] = jnp.where(low, to_right[0:FOLD], to_left[0:FOLD]).astype(BF16)
 
 
 def windows(row, halo, y):
+    if halo is None:
+        return [roll(row, -d) for d in range(-2, 3)]
     lane = lanes(row.shape[0])
     ring = roll(halo, -(8 * y + 4))
     out = []
@@ -91,17 +98,21 @@
     return out
 
 
-def strips(rows, halo):
+def strips(halo, own):
     lane = lanes(halo.shape[0])
-    low, left = (lane & 7) < 4, lane < 64
-    own = jnp.zeros_like(halo)
+    low, left, used = (lane & 7) < 4, lane < 64, lane < 32
+    halo, own = [jnp.where(used, x, jnp.zeros_like(x)) for x in (halo, own)]
+    return jnp.where(
+        left, jnp.where(low, roll(halo, 16), roll(own, 16)), jnp.where(low, roll(own, 80), roll(halo, 80))
+    )
+
+
+def own_edges(rows):
+    lane = lanes(rows[0].shape[0])
+    own = jnp.zeros_like(rows[0])
     for y in range(4):
-        here = (lane >= 8 * y + 16) & (lane < 8 * y + 24)
-        own = jnp.where(here, roll(rows[y], 8 * y + 20), own)
-    rim = jnp.where(lane < 32, halo, jnp.zeros_like(halo))
-    return jnp.where(
-        left, jnp.where(low, roll(rim, 16), own), jnp.where(low, roll(own, 64), roll(rim, 80))
-    )
+        own = jnp.where((lane >= 8 * y) & (lane < 8 * y + 8), roll(rows[y], 8 * y + 4), own)
+    return own
 
 
 def sigmoid(x):
@@ -125,12 +136,14 @@
 
 def rows_of(shards, ch):
     rows = [jnp.concatenate([s[y * ch : (y + 1) * ch] for s in shards], axis=0) for y in range(4)]
+    if shards[0].shape[0] == 4 * ch:
+        return rows, None
     halo = jnp.concatenate([unfold(s[4 * ch : 4 * ch + FOLD].astype(F32), ch) for s in shards], axis=0)
     return rows, halo.astype(BF16)
 
 
 def store_windows(xs, rows, halo):
-    depth = halo.shape[0]
+    depth = rows[0].shape[0]
     for b in range(5):
         xs[b, :, 0:128] = jnp.zeros((depth, 128), BF16)
         xs[b, :, 640:768] = jnp.zeros((depth, 128), BF16)
@@ -147,27 +160,29 @@
     return jnp.dot(left, right, preferred_element_type=F32)
 
 
-def hidden_rim(w, rows, halo, at):
-    depth = halo.shape[0]
-    strip = strips(rows, halo)
+def hidden_rim(w, strip):
     stack = jnp.concatenate([roll(strip, -8 * (a - 2)) for a in range(5)], axis=0)
     total = None
     for b in range(5):
-        left = jnp.concatenate([w[a, b, :, pl.ds(at, depth)] for a in range(5)], axis=1)
+        left = jnp.concatenate([w[a, b] for a in range(5)], axis=1)
         part = roll(jnp.dot(left, stack, preferred_element_type=F32), -(b - 2))
         total = part if total is None else total + part
     return total
 
 
-def store_inputs(step, xi, wxb, inp32, inp, from_left, from_right, wx, bias):
+def input_rows(step, inp32, inp, from_right, from_left):
     cin = inp.shape[0] // (4 * STEPS)
-    taps = 25 * cin
     inp32[...] = inp[...].astype(F32)
     rows = [inp32[pl.ds(4 * cin * step + y, cin, stride=4), :].astype(BF16) for y in range(4)]
     low = (lanes(8) & 7) < 4
     block = jnp.where(low, from_left[FOLD:], from_right[FOLD:])
     first = step * cin // 8
     halo = jnp.concatenate([roll(block, -32 * i) for i in range(first, first + cin // 8)], axis=0).astype(BF16)
+    return rows, halo
+
+
+def store_inputs(xi, rows, halo):
+    cin = halo.shape[0]
     wins = [windows(rows[y], halo, y) for y in range(4)]
     for a in range(5):
         for b in range(5):
@@ -177,14 +192,26 @@
                 xi[at : at + cin, 128 * y : 128 * (y + 1)] = (
                     wins[r][b] if 0 <= r < 4 else jnp.zeros((cin, 128), BF16)
                 )
-    if xi.shape[1] > 512:
-        strip = strips(rows, halo)
-        for a in range(5):
-            for b in range(5):
-                at = cin * (5 * a + b)
-                xi[at : at + cin, 512:640] = roll(strip, -(8 * (a - 2) + b - 2))
+    store_ones(xi, 25 * cin)
+
+
+def store_input_rim(xi, rows, halo):
+    cin = halo.shape[0]
+    strip = strips(halo, own_edges(rows))
+    for a in range(5):
+        for b in range(5):
+            at = cin * (5 * a + b)
+            xi[at : at + cin, :] = roll(strip, -(8 * (a - 2) + b - 2))
+    store_ones(xi, 25 * cin)
+
+
+def store_ones(xi, taps):
     ones = lax.broadcasted_iota(jnp.int32, (16, xi.shape[1]), 0) < 3
     xi[taps : taps + 16, :] = jnp.where(ones, 1.0, 0.0).astype(BF16)
+
+
+def store_input_weights(wxb, wx, bias):
+    taps = wx.shape[0]
     wxb[0:taps, :] = wx[...]
     b0 = bias[...]
     b1 = b0.astype(BF16).astype(F32)
@@ -200,7 +227,27 @@
     return lax.dot_general(wxb[...], xi[:, at : at + wide], DRIVE, preferred_element_type=F32)
 
 
-def finish(step, pre, cell, from_left, from_right, hid_out, cell_out, hid32):
+def rim_gates(pre, to_right, to_left, from_right, from_left, ch):
+    low = (lanes(FOLD) & 7) < 4
+    halo = unfold(jnp.where(low, from_right[0:FOLD], from_left[0:FOLD]), ch)
+    own = unfold(jnp.where(low, to_left[0:FOLD], to_right[0:FOLD]), ch)
+    halo, own = [jnp.where((lanes(ch) & 7) < 4, roll(x, -4), roll(x, 4)) for x in (halo, own)]
+    return gates(pre, ch, 0, strips(halo, own))
+
+
+def rim_fold(h):
+    h = jnp.where((lanes(h.shape[0]) & 7) < 4, roll(h, -16), roll(h, -80))
+    return fold(h).astype(BF16)
+
+
+def patch(row, rim, y):
+    lane = lanes(row.shape[0])
+    base = 8 * y + 16
+    row = jnp.where(lane < 2, roll(rim, -(base + 4)), row)
+    return jnp.where(lane >= 126, roll(rim, 60 - base), row)
+
+
+def finish(step, pre, cell, hid_out, cell_out, hid32):
     ch = cell.shape[0] // 4
     last = step == STEPS - 1
     for y in range(4):
@@ -214,26 +261,18 @@
             hid_out[y * ch : (y + 1) * ch, :] = h.astype(BF16)
     if last:
         hid_out[...] = hid32[...].astype(BF16)
-        return
-    lane = lanes(ch)
-    cells = unfold(jnp.where((lanes(FOLD) & 7) < 4, from_right[0:FOLD], from_left[0:FOLD]), ch)
-    h, _ = gates(pre, ch, 4, jnp.where(lane < 64, roll(cells, 12), roll(cells, 84)))
-    h = jnp.where((lane & 7) < 4, roll(h, -16), roll(h, -80))
-    hid_out[4 * ch : 4 * ch + FOLD, :] = fold(h).astype(BF16)
-
-
-def whole_kernel(step, gathered, from_left, from_right, inp, cell, w, wx, bias, hid_out, cell_out, xs, xi, wxb, pre, inp32, hid32):
+
+
+def whole_kernel(step, gathered, from_right, from_left, inp, cell, w, wx, bias, hid_out, cell_out, xs, xi, wxb, pre, inp32, hid32):
     shards, ch = gathered.shape[0], cell.shape[0] // 4
-    rows, halo = rows_of([gathered[c] for c in range(shards)], ch)
-    store_windows(xs, rows, halo)
-    store_inputs(step, xi, wxb, inp32, inp, from_left, from_right, wx, bias)
+    store_windows(xs, *rows_of([gathered[c] for c in range(shards)], ch))
+    store_inputs(xi, *input_rows(step, inp32, inp, from_right, from_left))
+    store_input_weights(wxb, wx, bias)
     for pair in range(2):
         total = hidden_rows(w, xs, 0, pair) + input_part(wxb, xi, 256 * pair, 256)
         pre[2 * pair] = total[:, 0:128]
         pre[2 * pair + 1] = total[:, 128:256]
-    if step < STEPS - 1:
-        pre[4] = hidden_rim(w, rows, halo, 0) + input_part(wxb, xi, 512, 128)
-    finish(step, pre, cell, from_left, from_right, hid_out, cell_out, hid32)
+    finish(step, pre, cell, hid_out, cell_out, hid32)
 
 
 def first_channel(depth, remote):
@@ -241,32 +280,57 @@
     return pl.multiple_of((1 - mine if remote else mine) * depth, depth)
 
 
-def near_kernel(step, own, other, from_left, from_right, inp, w, wx, bias, part, xs, xi, wxb, inp32):
+def after_kernel(x, before, out):
+    out[...] = x[...]
+
+
+def near_kernel(step, own, other, from_right, from_left, inp, w, wx, bias, part, xs, xi, wxb, inp32):
     ch = w.shape[2] // 4
-    rows, halo = near_far(own[...], other[...], ch)
     at = first_channel(2 * ch, False)
-    store_windows(xs, rows, halo)
-    store_inputs(step, xi, wxb, inp32, inp, from_left, from_right, wx, bias)
+    store_windows(xs, *near_far(own[...], other[...], ch))
+    store_inputs(xi, *input_rows(step, inp32, inp, from_right, from_left))
+    store_input_weights(wxb, wx, bias)
     for pair in range(2):
         total = hidden_rows(w, xs, at, pair) + input_part(wxb, xi, 256 * pair, 256)
         part[2 * pair] = total[:, 0:128]
         part[2 * pair + 1] = total[:, 128:256]
-    if step < STEPS - 1:
-        part[4] = hidden_rim(w, rows, halo, at) + input_part(wxb, xi, 512, 128)
-
-
-def far_kernel(step, same, cross, part, from_left, from_right, cell, w, hid_out, cell_out, xs, pre, hid32):
+
+
+def far_kernel(step, same, cross, part, cell, w, hid_out, cell_out, xs, pre, hid32):
     ch = cell.shape[0] // 4
-    rows, halo = near_far(same[...], cross[...], ch)
     at = first_channel(2 * ch, True)
-    store_windows(xs, rows, halo)
+    store_windows(xs, *near_far(same[...], cross[...], ch))
     for pair in range(2):
         total = hidden_rows(w, xs, at, pair)
         pre[2 * pair] = part[2 * pair] + total[:, 0:128]
         pre[2 * pair + 1] = part[2 * pair + 1] + total[:, 128:256]
-    if step < STEPS - 1:
-        pre[4] = part[4] + hidden_rim(w, rows, halo, at)
-    finish(step, pre, cell, from_left, from_right, hid_out, cell_out, hid32)
+    finish(step, pre, cell, hid_out, cell_out, hid32)
+
+
+def rim_kernel(*refs):
+    *blocks, hid, cell, to_right, to_left, from_right, from_left, inp, w, wx, bias = refs[:-6]
+    hid_out, cell_out, xi, wxb, pre, inp32 = refs[-6:]
+    ch = cell.shape[0] // 4
+    if len(blocks) == 4:
+        even, first = lax.axis_index("chan") % 2 == 0, lax.axis_index("chan") // 2 == 0
+        own, other, same, cross = [b[...] for b in blocks]
+        here = (jnp.where(even, own, other), jnp.where(even, other, own))
+        there = (jnp.where(even, same, cross), jnp.where(even, cross, same))
+        shards = [jnp.where(first, here[k], there[k]) for k in (0, 1)]
+        shards += [jnp.where(first, there[k], here[k]) for k in (0, 1)]
+    else:
+        shards = [blocks[0][c] for c in range(blocks[0].shape[0])]
+    halo = jnp.concatenate([unfold(s[0:FOLD].astype(F32), ch) for s in shards], axis=0).astype(BF16)
+    own = jnp.concatenate([unfold(s[FOLD:].astype(F32), ch) for s in shards], axis=0).astype(BF16)
+    store_input_rim(xi, *input_rows(0, inp32, inp, from_right, from_left))
+    store_input_weights(wxb, wx, bias)
+    pre[0] = hidden_rim(w, strips(halo, own)) + input_part(wxb, xi, 0, 128)
+    h, c = rim_gates(pre, to_right, to_left, from_right, from_left, ch)
+    for y in range(4):
+        at = slice(y * ch, (y + 1) * ch)
+        hid_out[at, :] = patch(hid[at, :].astype(F32), h, y).astype(BF16)
+        cell_out[at, :] = patch(cell[at, :], c, y)
+    hid_out[4 * ch : 4 * ch + FOLD, :] = rim_fold(h)
 
 
 def call(kernel, outs, scratch, *args, far=0, us=1):
@@ -292,45 +356,70 @@
     inp = inputs.reshape(-1, cols)
     wx = jnp.transpose(w_input, (0, 1, 3, 2)).reshape(25 * cin, gate)
     bias = gate_bias.reshape(1, gate)
-    to_left, to_right, main = call(
+    to_right, to_left, hid = call(
         pack_kernel,
-        [((FOLD + 8, 128), F32), ((FOLD + 8, 128), F32), ((4 * ch, 128), BF16)],
+        [((FOLD + 8, 128), F32), ((FOLD + 8, 128), F32), ((4 * ch, 128), F32)],
         [(hid.shape, BF16), (cell.shape, F32), (inp.shape, BF16), (hid.shape, F32), (inp.shape, F32)],
         hid, cell, inp, far=3, us=1,
     )
+    (main,) = call(main_kernel, [((4 * ch, 128), BF16)], [], hid, us=0.01)
     n = lax.axis_size("lon")
-    from_right = lax.ppermute(to_left, "lon", [((i + 1) % n, i) for i in range(n)])
-    from_left = lax.ppermute(to_right, "lon", [(i, (i + 1) % n) for i in range(n)])
-    (field,) = call(join_kernel, [((4 * ch + FOLD, 128), BF16)], [], main, from_left, from_right)
+    came_left = lax.ppermute(to_right, "lon", [(i, (i + 1) % n) for i in range(n)])
+    came_right = lax.ppermute(to_left, "lon", [((i + 1) % n, i) for i in range(n)])
+    from_right, from_left, strip = call(
+        strip_kernel, [(to_left.shape, F32), (to_left.shape, F32), ((2 * FOLD, 128), BF16)], [],
+        came_left, came_right, to_right, to_left,
+    )
     shards = lax.axis_size("chan")
+    paired = shards == 4 and 2 * ch == 128
+
+    def others(x):
+        return [lax.ppermute(x, "chan", [(i, i ^ k) for i in range(shards)]) for k in (1, 2)]
+
+    def onward(same, before):
+        (same,) = call(after_kernel, [(same.shape, BF16)], [], same, before, us=0.01)
+        return same, lax.ppermute(same, "chan", [(i, i ^ 1) for i in range(shards)])
+
+    field = main
+    traveling = [lax.ppermute(field, "chan", [(i, i ^ k) for i in range(shards)]) for k in (1, 2, 3)] if paired else None
+    blocks = [strip, *[lax.ppermute(strip, "chan", [(i, i ^ k) for i in range(shards)]) for k in (1, 2, 3)]] if paired else [lax.all_gather(strip, "chan", axis=0)]
+    kinds = [((25 * cin + 16, gate), BF16)]
     for step in range(STEPS):
         last = step == STEPS - 1
-        wide = 512 if last else 640
-        stack = [((25 * cin + 16, wide), BF16), ((25 * cin + 16, gate), BF16)]
+        stack = [((25 * cin + 16, 512), BF16), *kinds]
         inp32 = (inp.shape, F32)
         hid32 = ((4 * ch, 128), F32)
-        pre = ((wide // 128, gate, 128), F32)
-        outs = [((4 * ch + (0 if last else FOLD), 128), BF16), ((4 * ch, 128), F32)]
-        if shards == 4 and 2 * ch == 128:
-            other, same, cross = [
-                lax.ppermute(field, "chan", [(i, i ^ k) for i in range(shards)]) for k in (1, 2, 3)
-            ]
+        pre = ((4, gate, 128), F32)
+        outs = [((4 * ch, 128), BF16), ((4 * ch, 128), F32)]
+        if paired:
+            other, same, *cross = traveling
             windowed = ((5, 2 * ch, 768), BF16)
             (part,) = call(
                 functools.partial(near_kernel, step), [pre], [windowed, *stack, inp32],
-                field, other, from_left, from_right, inp, w_hidden, wx, bias, us=1.5,
+                field, other, from_right, from_left, inp, w_hidden, wx, bias, us=0.01,
             )
+            if cross:
+                (cross,) = cross
+            else:
+                same, cross = onward(same, part)
             field, cell = call(
                 functools.partial(far_kernel, step), outs, [windowed, pre, hid32],
-                same, cross, part, from_left, from_right, cell, w_hidden, us=2,
+                same, cross, part, cell, w_hidden, us=0.01,
             )
         else:
             gathered = lax.all_gather(field, "chan", axis=0)
             field, cell = call(
                 functools.partial(whole_kernel, step), outs,
                 [((5, depth, 768), BF16), *stack, pre, inp32, hid32],
-                gathered, from_left, from_right, inp, cell, w_hidden, wx, bias, us=3,
+                gathered, from_right, from_left, inp, cell, w_hidden, wx, bias, us=3,
             )
+        if not last:
+            field, cell = call(
+                rim_kernel, [((4 * ch + FOLD, 128), BF16), ((4 * ch, 128), F32)],
+                [((25 * cin + 16, 128), BF16), *kinds, ((1, gate, 128), F32), inp32],
+                *blocks, field, cell, to_right, to_left, from_right, from_left, inp, w_hidden, wx, bias, us=0.01,
+            )
+            traveling = others(field) if paired else None
     return field.reshape(ch, rows, cols), cell.reshape(ch, rows, cols)
 
 

time: 25 us -> 23.9 us (0.956)
  waiting for transfers between devices: 6.12 us -> 3.35 us
  starting transfers between devices: 9.55 us -> 11.1 us
    ppermute x6 -> x3, waiting for transfers between devices: 4.39 us -> 0.63 us  [shards(): lax.ppermute(field, 'chan', [(i, i ^ k) for i in range(shards)])]
    ppermute x0 -> x6, starting transfers between devices: none -> 3.69 us  [the longest x3 1.94 us: shards(): lax.ppermute(strip, 'chan', [(i, i ^ k) for i in range(shards)])]
    ppermute x0 -> x6, waiting for transfers between devices: none -> 2.72 us  [the longest x2 1.46 us: others(): lax.ppermute(x, 'chan', [(i, i ^ k) for i in range(shards)])]
    ppermute x6 -> x3, starting transfers between devices: 4.38 us -> 2.21 us  [shards(): lax.ppermute(field, 'chan', [(i, i ^ k) for i in range(shards)])]
    ppermute x1, waiting for transfers between devices: 1.71 us -> 0.01 us  [shards(): lax.ppermute(to_right, 'lon', [(i, (i + 1) % n) for i in range(n)])]
    pallas_call x6 -> x9, Pallas kernels: 8.39 us -> 8.53 us  [call(): pl.pallas_call(kernel, out_shape=[jax.ShapeDtypeStruct(s, d) for s, d in...]
  transfers between devices with their start and end apart: 8 -> 11, of which waited for: 5 -> 3; matrix products, arithmetic and copies ran while one was open for 0% -> 0% of each run, Pallas kernels for 14% -> 16%
where the time goes in v4:
time: 23.9 us; the launch traced here: 23.8 us
  starting transfers between devices  11.1 us (46%)
  Pallas kernels  8.53 us (36%)
  waiting for transfers between devices  3.35 us (14%)
  between operations  0.78 us (3%)
    pallas_call x9, Pallas kernels, call(): pl.pallas_call(kernel, out_shape=[jax.ShapeDtypeStruct(s, d) for s, d in...  8.53 us
    ppermute x1, starting transfers between devices, shards(): lax.ppermute(to_right, 'lon', [(i, (i + 1) % n) for i in range(n)])  3.08 us
    ppermute x3, starting transfers between devices, shards(): lax.ppermute(field, 'chan', [(i, i ^ k) for i in range(shards)])  2.21 us
    ppermute x1, starting transfers between devices, shards(): lax.ppermute(to_left, 'lon', [((i + 1) % n, i) for i in range(n)])  2.09 us
    ppermute x3, starting transfers between devices, shards(): lax.ppermute(strip, 'chan', [(i, i ^ k) for i in range(shards)])  1.94 us
    ppermute x2, starting transfers between devices, others(): lax.ppermute(x, 'chan', [(i, i ^ k) for i in range(shards)])  1.74 us
    ppermute x2, waiting for transfers between devices, others(): lax.ppermute(x, 'chan', [(i, i ^ k) for i in range(shards)])  1.46 us
    ppermute x1, waiting for transfers between devices, onward(): lax.ppermute(same, 'chan', [(i, i ^ 1) for i in range(shards)])  1.25 us
  transfers between devices with their start and end apart: 11, of which 3 were waited for; matrix products, arithmetic and copies ran while one was open for 0% of the time, Pallas kernels for 16%

profile of v4, /device:TPU:0, one launch (start us, length us, event | category | flops | bytes accessed | tf_op | source)
XLA Modules:
  0.0 23.8 jit_solution(1666946432012095563)
XLA Ops:
  0.6 0.0 copy-start
  0.7 1.3 %shard_map.77 = (f32[24,128]{1,0:T(8,128)S(1)}, f32[24,128]{1,0:T(8,128)S(1)}, f32[256,128]{1,0:T(8,128)S(1)}) custom-call(bf16[256,128]{1,0:T(8,128)(2,1)} %bitcast.22, f32[256,128]{1,0:T(8,128)} %bitcast.16, bf16[128,128]{1,0:T(8,128)(2,1)} %bitcast.12), custom_call_target="tpu_custom_call" | custom-call | flops 1000000000 | tf_op jit(solution)/shard_map/pallas_call | solution.py:337
  2.0 3.1 %collective-permute-start = (f32[24,128]{1,0:T(8,128)S(1)}, f32[24,128]{1,0:T(8,128)S(1)}, u32[]{:S(2)}, u32[]{:S(2)}) collective-permute-start(f32[24,128]{1,0:T(8,128)S(1)} %get-tuple-element.14.to_right.refs_6_), channel_id=1, source_target_pairs={{0,4},{4,8},{8,12},{12,0},{1,5},{5,9},{9,13},{13,1},{2,6},{6,10},{... | collective-permute-start | bytes 36872 | tf_op jit(solution)/shard_map/ppermute | solution.py:367
  5.1 2.1 %collective-permute-start.1 = (f32[24,128]{1,0:T(8,128)S(1)}, f32[24,128]{1,0:T(8,128)S(1)}, u32[]{:S(2)}, u32[]{:S(2)}) collective-permute-start(f32[24,128]{1,0:T(8,128)S(1)} %get-tuple-element.15.to_left.refs_7_), channel_id=1, source_target_pairs={{4,0},{8,4},{12,8},{0,12},{5,1},{9,5},{13,9},{1,13},{6,2},{10,6},{... | collective-permute-start | bytes 36872 | tf_op jit(solution)/shard_map/ppermute | solution.py:368
  7.2 0.0 copy-start.3
  7.2 0.1 collective-permute-start.7
  7.3 1.8 %collective-permute-start.6 = (bf16[256,128]{1,0:T(8,128)(2,1)S(1)}, bf16[256,128]{1,0:T(8,128)(2,1)S(1)}, u32[]{:S(2)}, u32[]{:S(2)}) collective-permute-start(bf16[256,128]{1,0:T(8,128)(2,1)S(1)} %shard_map.79.own), channel_id=1, source_target_pairs={{0,3},{1,2},{2,1},{3,0},{4,7},{5,6},{6,5},{7,4},{8,11},{9,10},{10,... | collective-permute-start | bytes 196616 | tf_op jit(solution)/shard_map/ppermute | solution.py:384
  9.0 0.4 %collective-permute-start.5 = (bf16[256,128]{1,0:T(8,128)(2,1)S(1)}, bf16[256,128]{1,0:T(8,128)(2,1)S(1)}, u32[]{:S(2)}, u32[]{:S(2)}) collective-permute-start(bf16[256,128]{1,0:T(8,128)(2,1)S(1)} %shard_map.79.own), channel_id=1, source_target_pairs={{0,2},{1,3},{2,0},{3,1},{4,6},{5,7},{6,4},{7,5},{8,10},{9,11},{10,... | collective-permute-start | bytes 196616 | tf_op jit(solution)/shard_map/ppermute | solution.py:384
  9.4 0.0 collective-permute-done.came_left
  9.4 0.0 collective-permute-done.1.came_right
  9.4 1.1 %collective-permute-start.4 = (bf16[32,128]{1,0:T(8,128)(2,1)S(1)}, bf16[32,128]{1,0:T(8,128)(2,1)S(1)}, u32[]{:S(2)}, u32[]{:S(2)}) collective-permute-start(bf16[32,128]{1,0:T(8,128)(2,1)S(1)} %get-tuple-element.16.refs_0_), channel_id=1, source_target_pairs={{0,3},{1,2},{2,1},{3,0},{4,7},{5,6},{6,5},{7,4},{8,11},{9,10},{10,... | collective-permute-start | bytes 24584 | tf_op jit(solution)/shard_map/ppermute | solution.py:385
  10.5 0.7 %collective-permute-start.3 = (bf16[32,128]{1,0:T(8,128)(2,1)S(1)}, bf16[32,128]{1,0:T(8,128)(2,1)S(1)}, u32[]{:S(2)}, u32[]{:S(2)}) collective-permute-start(bf16[32,128]{1,0:T(8,128)(2,1)S(1)} %get-tuple-element.16.refs_0_), channel_id=1, source_target_pairs={{0,2},{1,3},{2,0},{3,1},{4,6},{5,7},{6,4},{7,5},{8,10},{9,11},{10,... | collective-permute-start | bytes 24584 | tf_op jit(solution)/shard_map/ppermute | solution.py:385
  11.2 0.0 collective-permute-done.7.other
  11.2 0.1 collective-permute-start.2
  11.4 0.0 copy-done.2
  11.4 1.3 %shard_map.80.part = f32[4,256,128]{2,1,0:T(8,128)S(1)} custom-call(bf16[256,128]{1,0:T(8,128)(2,1)S(1)} %shard_map.79.own, bf16[256,128]{1,0:T(8,128)(2,1)S(1)} %collective-permute-done.7.other, f32[24,128]{1,0:T(8,128)S(1)} %get-tuple-element.18.from_right.refs_8_, f32[24,128]{1,0:T(8,128)S(1)} %get-tuple-element.19.from_left.refs_9_, ...), custom_call_target="tpu_custom_call" | custom-call | flops 10000000 | tf_op jit(solution)/shard_map/pallas_call | solution.py:337
  12.7 0.0 collective-permute-done.6.cross
  12.7 0.6 %collective-permute-done.5.same = bf16[256,128]{1,0:T(8,128)(2,1)S(1)} collective-permute-done((bf16[256,128]{1,0:T(8,128)(2,1)S(1)}, bf16[256,128]{1,0:T(8,128)(2,1)S(1)}, u32[]{:S(2)}, u32[]{:S(2)}) %collective-permute-start.5) | collective-permute-done | bytes 65568 | tf_op jit(solution)/shard_map/ppermute | solution.py:384
  13.3 0.0 copy-done.3
  13.3 1.1 %shard_map.81 = (bf16[256,128]{1,0:T(8,128)(2,1)S(1)}, f32[256,128]{1,0:T(8,128)S(1)}) custom-call(bf16[256,128]{1,0:T(8,128)(2,1)S(1)} %collective-permute-done.5.same, bf16[256,128]{1,0:T(8,128)(2,1)S(1)} %collective-permute-done.6.cross, f32[4,256,128]{2,1,0:T(8,128)S(1)} %shard_map.80.part, f32[256,128]{1,0:T(8,128)S(1)} %bitcast.17, ...), custom_call_target="tpu_custom_call" | custom-call | flops 10000000 | tf_op jit(solution)/shard_map/pallas_call | solution.py:337
  14.4 0.0 collective-permute-done.4.refs_3_
  14.4 0.0 collective-permute-done.3.refs_2_
  14.4 0.0 collective-permute-done.2.refs_1_
  14.4 1.6 %shard_map.82 = (bf16[272,128]{1,0:T(8,128)(2,1)S(1)}, f32[256,128]{1,0:T(8,128)S(1)}) custom-call(bf16[32,128]{1,0:T(8,128)(2,1)S(1)} %get-tuple-element.16.refs_0_, bf16[32,128]{1,0:T(8,128)(2,1)S(1)} %collective-permute-done.2.refs_1_, bf16[32,128]{1,0:T(8,128)(2,1)S(1)} %collective-permute-done.3.refs_2_, ...), custom_call_target="tpu_custom_call" | custom-call | flops 10000000 | tf_op jit(solution)/shard_map/pallas_call | solution.py:337
  15.9 0.0 collective-permute-start.9
  16.0 1.7 %collective-permute-start.8 = (bf16[272,128]{1,0:T(8,128)(2,1)S(1)}, bf16[272,128]{1,0:T(8,128)(2,1)S(1)}, u32[]{:S(2)}, u32[]{:S(2)}) collective-permute-start(bf16[272,128]{1,0:T(8,128)(2,1)S(1)} %get-tuple-element.22.own), channel_id=1, source_target_pairs={{0,2},{1,3},{2,0},{3,1},{4,6},{5,7},{6,4},{7,5},{8,10},{9,11},{10,... | collective-permute-start | bytes 208904 | tf_op jit(solution)/shard_map/ppermute | solution.py:377
  17.7 0.0 collective-permute-done.9.other
  17.7 1.4 %shard_map.83.before.part = f32[4,256,128]{2,1,0:T(8,128)S(1)} custom-call(bf16[272,128]{1,0:T(8,128)(2,1)S(1)} %get-tuple-element.22.own, bf16[272,128]{1,0:T(8,128)(2,1)S(1)} %collective-permute-done.9.other, f32[24,128]{1,0:T(8,128)S(1)} %get-tuple-element.18.from_right.refs_8_, f32[24,128]{1,0:T(8,128)S(1)} %get-tuple-element.19.from_left.refs_9_, ...), custom_call_target="tpu_custom_call" | custom-call | flops 10000000 | tf_op jit(solution)/shard_map/pallas_call | solution.py:337
  19.1 1.5 %collective-permute-done.8.x = bf16[272,128]{1,0:T(8,128)(2,1)S(1)} collective-permute-done((bf16[272,128]{1,0:T(8,128)(2,1)S(1)}, bf16[272,128]{1,0:T(8,128)(2,1)S(1)}, u32[]{:S(2)}, u32[]{:S(2)}) %collective-permute-start.8) | collective-permute-done | bytes 69664 | tf_op jit(solution)/shard_map/ppermute | solution.py:377
  20.6 0.0 collective-permute-start.10
  20.6 1.3 %collective-permute-done.10.cross = bf16[272,128]{1,0:T(8,128)(2,1)S(1)} collective-permute-done((bf16[272,128]{1,0:T(8,128)(2,1)S(1)}, bf16[272,128]{1,0:T(8,128)(2,1)S(1)}, u32[]{:S(2)}, u32[]{:S(2)}) %collective-permute-start.10) | collective-permute-done | bytes 69664 | tf_op jit(solution)/shard_map/ppermute | solution.py:381
  21.9 1.9 %shard_map.85 = (bf16[256,128]{1,0:T(8,128)(2,1)}, f32[256,128]{1,0:T(8,128)}) custom-call(bf16[272,128]{1,0:T(8,128)(2,1)S(1)} %shard_map.84.same, bf16[272,128]{1,0:T(8,128)(2,1)S(1)} %collective-permute-done.10.cross, f32[4,256,128]{2,1,0:T(8,128)S(1)} %shard_map.83.before.part, f32[256,128]{1,0:T(8,128)S(1)} %get-tuple-element.23.cell, ...), custom_call_target="tpu_custom_call" | custom-call | flops 10000000 | tf_op jit(solution)/shard_map/pallas_call | solution.py:337
  (9 shorter events, 0.0 us)
Async XLA Ops:
  0.6 10.7 %copy-start = (bf16[5,5,256,256]{3,2,1,0:T(8,128)(2,1)S(1)}, bf16[5,5,256,256]{3,2,1,0:T(8,128)(2,1)}, u32[]{:S(2)}) copy-start(bf16[5,5,256,256]{3,2,1,0:T(8,128)(2,1)} %w.7) | copy-start | bytes 9830404
  0.6 10.7 %copy-start.1 = (bf16[5,5,256,16]{2,3,1,0:T(8,128)(2,1)S(1)}, bf16[5,5,256,16]{2,3,1,0:T(8,128)(2,1)}, u32[]{:S(2)}) copy-start(bf16[5,5,256,16]{2,3,1,0:T(8,128)(2,1)} %param.9) | copy-start | bytes 614404
  0.7 10.7 %copy-start.2 = (bf16[2,16,4,128]{3,2,1,0:T(4,128)(2,1)S(1)}, bf16[2,16,4,128]{3,2,1,0:T(4,128)(2,1)}, u32[]{:S(2)}) copy-start(bf16[2,16,4,128]{3,2,1,0:T(4,128)(2,1)} %param.6) | copy-start | bytes 98308
  0.7 10.7 %copy-start.4 = (f32[256]{0:T(256)S(1)}, f32[256]{0:T(256)}, u32[]{:S(2)}) copy-start(f32[256]{0:T(256)} %param.11) | copy-start | bytes 3076
  2.0 7.4 %collective-permute-start = (f32[24,128]{1,0:T(8,128)S(1)}, f32[24,128]{1,0:T(8,128)S(1)}, u32[]{:S(2)}, u32[]{:S(2)}) collective-permute-start(f32[24,128]{1,0:T(8,128)S(1)} %get-tuple-element.14.to_right.refs_6_), channel_id=1, source_target_pairs={{0,4},{4,8},{8,12},{12,0},{1,5},{5,9},{9,13},{13,1},{2,6},{6,10},{... | collective-permute-start | bytes 36872 | tf_op jit(solution)/shard_map/ppermute | solution.py:367
  5.1 4.3 %collective-permute-start.1 = (f32[24,128]{1,0:T(8,128)S(1)}, f32[24,128]{1,0:T(8,128)S(1)}, u32[]{:S(2)}, u32[]{:S(2)}) collective-permute-start(f32[24,128]{1,0:T(8,128)S(1)} %get-tuple-element.15.to_left.refs_7_), channel_id=1, source_target_pairs={{4,0},{8,4},{12,8},{0,12},{5,1},{9,5},{13,9},{1,13},{6,2},{10,6},{... | collective-permute-start | bytes 36872 | tf_op jit(solution)/shard_map/ppermute | solution.py:368
  7.2 6.1 %copy-start.3 = (f32[64,4,128]{2,1,0:T(4,128)S(1)}, f32[64,4,128]{2,1,0:T(4,128)}, u32[]{:S(2)}) copy-start(f32[64,4,128]{2,1,0:T(4,128)} %param.8) | copy-start | bytes 393220
  7.2 4.0 %collective-permute-start.7 = (bf16[256,128]{1,0:T(8,128)(2,1)S(1)}, bf16[256,128]{1,0:T(8,128)(2,1)S(1)}, u32[]{:S(2)}, u32[]{:S(2)}) collective-permute-start(bf16[256,128]{1,0:T(8,128)(2,1)S(1)} %shard_map.79.own), channel_id=1, source_target_pairs={{0,1},{1,0},{2,3},{3,2},{4,5},{5,4},{6,7},{7,6},{8,9},{9,8},{10,11... | collective-permute-start | bytes 196616 | tf_op jit(solution)/shard_map/ppermute | solution.py:384
  7.3 5.4 %collective-permute-start.6 = (bf16[256,128]{1,0:T(8,128)(2,1)S(1)}, bf16[256,128]{1,0:T(8,128)(2,1)S(1)}, u32[]{:S(2)}, u32[]{:S(2)}) collective-permute-start(bf16[256,128]{1,0:T(8,128)(2,1)S(1)} %shard_map.79.own), channel_id=1, source_target_pairs={{0,3},{1,2},{2,1},{3,0},{4,7},{5,6},{6,5},{7,4},{8,11},{9,10},{10,... | collective-permute-start | bytes 196616 | tf_op jit(solution)/shard_map/ppermute | solution.py:384
  9.0 4.3 %collective-permute-start.5 = (bf16[256,128]{1,0:T(8,128)(2,1)S(1)}, bf16[256,128]{1,0:T(8,128)(2,1)S(1)}, u32[]{:S(2)}, u32[]{:S(2)}) collective-permute-start(bf16[256,128]{1,0:T(8,128)(2,1)S(1)} %shard_map.79.own), channel_id=1, source_target_pairs={{0,2},{1,3},{2,0},{3,1},{4,6},{5,7},{6,4},{7,5},{8,10},{9,11},{10,... | collective-permute-start | bytes 196616 | tf_op jit(solution)/shard_map/ppermute | solution.py:384
  9.4 4.9 %collective-permute-start.4 = (bf16[32,128]{1,0:T(8,128)(2,1)S(1)}, bf16[32,128]{1,0:T(8,128)(2,1)S(1)}, u32[]{:S(2)}, u32[]{:S(2)}) collective-permute-start(bf16[32,128]{1,0:T(8,128)(2,1)S(1)} %get-tuple-element.16.refs_0_), channel_id=1, source_target_pairs={{0,3},{1,2},{2,1},{3,0},{4,7},{5,6},{6,5},{7,4},{8,11},{9,10},{10,... | collective-permute-start | bytes 24584 | tf_op jit(solution)/shard_map/ppermute | solution.py:385
  10.5 3.9 %collective-permute-start.3 = (bf16[32,128]{1,0:T(8,128)(2,1)S(1)}, bf16[32,128]{1,0:T(8,128)(2,1)S(1)}, u32[]{:S(2)}, u32[]{:S(2)}) collective-permute-start(bf16[32,128]{1,0:T(8,128)(2,1)S(1)} %get-tuple-element.16.refs_0_), channel_id=1, source_target_pairs={{0,2},{1,3},{2,0},{3,1},{4,6},{5,7},{6,4},{7,5},{8,10},{9,11},{10,... | collective-permute-start | bytes 24584 | tf_op jit(solution)/shard_map/ppermute | solution.py:385
  11.2 3.2 %collective-permute-start.2 = (bf16[32,128]{1,0:T(8,128)(2,1)S(1)}, bf16[32,128]{1,0:T(8,128)(2,1)S(1)}, u32[]{:S(2)}, u32[]{:S(2)}) collective-permute-start(bf16[32,128]{1,0:T(8,128)(2,1)S(1)} %get-tuple-element.16.refs_0_), channel_id=1, source_target_pairs={{0,1},{1,0},{2,3},{3,2},{4,5},{5,4},{6,7},{7,6},{8,9},{9,8},{10,11... | collective-permute-start | bytes 24584 | tf_op jit(solution)/shard_map/ppermute | solution.py:385
  15.9 1.8 %collective-permute-start.9 = (bf16[272,128]{1,0:T(8,128)(2,1)S(1)}, bf16[272,128]{1,0:T(8,128)(2,1)S(1)}, u32[]{:S(2)}, u32[]{:S(2)}) collective-permute-start(bf16[272,128]{1,0:T(8,128)(2,1)S(1)} %get-tuple-element.22.own), channel_id=1, source_target_pairs={{0,1},{1,0},{2,3},{3,2},{4,5},{5,4},{6,7},{7,6},{8,9},{9,8},{10,11... | collective-permute-start | bytes 208904 | tf_op jit(solution)/shard_map/ppermute | solution.py:377
  16.0 4.6 %collective-permute-start.8 = (bf16[272,128]{1,0:T(8,128)(2,1)S(1)}, bf16[272,128]{1,0:T(8,128)(2,1)S(1)}, u32[]{:S(2)}, u32[]{:S(2)}) collective-permute-start(bf16[272,128]{1,0:T(8,128)(2,1)S(1)} %get-tuple-element.22.own), channel_id=1, source_target_pairs={{0,2},{1,3},{2,0},{3,1},{4,6},{5,7},{6,4},{7,5},{8,10},{9,11},{10,... | collective-permute-start | bytes 208904 | tf_op jit(solution)/shard_map/ppermute | solution.py:377
  20.6 1.3 %collective-permute-start.10 = (bf16[272,128]{1,0:T(8,128)(2,1)S(1)}, bf16[272,128]{1,0:T(8,128)(2,1)S(1)}, u32[]{:S(2)}, u32[]{:S(2)}) collective-permute-start(bf16[272,128]{1,0:T(8,128)(2,1)S(1)} %shard_map.84.same), channel_id=1, source_target_pairs={{0,1},{1,0},{2,3},{3,2},{4,5},{5,4},{6,7},{7,6},{8,9},{9,8},{10,11... | collective-permute-start | bytes 208904 | tf_op jit(solution)/shard_map/ppermute | solution.py:381

commit v5 on v4

--- a/solution.py
+++ b/solution.py
@@ -50,9 +50,11 @@
     return jnp.concatenate(left, axis=0), jnp.concatenate(right, axis=0)
 
 
-def pack_kernel(hid_far, cell_far, inp_far, to_right, to_left, hid_out, hid, cell, inp, hid32, inp32, arrived):
+def pack_kernel(*refs):
+    fars, (to_right, to_left, hid_out, weights, part) = refs[:5], refs[5:10]
+    hid, cell, inp, wx, bias, hid32, inp32, xi, arrived = refs[10:]
     ch = hid.shape[0] // 4
-    pairs = ((hid_far, hid), (cell_far, cell), (inp_far, inp))
+    pairs = tuple(zip(fars, (hid, cell, inp, wx, bias)))
     copies = [pltpu.make_async_copy(a, b, arrived.at[i]) for i, (a, b) in enumerate(pairs)]
     for copy in copies:
         copy.start()
@@ -69,6 +71,10 @@
     to_right[FOLD:] = ir
     hid_out[...] = hid32[...]
 
+    @pl.when(lax.axis_index("lon") == 0)
+    def _():
+        drive(inp, inp32, wx, bias, weights, part, xi)
+
 
 def main_kernel(hid, main):
     ch = hid.shape[0] // 4
@@ -125,13 +131,8 @@
     return sigmoid(part[3]) * jnp.tanh(cell), cell
 
 
-DRIVE = (((0,), (0,)), ((), ()))
-
-
 def near_far(own, other, ch):
-    even = lax.axis_index("chan") % 2 == 0
-    low, high = jnp.where(even, own, other), jnp.where(even, other, own)
-    return rows_of([low, high], ch)
+    return rows_of(ordered(own, other), ch)
 
 
 def rows_of(shards, ch):
@@ -160,11 +161,11 @@
     return jnp.dot(left, right, preferred_element_type=F32)
 
 
-def hidden_rim(w, strip):
+def hidden_rim(w, strip, at):
     stack = jnp.concatenate([roll(strip, -8 * (a - 2)) for a in range(5)], axis=0)
     total = None
     for b in range(5):
-        left = jnp.concatenate([w[a, b] for a in range(5)], axis=1)
+        left = jnp.concatenate([w[a, b, :, pl.ds(at, strip.shape[0])] for a in range(5)], axis=1)
         part = roll(jnp.dot(left, stack, preferred_element_type=F32), -(b - 2))
         total = part if total is None else total + part
     return total
@@ -182,7 +183,7 @@
 
 
 def store_inputs(xi, rows, halo):
-    cin = halo.shape[0]
+    cin = rows[0].shape[0]
     wins = [windows(rows[y], halo, y) for y in range(4)]
     for a in range(5):
         for b in range(5):
@@ -208,23 +209,44 @@
 def store_ones(xi, taps):
     ones = lax.broadcasted_iota(jnp.int32, (16, xi.shape[1]), 0) < 3
     xi[taps : taps + 16, :] = jnp.where(ones, 1.0, 0.0).astype(BF16)
-
-
-def store_input_weights(wxb, wx, bias):
-    taps = wx.shape[0]
-    wxb[0:taps, :] = wx[...]
+    xi[taps + 16 :, :] = jnp.zeros((xi.shape[0] - taps - 16, xi.shape[1]), BF16)
+
+
+def input_weights(wx, bias):
+    taps, gate = wx.shape
     b0 = bias[...]
     b1 = b0.astype(BF16).astype(F32)
     b2 = (b0 - b1).astype(BF16).astype(F32)
     b3 = b0 - b1 - b2
-    sub = lax.broadcasted_iota(jnp.int32, (16, wxb.shape[1]), 0)
-    wxb[taps : taps + 16, :] = jnp.where(
-        sub == 0, b1, jnp.where(sub == 1, b2, jnp.where(sub == 2, b3, 0.0))
-    ).astype(BF16)
-
-
-def input_part(wxb, xi, at, wide):
-    return lax.dot_general(wxb[...], xi[:, at : at + wide], DRIVE, preferred_element_type=F32)
+    sub = lax.broadcasted_iota(jnp.int32, (16, gate), 0)
+    extra = jnp.where(sub == 0, b1, jnp.where(sub == 1, b2, jnp.where(sub == 2, b3, 0.0)))
+    blank = jnp.zeros((padded(taps) - taps - 16, gate), F32)
+    return jnp.concatenate([wx[...].astype(F32), extra, blank], axis=0).T.astype(BF16)
+
+
+def padded(taps):
+    return (taps + 16 + 127) // 128 * 128
+
+
+def drive(inp, inp32, wx, bias, weights, part, xi):
+    cin = inp.shape[0] // (4 * STEPS)
+    inp32[...] = inp[...].astype(F32)
+    weights[...] = input_weights(wx, bias)
+    store_inputs(xi, [inp32[pl.ds(y, cin, stride=4), :].astype(BF16) for y in range(4)], None)
+    for pair in range(2):
+        total = input_part(weights, xi, 256 * pair, 256)
+        part[2 * pair] = total[:, 0:128]
+        part[2 * pair + 1] = total[:, 128:256]
+
+
+def drive_kernel(inp, wx, bias, weights_in, part_in, weights, part, inp32, xi):
+    @pl.when(lax.axis_index("lon") != 0)
+    def _():
+        drive(inp, inp32, wx, bias, weights, part, xi)
+
+
+def input_part(weights, xi, at, wide):
+    return jnp.dot(weights[...], xi[:, at : at + wide], preferred_element_type=F32)
 
 
 def rim_gates(pre, to_right, to_left, from_right, from_left, ch):
@@ -263,15 +285,13 @@
         hid_out[...] = hid32[...].astype(BF16)
 
 
-def whole_kernel(step, gathered, from_right, from_left, inp, cell, w, wx, bias, hid_out, cell_out, xs, xi, wxb, pre, inp32, hid32):
+def whole_kernel(step, gathered, driven, cell, w, hid_out, cell_out, xs, pre, hid32):
     shards, ch = gathered.shape[0], cell.shape[0] // 4
     store_windows(xs, *rows_of([gathered[c] for c in range(shards)], ch))
-    store_inputs(xi, *input_rows(step, inp32, inp, from_right, from_left))
-    store_input_weights(wxb, wx, bias)
     for pair in range(2):
-        total = hidden_rows(w, xs, 0, pair) + input_part(wxb, xi, 256 * pair, 256)
-        pre[2 * pair] = total[:, 0:128]
-        pre[2 * pair + 1] = total[:, 128:256]
+        total = hidden_rows(w, xs, 0, pair)
+        pre[2 * pair] = driven[2 * pair] + total[:, 0:128]
+        pre[2 * pair + 1] = driven[2 * pair + 1] + total[:, 128:256]
     finish(step, pre, cell, hid_out, cell_out, hid32)
 
 
@@ -284,22 +304,29 @@
     out[...] = x[...]
 
 
-def near_kernel(step, own, other, from_right, from_left, inp, w, wx, bias, part, xs, xi, wxb, inp32):
+def near_kernel(own, other, driven, w, part, xs):
     ch = w.shape[2] // 4
     at = first_channel(2 * ch, False)
-    store_windows(xs, *near_far(own[...], other[...], ch))
+    store_windows(xs, *near_far(own, other, ch))
+    for pair in range(2):
+        total = hidden_rows(w, xs, at, pair)
+        part[2 * pair] = driven[2 * pair] + total[:, 0:128]
+        part[2 * pair + 1] = driven[2 * pair + 1] + total[:, 128:256]
+
+
+def next_drive_kernel(step, from_right, from_left, inp, weights, before, part, xi, inp32):
     store_inputs(xi, *input_rows(step, inp32, inp, from_right, from_left))
-    store_input_weights(wxb, wx, bias)
     for pair in range(2):
-        total = hidden_rows(w, xs, at, pair) + input_part(wxb, xi, 256 * pair, 256)
+        total = input_part(weights, xi, 256 * pair, 256)
         part[2 * pair] = total[:, 0:128]
         part[2 * pair + 1] = total[:, 128:256]
 
 
-def far_kernel(step, same, cross, part, cell, w, hid_out, cell_out, xs, pre, hid32):
+def far_kernel(step, same, cross, part, cell, w, *refs):
     ch = cell.shape[0] // 4
+    hid_out, cell_out, xs, pre, hid32 = refs[-5:]
     at = first_channel(2 * ch, True)
-    store_windows(xs, *near_far(same[...], cross[...], ch))
+    store_windows(xs, *near_far(same, cross, ch))
     for pair in range(2):
         total = hidden_rows(w, xs, at, pair)
         pre[2 * pair] = part[2 * pair] + total[:, 0:128]
@@ -307,24 +334,74 @@
     finish(step, pre, cell, hid_out, cell_out, hid32)
 
 
+SETS = ((1, 2), (3, 4), (0, 3))
+
+
+def split_kernel(w, before, out):
+    half = w.shape[3] // 4
+    at = first_channel(2 * half, True)
+    even = lax.axis_index("chan") % 2 == 0
+    left = lanes(w.shape[2]) < half
+    for k, (one, two) in enumerate(SETS):
+        for b in range(5):
+            x, y = w[one, b, :, pl.ds(at, 2 * half)], w[two, b, :, pl.ds(at, 2 * half)]
+            low, high = jnp.where(left, x, roll(y, half)), jnp.where(left, roll(x, half), y)
+            out[0, 5 * k + b] = jnp.where(even, low, high)
+            out[1, 5 * k + b] = jnp.where(even, high, low)
+
+
+def shard_rows(weights, which, xs, pair):
+    left, right = [], []
+    for k in (0, pair + 1):
+        for b in range(5):
+            left.append(weights[which, 5 * k + b])
+            for a in SETS[k]:
+                lo = 2 * pair + a - 2
+                right.append(xs[b, :, 128 * (lo + 1) : 128 * (lo + 3)])
+    return jnp.dot(jnp.concatenate(left, axis=1), jnp.concatenate(right, axis=0), preferred_element_type=F32)
+
+
+def shard_kernel(step, which, shard, part, weights, *refs):
+    *ends, xs = refs if which == 0 else (*refs[:-3], refs[-3])
+    ch = shard.shape[0] // 4 - FOLD // 4
+    store_windows(xs, *rows_of([shard[...]], ch))
+    pre = ends[0] if which == 0 else refs[-2]
+    for pair in range(2):
+        total = shard_rows(weights, which, xs, pair)
+        pre[2 * pair] = part[2 * pair] + total[:, 0:128]
+        pre[2 * pair + 1] = part[2 * pair + 1] + total[:, 128:256]
+    if which == 1:
+        finish(step, pre, *ends, refs[-1])
+
+
+def rim_strips(shards, ch):
+    halo = jnp.concatenate([unfold(s[0:FOLD].astype(F32), ch) for s in shards], axis=0).astype(BF16)
+    own = jnp.concatenate([unfold(s[FOLD:].astype(F32), ch) for s in shards], axis=0).astype(BF16)
+    return strips(halo, own)
+
+
+def ordered(own, other):
+    even = lax.axis_index("chan") % 2 == 0
+    return [jnp.where(even, own[...], other[...]), jnp.where(even, other[...], own[...])]
+
+
+def rim_drive_kernel(from_right, from_left, inp, weights, *refs):
+    part, xi, inp32 = refs[-3:]
+    store_input_rim(xi, *input_rows(0, inp32, inp, from_right, from_left))
+    part[...] = input_part(weights, xi, 0, 128)
+
+
 def rim_kernel(*refs):
-    *blocks, hid, cell, to_right, to_left, from_right, from_left, inp, w, wx, bias = refs[:-6]
-    hid_out, cell_out, xi, wxb, pre, inp32 = refs[-6:]
+    *blocks, part, hid, cell, to_right, to_left, from_right, from_left, w, hid_out, cell_out, pre = refs
     ch = cell.shape[0] // 4
     if len(blocks) == 4:
-        even, first = lax.axis_index("chan") % 2 == 0, lax.axis_index("chan") // 2 == 0
-        own, other, same, cross = [b[...] for b in blocks]
-        here = (jnp.where(even, own, other), jnp.where(even, other, own))
-        there = (jnp.where(even, same, cross), jnp.where(even, cross, same))
+        first = lax.axis_index("chan") // 2 == 0
+        here, there = ordered(*blocks[:2]), ordered(*blocks[2:])
         shards = [jnp.where(first, here[k], there[k]) for k in (0, 1)]
         shards += [jnp.where(first, there[k], here[k]) for k in (0, 1)]
     else:
         shards = [blocks[0][c] for c in range(blocks[0].shape[0])]
-    halo = jnp.concatenate([unfold(s[0:FOLD].astype(F32), ch) for s in shards], axis=0).astype(BF16)
-    own = jnp.concatenate([unfold(s[FOLD:].astype(F32), ch) for s in shards], axis=0).astype(BF16)
-    store_input_rim(xi, *input_rows(0, inp32, inp, from_right, from_left))
-    store_input_weights(wxb, wx, bias)
-    pre[0] = hidden_rim(w, strips(halo, own)) + input_part(wxb, xi, 0, 128)
+    pre[0] = part[...] + hidden_rim(w, rim_strips(shards, ch), 0)
     h, c = rim_gates(pre, to_right, to_left, from_right, from_left, ch)
     for y in range(4):
         at = slice(y * ch, (y + 1) * ch)
@@ -333,7 +410,7 @@
     hid_out[4 * ch : 4 * ch + FOLD, :] = rim_fold(h)
 
 
-def call(kernel, outs, scratch, *args, far=0, us=1):
+def call(kernel, outs, scratch, *args, far=0, us=1, same=None):
     return pl.pallas_call(
         kernel,
         out_shape=[jax.ShapeDtypeStruct(s, d) for s, d in outs],
@@ -341,6 +418,7 @@
         + [pl.BlockSpec(memory_space=pltpu.VMEM)] * (len(args) - far),
         out_specs=[pl.BlockSpec(memory_space=pltpu.VMEM)] * len(outs),
         scratch_shapes=[pltpu.VMEM(s, d) for s, d in scratch] + ([pltpu.SemaphoreType.DMA((far,))] if far else []),
+        input_output_aliases=same or {},
         cost_estimate=pl.CostEstimate(flops=int(us * 1e9), bytes_accessed=0, transcendentals=0),
         compiler_params=pltpu.CompilerParams(vmem_limit_bytes=24 << 20),
     )(*[pltpu.with_memory_space_constraint(a, pltpu.HBM) if i < far else a for i, a in enumerate(args)])
@@ -356,12 +434,17 @@
     inp = inputs.reshape(-1, cols)
     wx = jnp.transpose(w_input, (0, 1, 3, 2)).reshape(25 * cin, gate)
     bias = gate_bias.reshape(1, gate)
-    to_right, to_left, hid = call(
+    driven = [((gate, padded(25 * cin)), BF16), ((4, gate, 128), F32)]
+    stack = ((padded(25 * cin), 512), BF16)
+    inp32 = (inp.shape, F32)
+    to_right, to_left, hid, weights, part = call(
         pack_kernel,
-        [((FOLD + 8, 128), F32), ((FOLD + 8, 128), F32), ((4 * ch, 128), F32)],
-        [(hid.shape, BF16), (cell.shape, F32), (inp.shape, BF16), (hid.shape, F32), (inp.shape, F32)],
-        hid, cell, inp, far=3, us=1,
+        [((FOLD + 8, 128), F32), ((FOLD + 8, 128), F32), ((4 * ch, 128), F32), *driven],
+        [(hid.shape, BF16), (cell.shape, F32), (inp.shape, BF16), (wx.shape, BF16), (bias.shape, F32),
+         (hid.shape, F32), inp32, stack],
+        hid, cell, inp, wx, bias, far=5, us=20,
     )
+    weights, driven = call(drive_kernel, driven, [inp32, stack], inp, wx, bias, weights, part, us=0.01, same={3: 0, 4: 1})
     (main,) = call(main_kernel, [((4 * ch, 128), BF16)], [], hid, us=0.01)
     n = lax.axis_size("lon")
     came_left = lax.ppermute(to_right, "lon", [(i, (i + 1) % n) for i in range(n)])
@@ -383,43 +466,59 @@
     field = main
     traveling = [lax.ppermute(field, "chan", [(i, i ^ k) for i in range(shards)]) for k in (1, 2, 3)] if paired else None
     blocks = [strip, *[lax.ppermute(strip, "chan", [(i, i ^ k) for i in range(shards)]) for k in (1, 2, 3)]] if paired else [lax.all_gather(strip, "chan", axis=0)]
-    kinds = [((25 * cin + 16, gate), BF16)]
     for step in range(STEPS):
         last = step == STEPS - 1
-        stack = [((25 * cin + 16, 512), BF16), *kinds]
-        inp32 = (inp.shape, F32)
         hid32 = ((4 * ch, 128), F32)
         pre = ((4, gate, 128), F32)
         outs = [((4 * ch, 128), BF16), ((4 * ch, 128), F32)]
+        rim = None
         if paired:
             other, same, *cross = traveling
             windowed = ((5, 2 * ch, 768), BF16)
-            (part,) = call(
-                functools.partial(near_kernel, step), [pre], [windowed, *stack, inp32],
-                field, other, from_right, from_left, inp, w_hidden, wx, bias, us=0.01,
-            )
+            (part,) = call(near_kernel, [pre], [windowed], field, other, driven, w_hidden, us=0.01)
             if cross:
                 (cross,) = cross
             else:
-                same, cross = onward(same, part)
+                (split,) = call(
+                    split_kernel, [((2, 5 * len(SETS), gate, 128), BF16)], [], w_hidden, part, us=0.01
+                )
+                same, cross = onward(same, split)
+        if not last:
+            rim = call(
+                rim_drive_kernel, [((gate, 128), F32)], [((padded(25 * cin), 128), BF16), inp32],
+                from_right, from_left, inp, weights, *([part] if paired else []), us=0.01,
+            )
+        if paired and last:
+            (part,) = call(
+                functools.partial(shard_kernel, step, 0), [pre], [((5, ch, 768), BF16)],
+                same, part, split, us=0.01,
+            )
+            field, cell = call(
+                functools.partial(shard_kernel, step, 1), outs, [((5, ch, 768), BF16), pre, hid32],
+                cross, part, split, cell, us=0.01,
+            )
+        elif paired:
             field, cell = call(
                 functools.partial(far_kernel, step), outs, [windowed, pre, hid32],
-                same, cross, part, cell, w_hidden, us=0.01,
+                same, cross, part, cell, w_hidden, *(rim or []), us=0.01,
             )
         else:
             gathered = lax.all_gather(field, "chan", axis=0)
             field, cell = call(
                 functools.partial(whole_kernel, step), outs,
-                [((5, depth, 768), BF16), *stack, pre, inp32, hid32],
-                gathered, from_right, from_left, inp, cell, w_hidden, wx, bias, us=3,
+                [((5, depth, 768), BF16), pre, hid32], gathered, driven, cell, w_hidden, us=3,
             )
         if not last:
             field, cell = call(
-                rim_kernel, [((4 * ch + FOLD, 128), BF16), ((4 * ch, 128), F32)],
-                [((25 * cin + 16, 128), BF16), *kinds, ((1, gate, 128), F32), inp32],
-                *blocks, field, cell, to_right, to_left, from_right, from_left, inp, w_hidden, wx, bias, us=0.01,
+                rim_kernel, [((4 * ch + FOLD, 128), BF16), ((4 * ch, 128), F32)], [((1, gate, 128), F32)],
+                *blocks, *rim, field, cell,
+                to_right, to_left, from_right, from_left, w_hidden, us=0.01,
             )
             traveling = others(field) if paired else None
+            (driven,) = call(
+                functools.partial(next_drive_kernel, step + 1), [pre], [stack, inp32],
+                from_right, from_left, inp, weights, field, us=0.01,
+            )
     return field.reshape(ch, rows, cols), cell.reshape(ch, rows, cols)
 
 

time: 23.9 us -> 23.6 us (0.987)
  waiting for transfers between devices: 3.35 us -> 1.54 us
  Pallas kernels: 8.53 us -> 10.3 us
  starting transfers between devices: 11.1 us -> 10.7 us
    pallas_call x9 -> x14, Pallas kernels: 8.53 us -> 10.3 us  [call(): pl.pallas_call(kernel, out_shape=[jax.ShapeDtypeStruct(s, d) for s, d in...]
    ppermute x1, waiting for transfers between devices: 1.25 us -> 0.51 us  [onward(): lax.ppermute(same, 'chan', [(i, i ^ 1) for i in range(shards)])]
    ppermute x2, waiting for transfers between devices: 1.46 us -> 0.75 us  [others(): lax.ppermute(x, 'chan', [(i, i ^ k) for i in range(shards)])]
    ppermute x3, waiting for transfers between devices: 0.63 us -> 0.01 us  [shards(): lax.ppermute(field, 'chan', [(i, i ^ k) for i in range(shards)])]
    ppermute x1, starting transfers between devices: 3.08 us -> 2.68 us  [shards(): lax.ppermute(to_right, 'lon', [(i, (i + 1) % n) for i in range(n)])]
    ppermute x3, waiting for transfers between devices: 0.01 us -> 0.26 us  [shards(): lax.ppermute(strip, 'chan', [(i, i ^ k) for i in range(shards)])]
  transfers between devices with their start and end apart: 11 -> 11, of which waited for: 3 -> 3; matrix products, arithmetic and copies ran while one was open for 0% -> 0% of each run, Pallas kernels for 16% -> 24%
where the time goes in v5:
time: 23.6 us; the launch traced here: 23.4 us
  starting transfers between devices  10.7 us (45%)
  Pallas kernels  10.3 us (44%)
  waiting for transfers between devices  1.54 us (7%)
  between operations  0.82 us (3%)
    pallas_call x14, Pallas kernels, call(): pl.pallas_call(kernel, out_shape=[jax.ShapeDtypeStruct(s, d) for s, d in...  10.3 us
    ppermute x1, starting transfers between devices, shards(): lax.ppermute(to_right, 'lon', [(i, (i + 1) % n) for i in range(n)])  2.68 us
    ppermute x3, starting transfers between devices, shards(): lax.ppermute(field, 'chan', [(i, i ^ k) for i in range(shards)])  2.23 us
    ppermute x3, starting transfers between devices, shards(): lax.ppermute(strip, 'chan', [(i, i ^ k) for i in range(shards)])  2.17 us
    ppermute x1, starting transfers between devices, shards(): lax.ppermute(to_left, 'lon', [((i + 1) % n, i) for i in range(n)])  2.09 us
    ppermute x2, starting transfers between devices, others(): lax.ppermute(x, 'chan', [(i, i ^ k) for i in range(shards)])  1.57 us
    ppermute x2, waiting for transfers between devices, others(): lax.ppermute(x, 'chan', [(i, i ^ k) for i in range(shards)])  0.75 us
    ppermute x1, waiting for transfers between devices, onward(): lax.ppermute(same, 'chan', [(i, i ^ 1) for i in range(shards)])  0.51 us
  transfers between devices with their start and end apart: 11, of which 3 were waited for; matrix products, arithmetic and copies ran while one was open for 0% of the time, Pallas kernels for 24%

profile of v5, /device:TPU:0, one launch (start us, length us, event | category | flops | bytes accessed | tf_op | source)
XLA Modules:
  0.0 23.4 jit_solution(10867891341143008260)
XLA Ops:
  0.6 1.7 %shard_map.77 = (f32[24,128]{1,0:T(8,128)S(1)}, f32[24,128]{1,0:T(8,128)S(1)}, f32[256,128]{1,0:T(8,128)S(1)}, bf16[256,512]{1,0:T(8,128)(2,1)S(1)}, f32[4,256,128]{2,1,0:T(8,128)S(1)}) custom-call(bf16[256,128]{1,0:T(8,128)(2,1)} %bitcast.20, f32[256,128]{1,0:T(8,128)} %bitcast.15, bf16[128,128]{1,0:T(8,128)(2,1)} %bitcast.9, bf16[400,256]{1,0:T(8,128)(2,1)} %bitcast.13, ...), custom_call_target="tpu_custom_call" | custom-call | flops 20000000000 | tf_op jit(solution)/shard_map/pallas_call | solution.py:414
  2.3 0.0 copy-start.1
  2.3 0.0 copy-start.2
  2.3 0.0 copy-start.4
  2.4 0.0 copy-start
  2.4 2.7 %collective-permute-start = (f32[24,128]{1,0:T(8,128)S(1)}, f32[24,128]{1,0:T(8,128)S(1)}, u32[]{:S(2)}, u32[]{:S(2)}) collective-permute-start(f32[24,128]{1,0:T(8,128)S(1)} %get-tuple-element.18.to_right.refs_7_), channel_id=1, source_target_pairs={{0,4},{4,8},{8,12},{12,0},{1,5},{5,9},{9,13},{13,1},{2,6},{6,10},{... | collective-permute-start | bytes 36872 | tf_op jit(solution)/shard_map/ppermute | solution.py:450
  5.1 2.1 %collective-permute-start.1 = (f32[24,128]{1,0:T(8,128)S(1)}, f32[24,128]{1,0:T(8,128)S(1)}, u32[]{:S(2)}, u32[]{:S(2)}) collective-permute-start(f32[24,128]{1,0:T(8,128)S(1)} %get-tuple-element.19.to_left.refs_8_), channel_id=1, source_target_pairs={{4,0},{8,4},{12,8},{0,12},{5,1},{9,5},{13,9},{1,13},{6,2},{10,6},{... | collective-permute-start | bytes 36872 | tf_op jit(solution)/shard_map/ppermute | solution.py:451
  7.2 1.0 %collective-permute-start.7 = (bf16[256,128]{1,0:T(8,128)(2,1)S(1)}, bf16[256,128]{1,0:T(8,128)(2,1)S(1)}, u32[]{:S(2)}, u32[]{:S(2)}) collective-permute-start(bf16[256,128]{1,0:T(8,128)(2,1)S(1)} %shard_map.80.own), channel_id=1, source_target_pairs={{0,3},{1,2},{2,1},{3,0},{4,7},{5,6},{6,5},{7,4},{8,11},{9,10},{10,... | collective-permute-start | bytes 196616 | tf_op jit(solution)/shard_map/ppermute | solution.py:467
  8.1 1.2 %collective-permute-start.6 = (bf16[256,128]{1,0:T(8,128)(2,1)S(1)}, bf16[256,128]{1,0:T(8,128)(2,1)S(1)}, u32[]{:S(2)}, u32[]{:S(2)}) collective-permute-start(bf16[256,128]{1,0:T(8,128)(2,1)S(1)} %shard_map.80.own), channel_id=1, source_target_pairs={{0,2},{1,3},{2,0},{3,1},{4,6},{5,7},{6,4},{7,5},{8,10},{9,11},{10,... | collective-permute-start | bytes 196616 | tf_op jit(solution)/shard_map/ppermute | solution.py:467
  9.3 0.0 collective-permute-start.5
  9.4 0.0 collective-permute-done.came_left
  9.4 0.0 collective-permute-done.1.came_right
  9.4 0.0 copy-start.3
  9.4 1.4 %collective-permute-start.4 = (bf16[32,128]{1,0:T(8,128)(2,1)S(1)}, bf16[32,128]{1,0:T(8,128)(2,1)S(1)}, u32[]{:S(2)}, u32[]{:S(2)}) collective-permute-start(bf16[32,128]{1,0:T(8,128)(2,1)S(1)} %get-tuple-element.20.refs_0_), channel_id=1, source_target_pairs={{0,3},{1,2},{2,1},{3,0},{4,7},{5,6},{6,5},{7,4},{8,11},{9,10},{10,... | collective-permute-start | bytes 24584 | tf_op jit(solution)/shard_map/ppermute | solution.py:468
  10.8 0.7 %collective-permute-start.3 = (bf16[32,128]{1,0:T(8,128)(2,1)S(1)}, bf16[32,128]{1,0:T(8,128)(2,1)S(1)}, u32[]{:S(2)}, u32[]{:S(2)}) collective-permute-start(bf16[32,128]{1,0:T(8,128)(2,1)S(1)} %get-tuple-element.20.refs_0_), channel_id=1, source_target_pairs={{0,2},{1,3},{2,0},{3,1},{4,6},{5,7},{6,4},{7,5},{8,10},{9,11},{10,... | collective-permute-start | bytes 24584 | tf_op jit(solution)/shard_map/ppermute | solution.py:468
  11.6 0.0 collective-permute-start.2
  11.6 1.0 %shard_map.81.refs_0_.part = f32[4,256,128]{2,1,0:T(8,128)S(1)} custom-call(bf16[256,128]{1,0:T(8,128)(2,1)S(1)} %shard_map.80.own, bf16[256,128]{1,0:T(8,128)(2,1)S(1)} %collective-permute-done.5.other, f32[4,256,128]{2,1,0:T(8,128)S(1)} %get-tuple-element.27.driven, bf16[5,5,256,256]{3,2,1,0:T(8,128)(2,1)S(1)} %copy-done), custom_call_target="tpu_custom_call" | custom-call | flops 10000000 | tf_op jit(solution)/shard_map/pallas_call | solution.py:414
  12.6 0.5 %shard_map.82.refs_0_.refs_4_ = f32[256,128]{1,0:T(8,128)S(1)} custom-call(f32[24,128]{1,0:T(8,128)S(1)} %get-tuple-element.21.from_right.refs_9_, f32[24,128]{1,0:T(8,128)S(1)} %get-tuple-element.22.from_left.refs_10_, bf16[128,128]{1,0:T(8,128)(2,1)S(1)} %bitcast.11, bf16[256,512]{1,0:T(8,128)(2,1)S(1)} %get-tuple-element.25.weights, ...), custom_call_target="tpu_custom_call" | custom-call | flops 10000000 | tf_op jit(solution)/shard_map/pallas_call | solution.py:414
  13.1 0.0 collective-permute-done.7.cross
  13.1 1.1 %shard_map.83 = (bf16[256,128]{1,0:T(8,128)(2,1)S(1)}, f32[256,128]{1,0:T(8,128)S(1)}) custom-call(bf16[256,128]{1,0:T(8,128)(2,1)S(1)} %collective-permute-done.6.same, bf16[256,128]{1,0:T(8,128)(2,1)S(1)} %collective-permute-done.7.cross, f32[4,256,128]{2,1,0:T(8,128)S(1)} %shard_map.81.refs_0_.part, f32[256,128]{1,0:T(8,128)S(1)} %bitcast.16, ...), custom_call_target="tpu_custom_call" | custom-call | flops 10000000 | tf_op jit(solution)/shard_map/pallas_call | solution.py:414
  14.2 0.3 %collective-permute-done.3.refs_2_ = bf16[32,128]{1,0:T(8,128)(2,1)S(1)} collective-permute-done((bf16[32,128]{1,0:T(8,128)(2,1)S(1)}, bf16[32,128]{1,0:T(8,128)(2,1)S(1)}, u32[]{:S(2)}, u32[]{:S(2)}) %collective-permute-start.3) | collective-permute-done | bytes 8224 | tf_op jit(solution)/shard_map/ppermute | solution.py:468
  14.5 1.5 %shard_map.84 = (bf16[272,128]{1,0:T(8,128)(2,1)S(1)}, f32[256,128]{1,0:T(8,128)S(1)}) custom-call(bf16[32,128]{1,0:T(8,128)(2,1)S(1)} %get-tuple-element.20.refs_0_, bf16[32,128]{1,0:T(8,128)(2,1)S(1)} %collective-permute-done.2.refs_1_, bf16[32,128]{1,0:T(8,128)(2,1)S(1)} %collective-permute-done.3.refs_2_, ...), custom_call_target="tpu_custom_call" | custom-call | flops 10000000 | tf_op jit(solution)/shard_map/pallas_call | solution.py:414
  16.0 0.3 %collective-permute-start.9 = (bf16[272,128]{1,0:T(8,128)(2,1)S(1)}, bf16[272,128]{1,0:T(8,128)(2,1)S(1)}, u32[]{:S(2)}, u32[]{:S(2)}) collective-permute-start(bf16[272,128]{1,0:T(8,128)(2,1)S(1)} %get-tuple-element.30.before.own), channel_id=1, source_target_pairs={{0,1},{1,0},{2,3},{3,2},{4,5},{5,4},{6,7},{7,6},{8,9},{9,8},{10,11... | collective-permute-start | bytes 208904 | tf_op jit(solution)/shard_map/ppermute | solution.py:460
  16.3 1.3 %collective-permute-start.8 = (bf16[272,128]{1,0:T(8,128)(2,1)S(1)}, bf16[272,128]{1,0:T(8,128)(2,1)S(1)}, u32[]{:S(2)}, u32[]{:S(2)}) collective-permute-start(bf16[272,128]{1,0:T(8,128)(2,1)S(1)} %get-tuple-element.30.before.own), channel_id=1, source_target_pairs={{0,2},{1,3},{2,0},{3,1},{4,6},{5,7},{6,4},{7,5},{8,10},{9,11},{10,... | collective-permute-start | bytes 208904 | tf_op jit(solution)/shard_map/ppermute | solution.py:460
  17.6 0.5 %shard_map.85.driven = f32[4,256,128]{2,1,0:T(8,128)S(1)} custom-call(f32[24,128]{1,0:T(8,128)S(1)} %get-tuple-element.21.from_right.refs_9_, f32[24,128]{1,0:T(8,128)S(1)} %get-tuple-element.22.from_left.refs_10_, bf16[128,128]{1,0:T(8,128)(2,1)S(1)} %bitcast.12, bf16[256,512]{1,0:T(8,128)(2,1)S(1)} %get-tuple-element.25.weights, ...), custom_call_target="tpu_custom_call" | custom-call | flops 10000000 | tf_op jit(solution)/shard_map/pallas_call | solution.py:414
  18.1 0.0 collective-permute-done.9.other
  18.1 1.1 %shard_map.86.before.part = f32[4,256,128]{2,1,0:T(8,128)S(1)} custom-call(bf16[272,128]{1,0:T(8,128)(2,1)S(1)} %get-tuple-element.30.before.own, bf16[272,128]{1,0:T(8,128)(2,1)S(1)} %collective-permute-done.9.other, f32[4,256,128]{2,1,0:T(8,128)S(1)} %shard_map.85.driven, bf16[5,5,256,256]{3,2,1,0:T(8,128)(2,1)S(1)} %copy-done), custom_call_target="tpu_custom_call" | custom-call | flops 10000000 | tf_op jit(solution)/shard_map/pallas_call | solution.py:414
  19.2 0.7 %shard_map.87.before.weights = bf16[2,15,256,128]{3,2,1,0:T(8,128)(2,1)S(1)} custom-call(bf16[5,5,256,256]{3,2,1,0:T(8,128)(2,1)S(1)} %copy-done, f32[4,256,128]{2,1,0:T(8,128)S(1)} %shard_map.86.before.part), custom_call_target="tpu_custom_call" | custom-call | flops 10000000 | tf_op jit(solution)/shard_map/pallas_call | solution.py:414
  19.9 0.7 %collective-permute-done.8.x = bf16[272,128]{1,0:T(8,128)(2,1)S(1)} collective-permute-done((bf16[272,128]{1,0:T(8,128)(2,1)S(1)}, bf16[272,128]{1,0:T(8,128)(2,1)S(1)}, u32[]{:S(2)}, u32[]{:S(2)}) %collective-permute-start.8) | collective-permute-done | bytes 69664 | tf_op jit(solution)/shard_map/ppermute | solution.py:460
  20.7 0.7 %shard_map.89.part = f32[4,256,128]{2,1,0:T(8,128)S(1)} custom-call(bf16[272,128]{1,0:T(8,128)(2,1)S(1)} %shard_map.88.shard, f32[4,256,128]{2,1,0:T(8,128)S(1)} %shard_map.86.before.part, bf16[2,15,256,128]{3,2,1,0:T(8,128)(2,1)S(1)} %shard_map.87.before.weights), custom_call_target="tpu_custom_call" | custom-call | flops 10000000 | tf_op jit(solution)/shard_map/pallas_call | solution.py:414
  21.4 0.5 %collective-permute-done.10.shard = bf16[272,128]{1,0:T(8,128)(2,1)S(1)} collective-permute-done((bf16[272,128]{1,0:T(8,128)(2,1)S(1)}, bf16[272,128]{1,0:T(8,128)(2,1)S(1)}, u32[]{:S(2)}, u32[]{:S(2)}) %collective-permute-start.10) | collective-permute-done | bytes 69664 | tf_op jit(solution)/shard_map/ppermute | solution.py:464
  21.9 1.5 %shard_map.90 = (bf16[256,128]{1,0:T(8,128)(2,1)}, f32[256,128]{1,0:T(8,128)}) custom-call(bf16[272,128]{1,0:T(8,128)(2,1)S(1)} %collective-permute-done.10.shard, f32[4,256,128]{2,1,0:T(8,128)S(1)} %shard_map.89.part, bf16[2,15,256,128]{3,2,1,0:T(8,128)(2,1)S(1)} %shard_map.87.before.weights, f32[256,128]{1,0:T(8,128)S(1)} %get-tuple-element.31.refs_0_), custom_call_target="tpu_custom_call" | custom-call | flops 10000000 | tf_op jit(solution)/shard_map/pallas_call | solution.py:414
  (14 shorter events, 0.1 us)
Async XLA Ops:
  2.3 9.3 %copy-start.1 = (bf16[2,16,4,128]{3,2,1,0:T(4,128)(2,1)S(1)}, bf16[2,16,4,128]{3,2,1,0:T(4,128)(2,1)}, u32[]{:S(2)}) copy-start(bf16[2,16,4,128]{3,2,1,0:T(4,128)(2,1)} %param.6) | copy-start | bytes 98308
  2.3 9.3 %copy-start.2 = (bf16[5,5,256,16]{2,3,1,0:T(8,128)(2,1)S(1)}, bf16[5,5,256,16]{2,3,1,0:T(8,128)(2,1)}, u32[]{:S(2)}) copy-start(bf16[5,5,256,16]{2,3,1,0:T(8,128)(2,1)} %param.9) | copy-start | bytes 614404
  2.3 9.3 %copy-start.4 = (f32[256]{0:T(256)S(1)}, f32[256]{0:T(256)}, u32[]{:S(2)}) copy-start(f32[256]{0:T(256)} %param.11) | copy-start | bytes 3076
  2.4 9.3 %copy-start = (bf16[5,5,256,256]{3,2,1,0:T(8,128)(2,1)S(1)}, bf16[5,5,256,256]{3,2,1,0:T(8,128)(2,1)}, u32[]{:S(2)}) copy-start(bf16[5,5,256,256]{3,2,1,0:T(8,128)(2,1)} %w.7) | copy-start | bytes 9830404
  2.4 7.0 %collective-permute-start = (f32[24,128]{1,0:T(8,128)S(1)}, f32[24,128]{1,0:T(8,128)S(1)}, u32[]{:S(2)}, u32[]{:S(2)}) collective-permute-start(f32[24,128]{1,0:T(8,128)S(1)} %get-tuple-element.18.to_right.refs_7_), channel_id=1, source_target_pairs={{0,4},{4,8},{8,12},{12,0},{1,5},{5,9},{9,13},{13,1},{2,6},{6,10},{... | collective-permute-start | bytes 36872 | tf_op jit(solution)/shard_map/ppermute | solution.py:450
  5.1 4.3 %collective-permute-start.1 = (f32[24,128]{1,0:T(8,128)S(1)}, f32[24,128]{1,0:T(8,128)S(1)}, u32[]{:S(2)}, u32[]{:S(2)}) collective-permute-start(f32[24,128]{1,0:T(8,128)S(1)} %get-tuple-element.19.to_left.refs_8_), channel_id=1, source_target_pairs={{4,0},{8,4},{12,8},{0,12},{5,1},{9,5},{13,9},{1,13},{6,2},{10,6},{... | collective-permute-start | bytes 36872 | tf_op jit(solution)/shard_map/ppermute | solution.py:451
  7.2 6.0 %collective-permute-start.7 = (bf16[256,128]{1,0:T(8,128)(2,1)S(1)}, bf16[256,128]{1,0:T(8,128)(2,1)S(1)}, u32[]{:S(2)}, u32[]{:S(2)}) collective-permute-start(bf16[256,128]{1,0:T(8,128)(2,1)S(1)} %shard_map.80.own), channel_id=1, source_target_pairs={{0,3},{1,2},{2,1},{3,0},{4,7},{5,6},{6,5},{7,4},{8,11},{9,10},{10,... | collective-permute-start | bytes 196616 | tf_op jit(solution)/shard_map/ppermute | solution.py:467
  8.1 5.0 %collective-permute-start.6 = (bf16[256,128]{1,0:T(8,128)(2,1)S(1)}, bf16[256,128]{1,0:T(8,128)(2,1)S(1)}, u32[]{:S(2)}, u32[]{:S(2)}) collective-permute-start(bf16[256,128]{1,0:T(8,128)(2,1)S(1)} %shard_map.80.own), channel_id=1, source_target_pairs={{0,2},{1,3},{2,0},{3,1},{4,6},{5,7},{6,4},{7,5},{8,10},{9,11},{10,... | collective-permute-start | bytes 196616 | tf_op jit(solution)/shard_map/ppermute | solution.py:467
  9.3 2.2 %collective-permute-start.5 = (bf16[256,128]{1,0:T(8,128)(2,1)S(1)}, bf16[256,128]{1,0:T(8,128)(2,1)S(1)}, u32[]{:S(2)}, u32[]{:S(2)}) collective-permute-start(bf16[256,128]{1,0:T(8,128)(2,1)S(1)} %shard_map.80.own), channel_id=1, source_target_pairs={{0,1},{1,0},{2,3},{3,2},{4,5},{5,4},{6,7},{7,6},{8,9},{9,8},{10,11... | collective-permute-start | bytes 196616 | tf_op jit(solution)/shard_map/ppermute | solution.py:467
  9.4 3.7 %copy-start.3 = (f32[64,4,128]{2,1,0:T(4,128)S(1)}, f32[64,4,128]{2,1,0:T(4,128)}, u32[]{:S(2)}) copy-start(f32[64,4,128]{2,1,0:T(4,128)} %param.8) | copy-start | bytes 393220
  9.4 4.8 %collective-permute-start.4 = (bf16[32,128]{1,0:T(8,128)(2,1)S(1)}, bf16[32,128]{1,0:T(8,128)(2,1)S(1)}, u32[]{:S(2)}, u32[]{:S(2)}) collective-permute-start(bf16[32,128]{1,0:T(8,128)(2,1)S(1)} %get-tuple-element.20.refs_0_), channel_id=1, source_target_pairs={{0,3},{1,2},{2,1},{3,0},{4,7},{5,6},{6,5},{7,4},{8,11},{9,10},{10,... | collective-permute-start | bytes 24584 | tf_op jit(solution)/shard_map/ppermute | solution.py:468
  10.8 3.7 %collective-permute-start.3 = (bf16[32,128]{1,0:T(8,128)(2,1)S(1)}, bf16[32,128]{1,0:T(8,128)(2,1)S(1)}, u32[]{:S(2)}, u32[]{:S(2)}) collective-permute-start(bf16[32,128]{1,0:T(8,128)(2,1)S(1)} %get-tuple-element.20.refs_0_), channel_id=1, source_target_pairs={{0,2},{1,3},{2,0},{3,1},{4,6},{5,7},{6,4},{7,5},{8,10},{9,11},{10,... | collective-permute-start | bytes 24584 | tf_op jit(solution)/shard_map/ppermute | solution.py:468
  11.6 2.9 %collective-permute-start.2 = (bf16[32,128]{1,0:T(8,128)(2,1)S(1)}, bf16[32,128]{1,0:T(8,128)(2,1)S(1)}, u32[]{:S(2)}, u32[]{:S(2)}) collective-permute-start(bf16[32,128]{1,0:T(8,128)(2,1)S(1)} %get-tuple-element.20.refs_0_), channel_id=1, source_target_pairs={{0,1},{1,0},{2,3},{3,2},{4,5},{5,4},{6,7},{7,6},{8,9},{9,8},{10,11... | collective-permute-start | bytes 24584 | tf_op jit(solution)/shard_map/ppermute | solution.py:468
  16.0 2.1 %collective-permute-start.9 = (bf16[272,128]{1,0:T(8,128)(2,1)S(1)}, bf16[272,128]{1,0:T(8,128)(2,1)S(1)}, u32[]{:S(2)}, u32[]{:S(2)}) collective-permute-start(bf16[272,128]{1,0:T(8,128)(2,1)S(1)} %get-tuple-element.30.before.own), channel_id=1, source_target_pairs={{0,1},{1,0},{2,3},{3,2},{4,5},{5,4},{6,7},{7,6},{8,9},{9,8},{10,11... | collective-permute-start | bytes 208904 | tf_op jit(solution)/shard_map/ppermute | solution.py:460
  16.3 4.3 %collective-permute-start.8 = (bf16[272,128]{1,0:T(8,128)(2,1)S(1)}, bf16[272,128]{1,0:T(8,128)(2,1)S(1)}, u32[]{:S(2)}, u32[]{:S(2)}) collective-permute-start(bf16[272,128]{1,0:T(8,128)(2,1)S(1)} %get-tuple-element.30.before.own), channel_id=1, source_target_pairs={{0,2},{1,3},{2,0},{3,1},{4,6},{5,7},{6,4},{7,5},{8,10},{9,11},{10,... | collective-permute-start | bytes 208904 | tf_op jit(solution)/shard_map/ppermute | solution.py:460
  20.7 1.3 %collective-permute-start.10 = (bf16[272,128]{1,0:T(8,128)(2,1)S(1)}, bf16[272,128]{1,0:T(8,128)(2,1)S(1)}, u32[]{:S(2)}, u32[]{:S(2)}) collective-permute-start(bf16[272,128]{1,0:T(8,128)(2,1)S(1)} %shard_map.88.shard), channel_id=1, source_target_pairs={{0,1},{1,0},{2,3},{3,2},{4,5},{5,4},{6,7},{7,6},{8,9},{9,8},{10,11... | collective-permute-start | bytes 208904 | tf_op jit(solution)/shard_map/ppermute | solution.py:464

commit v6 on v5

--- a/solution.py
+++ b/solution.py
@@ -58,18 +58,21 @@
     copies = [pltpu.make_async_copy(a, b, arrived.at[i]) for i, (a, b) in enumerate(pairs)]
     for copy in copies:
         copy.start()
-    for copy in copies:
+    copies[0].wait()
+    hid32[...] = hid[...].astype(F32)
+    hl, hr = edges_of(lambda i, y: hid32[pl.ds(32 * i + y, 8, stride=4), :], ch // 8, 2)
+    hid_out[...] = hid32[...]
+    copies[1].wait()
+    cl, cr = edges_of(lambda i, y: cell[pl.ds(32 * i + y, 8, stride=4), :], ch // 8, 2)
+    to_left[0:FOLD] = hl + roll(cl, -4)
+    to_right[0:FOLD] = hr + roll(cr, 4)
+    copies[2].wait()
+    inp32[...] = inp[...].astype(F32)
+    il, ir = edges_of(lambda i, y: inp32[pl.ds(32 * i + y, 8, stride=4), :], inp.shape[0] // 32, 1)
+    to_left[FOLD:] = il
+    to_right[FOLD:] = ir
+    for copy in copies[3:]:
         copy.wait()
-    hid32[...] = hid[...].astype(F32)
-    inp32[...] = inp[...].astype(F32)
-    hl, hr = edges_of(lambda i, y: hid32[pl.ds(32 * i + y, 8, stride=4), :], ch // 8, 2)
-    cl, cr = edges_of(lambda i, y: cell[pl.ds(32 * i + y, 8, stride=4), :], ch // 8, 2)
-    il, ir = edges_of(lambda i, y: inp32[pl.ds(32 * i + y, 8, stride=4), :], inp.shape[0] // 32, 1)
-    to_left[0:FOLD] = hl + roll(cl, -4)
-    to_left[FOLD:] = il
-    to_right[0:FOLD] = hr + roll(cr, 4)
-    to_right[FOLD:] = ir
-    hid_out[...] = hid32[...]
 
     @pl.when(lax.axis_index("lon") == 0)
     def _():
@@ -362,16 +365,32 @@
 
 
 def shard_kernel(step, which, shard, part, weights, *refs):
-    *ends, xs = refs if which == 0 else (*refs[:-3], refs[-3])
+    if which == 0:
+        pre, xs = refs
+    else:
+        *ends, xs, pre = (*refs[:3], *refs[5:], *refs[3:5])
     ch = shard.shape[0] // 4 - FOLD // 4
     store_windows(xs, *rows_of([shard[...]], ch))
-    pre = ends[0] if which == 0 else refs[-2]
     for pair in range(2):
         total = shard_rows(weights, which, xs, pair)
         pre[2 * pair] = part[2 * pair] + total[:, 0:128]
         pre[2 * pair + 1] = part[2 * pair + 1] + total[:, 128:256]
     if which == 1:
-        finish(step, pre, *ends, refs[-1])
+        cell, hid_out, cell_out, hid32, cell32, hid16, sent = ends
+        for y in range(4):
+            part = [pre[y, pl.ds(g, ch, stride=4), :] for g in range(3)]
+            c = sigmoid(part[1]) * cell[y * ch : (y + 1) * ch, :] + sigmoid(part[0]) * jnp.tanh(part[2])
+            cell32[pl.ds(y, ch, stride=4), :] = c
+        copy = pltpu.make_async_copy(cell32, cell_out, sent.at[0])
+        copy.start()
+        for y in range(4):
+            c = cell32[pl.ds(y, ch, stride=4), :]
+            hid32[pl.ds(y, ch, stride=4), :] = sigmoid(pre[y, pl.ds(3, ch, stride=4), :]) * jnp.tanh(c)
+        hid16[...] = hid32[...].astype(BF16)
+        other = pltpu.make_async_copy(hid16, hid_out, sent.at[1])
+        other.start()
+        copy.wait()
+        other.wait()
 
 
 def rim_strips(shards, ch):
@@ -410,14 +429,15 @@
     hid_out[4 * ch : 4 * ch + FOLD, :] = rim_fold(h)
 
 
-def call(kernel, outs, scratch, *args, far=0, us=1, same=None):
+def call(kernel, outs, scratch, *args, far=0, us=1, same=None, kept=0):
     return pl.pallas_call(
         kernel,
         out_shape=[jax.ShapeDtypeStruct(s, d) for s, d in outs],
         in_specs=[pl.BlockSpec(memory_space=pltpu.HBM)] * far
         + [pl.BlockSpec(memory_space=pltpu.VMEM)] * (len(args) - far),
-        out_specs=[pl.BlockSpec(memory_space=pltpu.VMEM)] * len(outs),
-        scratch_shapes=[pltpu.VMEM(s, d) for s, d in scratch] + ([pltpu.SemaphoreType.DMA((far,))] if far else []),
+        out_specs=[pl.BlockSpec(memory_space=pltpu.VMEM)] * (len(outs) - kept)
+        + [pl.BlockSpec(memory_space=pltpu.HBM)] * kept,
+        scratch_shapes=[pltpu.VMEM(s, d) for s, d in scratch] + ([pltpu.SemaphoreType.DMA((far + kept,))] if far + kept else []),
         input_output_aliases=same or {},
         cost_estimate=pl.CostEstimate(flops=int(us * 1e9), bytes_accessed=0, transcendentals=0),
         compiler_params=pltpu.CompilerParams(vmem_limit_bytes=24 << 20),
@@ -494,8 +514,9 @@
                 same, part, split, us=0.01,
             )
             field, cell = call(
-                functools.partial(shard_kernel, step, 1), outs, [((5, ch, 768), BF16), pre, hid32],
-                cross, part, split, cell, us=0.01,
+                functools.partial(shard_kernel, step, 1), outs,
+                [((5, ch, 768), BF16), pre, hid32, hid32, ((4 * ch, 128), BF16)], cross, part, split, cell,
+                us=0.01, kept=2,
             )
         elif paired:
             field, cell = call(

time: 23.6 us -> 23.6 us (level)
  no operation moved by 1% of the time
where the time goes in v6:
time: 23.6 us; the launch traced here: 23.5 us
  starting transfers between devices  10.7 us (45%)
  Pallas kernels  10.3 us (44%)
  waiting for transfers between devices  1.54 us (7%)
  between operations  0.82 us (3%)
    pallas_call x14, Pallas kernels, call(): pl.pallas_call(kernel, out_shape=[jax.ShapeDtypeStruct(s, d) for s, d in...  10.3 us
    ppermute x1, starting transfers between devices, shards(): lax.ppermute(to_right, 'lon', [(i, (i + 1) % n) for i in range(n)])  2.65 us
    ppermute x3, starting transfers between devices, shards(): lax.ppermute(field, 'chan', [(i, i ^ k) for i in range(shards)])  2.25 us
    ppermute x3, starting transfers between devices, shards(): lax.ppermute(strip, 'chan', [(i, i ^ k) for i in range(shards)])  2.17 us
    ppermute x1, starting transfers between devices, shards(): lax.ppermute(to_left, 'lon', [((i + 1) % n, i) for i in range(n)])  2.09 us
    ppermute x2, starting transfers between devices, others(): lax.ppermute(x, 'chan', [(i, i ^ k) for i in range(shards)])  1.57 us
    ppermute x2, waiting for transfers between devices, others(): lax.ppermute(x, 'chan', [(i, i ^ k) for i in range(shards)])  0.75 us
    ppermute x1, waiting for transfers between devices, onward(): lax.ppermute(same, 'chan', [(i, i ^ 1) for i in range(shards)])  0.51 us
  transfers between devices with their start and end apart: 11, of which 3 were waited for; matrix products, arithmetic and copies ran while one was open for 0% of the time, Pallas kernels for 24%

profile of v6, /device:TPU:0, one launch (start us, length us, event | category | flops | bytes accessed | tf_op | source)
XLA Modules:
  0.0 23.5 jit_solution(7458800973300539451)
XLA Ops:
  0.6 1.7 %shard_map.77 = (f32[24,128]{1,0:T(8,128)S(1)}, f32[24,128]{1,0:T(8,128)S(1)}, f32[256,128]{1,0:T(8,128)S(1)}, bf16[256,512]{1,0:T(8,128)(2,1)S(1)}, f32[4,256,128]{2,1,0:T(8,128)S(1)}) custom-call(bf16[256,128]{1,0:T(8,128)(2,1)} %bitcast.20, f32[256,128]{1,0:T(8,128)} %bitcast.15, bf16[128,128]{1,0:T(8,128)(2,1)} %bitcast.9, bf16[400,256]{1,0:T(8,128)(2,1)} %bitcast.13, ...), custom_call_target="tpu_custom_call" | custom-call | flops 20000000000 | tf_op jit(solution)/shard_map/pallas_call | solution.py:433
  2.3 0.0 copy-start.1
  2.4 0.0 copy-start.2
  2.4 0.0 copy-start.4
  2.4 0.0 copy-start
  2.4 2.7 %collective-permute-start = (f32[24,128]{1,0:T(8,128)S(1)}, f32[24,128]{1,0:T(8,128)S(1)}, u32[]{:S(2)}, u32[]{:S(2)}) collective-permute-start(f32[24,128]{1,0:T(8,128)S(1)} %get-tuple-element.18.to_right.refs_7_), channel_id=1, source_target_pairs={{0,4},{4,8},{8,12},{12,0},{1,5},{5,9},{9,13},{13,1},{2,6},{6,10},{... | collective-permute-start | bytes 36872 | tf_op jit(solution)/shard_map/ppermute | solution.py:470
  5.0 2.1 %collective-permute-start.1 = (f32[24,128]{1,0:T(8,128)S(1)}, f32[24,128]{1,0:T(8,128)S(1)}, u32[]{:S(2)}, u32[]{:S(2)}) collective-permute-start(f32[24,128]{1,0:T(8,128)S(1)} %get-tuple-element.19.to_left.refs_8_), channel_id=1, source_target_pairs={{4,0},{8,4},{12,8},{0,12},{5,1},{9,5},{13,9},{1,13},{6,2},{10,6},{... | collective-permute-start | bytes 36872 | tf_op jit(solution)/shard_map/ppermute | solution.py:471
  7.1 1.0 %collective-permute-start.7 = (bf16[256,128]{1,0:T(8,128)(2,1)S(1)}, bf16[256,128]{1,0:T(8,128)(2,1)S(1)}, u32[]{:S(2)}, u32[]{:S(2)}) collective-permute-start(bf16[256,128]{1,0:T(8,128)(2,1)S(1)} %shard_map.80.own), channel_id=1, source_target_pairs={{0,3},{1,2},{2,1},{3,0},{4,7},{5,6},{6,5},{7,4},{8,11},{9,10},{10,... | collective-permute-start | bytes 196616 | tf_op jit(solution)/shard_map/ppermute | solution.py:487
  8.2 1.2 %collective-permute-start.6 = (bf16[256,128]{1,0:T(8,128)(2,1)S(1)}, bf16[256,128]{1,0:T(8,128)(2,1)S(1)}, u32[]{:S(2)}, u32[]{:S(2)}) collective-permute-start(bf16[256,128]{1,0:T(8,128)(2,1)S(1)} %shard_map.80.own), channel_id=1, source_target_pairs={{0,2},{1,3},{2,0},{3,1},{4,6},{5,7},{6,4},{7,5},{8,10},{9,11},{10,... | collective-permute-start | bytes 196616 | tf_op jit(solution)/shard_map/ppermute | solution.py:487
  9.4 0.0 collective-permute-start.5
  9.4 0.0 collective-permute-done.came_left
  9.4 0.0 collective-permute-done.1.came_right
  9.4 0.0 copy-start.3
  9.4 1.4 %collective-permute-start.4 = (bf16[32,128]{1,0:T(8,128)(2,1)S(1)}, bf16[32,128]{1,0:T(8,128)(2,1)S(1)}, u32[]{:S(2)}, u32[]{:S(2)}) collective-permute-start(bf16[32,128]{1,0:T(8,128)(2,1)S(1)} %get-tuple-element.20.refs_0_), channel_id=1, source_target_pairs={{0,3},{1,2},{2,1},{3,0},{4,7},{5,6},{6,5},{7,4},{8,11},{9,10},{10,... | collective-permute-start | bytes 24584 | tf_op jit(solution)/shard_map/ppermute | solution.py:488
  10.9 0.7 %collective-permute-start.3 = (bf16[32,128]{1,0:T(8,128)(2,1)S(1)}, bf16[32,128]{1,0:T(8,128)(2,1)S(1)}, u32[]{:S(2)}, u32[]{:S(2)}) collective-permute-start(bf16[32,128]{1,0:T(8,128)(2,1)S(1)} %get-tuple-element.20.refs_0_), channel_id=1, source_target_pairs={{0,2},{1,3},{2,0},{3,1},{4,6},{5,7},{6,4},{7,5},{8,10},{9,11},{10,... | collective-permute-start | bytes 24584 | tf_op jit(solution)/shard_map/ppermute | solution.py:488
  11.6 0.0 collective-permute-done.5.other
  11.7 1.0 %shard_map.81.refs_0_.part = f32[4,256,128]{2,1,0:T(8,128)S(1)} custom-call(bf16[256,128]{1,0:T(8,128)(2,1)S(1)} %shard_map.80.own, bf16[256,128]{1,0:T(8,128)(2,1)S(1)} %collective-permute-done.5.other, f32[4,256,128]{2,1,0:T(8,128)S(1)} %get-tuple-element.27.driven, bf16[5,5,256,256]{3,2,1,0:T(8,128)(2,1)S(1)} %copy-done), custom_call_target="tpu_custom_call" | custom-call | flops 10000000 | tf_op jit(solution)/shard_map/pallas_call | solution.py:433
  12.7 0.5 %shard_map.82.refs_0_.refs_4_ = f32[256,128]{1,0:T(8,128)S(1)} custom-call(f32[24,128]{1,0:T(8,128)S(1)} %get-tuple-element.21.from_right.refs_9_, f32[24,128]{1,0:T(8,128)S(1)} %get-tuple-element.22.from_left.refs_10_, bf16[128,128]{1,0:T(8,128)(2,1)S(1)} %bitcast.11, bf16[256,512]{1,0:T(8,128)(2,1)S(1)} %get-tuple-element.25.weights, ...), custom_call_target="tpu_custom_call" | custom-call | flops 10000000 | tf_op jit(solution)/shard_map/pallas_call | solution.py:433
  13.1 0.0 collective-permute-done.6.same
  13.2 1.1 %shard_map.83 = (bf16[256,128]{1,0:T(8,128)(2,1)S(1)}, f32[256,128]{1,0:T(8,128)S(1)}) custom-call(bf16[256,128]{1,0:T(8,128)(2,1)S(1)} %collective-permute-done.6.same, bf16[256,128]{1,0:T(8,128)(2,1)S(1)} %collective-permute-done.7.cross, f32[4,256,128]{2,1,0:T(8,128)S(1)} %shard_map.81.refs_0_.part, f32[256,128]{1,0:T(8,128)S(1)} %bitcast.16, ...), custom_call_target="tpu_custom_call" | custom-call | flops 10000000 | tf_op jit(solution)/shard_map/pallas_call | solution.py:433
  14.2 0.0 collective-permute-done.4.refs_3_
  14.2 0.3 %collective-permute-done.3.refs_2_ = bf16[32,128]{1,0:T(8,128)(2,1)S(1)} collective-permute-done((bf16[32,128]{1,0:T(8,128)(2,1)S(1)}, bf16[32,128]{1,0:T(8,128)(2,1)S(1)}, u32[]{:S(2)}, u32[]{:S(2)}) %collective-permute-start.3) | collective-permute-done | bytes 8224 | tf_op jit(solution)/shard_map/ppermute | solution.py:488
  14.5 1.5 %shard_map.84 = (bf16[272,128]{1,0:T(8,128)(2,1)S(1)}, f32[256,128]{1,0:T(8,128)S(1)}) custom-call(bf16[32,128]{1,0:T(8,128)(2,1)S(1)} %get-tuple-element.20.refs_0_, bf16[32,128]{1,0:T(8,128)(2,1)S(1)} %collective-permute-done.2.refs_1_, bf16[32,128]{1,0:T(8,128)(2,1)S(1)} %collective-permute-done.3.refs_2_, ...), custom_call_target="tpu_custom_call" | custom-call | flops 10000000 | tf_op jit(solution)/shard_map/pallas_call | solution.py:433
  16.0 0.3 %collective-permute-start.9 = (bf16[272,128]{1,0:T(8,128)(2,1)S(1)}, bf16[272,128]{1,0:T(8,128)(2,1)S(1)}, u32[]{:S(2)}, u32[]{:S(2)}) collective-permute-start(bf16[272,128]{1,0:T(8,128)(2,1)S(1)} %get-tuple-element.30.before.own), channel_id=1, source_target_pairs={{0,1},{1,0},{2,3},{3,2},{4,5},{5,4},{6,7},{7,6},{8,9},{9,8},{10,11... | collective-permute-start | bytes 208904 | tf_op jit(solution)/shard_map/ppermute | solution.py:480
  16.3 1.3 %collective-permute-start.8 = (bf16[272,128]{1,0:T(8,128)(2,1)S(1)}, bf16[272,128]{1,0:T(8,128)(2,1)S(1)}, u32[]{:S(2)}, u32[]{:S(2)}) collective-permute-start(bf16[272,128]{1,0:T(8,128)(2,1)S(1)} %get-tuple-element.30.before.own), channel_id=1, source_target_pairs={{0,2},{1,3},{2,0},{3,1},{4,6},{5,7},{6,4},{7,5},{8,10},{9,11},{10,... | collective-permute-start | bytes 208904 | tf_op jit(solution)/shard_map/ppermute | solution.py:480
  17.6 0.5 %shard_map.85.driven = f32[4,256,128]{2,1,0:T(8,128)S(1)} custom-call(f32[24,128]{1,0:T(8,128)S(1)} %get-tuple-element.21.from_right.refs_9_, f32[24,128]{1,0:T(8,128)S(1)} %get-tuple-element.22.from_left.refs_10_, bf16[128,128]{1,0:T(8,128)(2,1)S(1)} %bitcast.12, bf16[256,512]{1,0:T(8,128)(2,1)S(1)} %get-tuple-element.25.weights, ...), custom_call_target="tpu_custom_call" | custom-call | flops 10000000 | tf_op jit(solution)/shard_map/pallas_call | solution.py:433
  18.2 1.1 %shard_map.86.before.part = f32[4,256,128]{2,1,0:T(8,128)S(1)} custom-call(bf16[272,128]{1,0:T(8,128)(2,1)S(1)} %get-tuple-element.30.before.own, bf16[272,128]{1,0:T(8,128)(2,1)S(1)} %collective-permute-done.9.other, f32[4,256,128]{2,1,0:T(8,128)S(1)} %shard_map.85.driven, bf16[5,5,256,256]{3,2,1,0:T(8,128)(2,1)S(1)} %copy-done), custom_call_target="tpu_custom_call" | custom-call | flops 10000000 | tf_op jit(solution)/shard_map/pallas_call | solution.py:433
  19.2 0.7 %shard_map.87.before.weights = bf16[2,15,256,128]{3,2,1,0:T(8,128)(2,1)S(1)} custom-call(bf16[5,5,256,256]{3,2,1,0:T(8,128)(2,1)S(1)} %copy-done, f32[4,256,128]{2,1,0:T(8,128)S(1)} %shard_map.86.before.part), custom_call_target="tpu_custom_call" | custom-call | flops 10000000 | tf_op jit(solution)/shard_map/pallas_call | solution.py:433
  19.9 0.7 %collective-permute-done.8.x = bf16[272,128]{1,0:T(8,128)(2,1)S(1)} collective-permute-done((bf16[272,128]{1,0:T(8,128)(2,1)S(1)}, bf16[272,128]{1,0:T(8,128)(2,1)S(1)}, u32[]{:S(2)}, u32[]{:S(2)}) %collective-permute-start.8) | collective-permute-done | bytes 69664 | tf_op jit(solution)/shard_map/ppermute | solution.py:480
  20.7 0.7 %shard_map.89.part = f32[4,256,128]{2,1,0:T(8,128)S(1)} custom-call(bf16[272,128]{1,0:T(8,128)(2,1)S(1)} %shard_map.88.shard, f32[4,256,128]{2,1,0:T(8,128)S(1)} %shard_map.86.before.part, bf16[2,15,256,128]{3,2,1,0:T(8,128)(2,1)S(1)} %shard_map.87.before.weights), custom_call_target="tpu_custom_call" | custom-call | flops 10000000 | tf_op jit(solution)/shard_map/pallas_call | solution.py:433
  21.4 0.5 %collective-permute-done.10.shard = bf16[272,128]{1,0:T(8,128)(2,1)S(1)} collective-permute-done((bf16[272,128]{1,0:T(8,128)(2,1)S(1)}, bf16[272,128]{1,0:T(8,128)(2,1)S(1)}, u32[]{:S(2)}, u32[]{:S(2)}) %collective-permute-start.10) | collective-permute-done | bytes 69664 | tf_op jit(solution)/shard_map/ppermute | solution.py:484
  21.9 1.5 %shard_map.90 = (bf16[256,128]{1,0:T(8,128)(2,1)}, f32[256,128]{1,0:T(8,128)}) custom-call(bf16[272,128]{1,0:T(8,128)(2,1)S(1)} %collective-permute-done.10.shard, f32[4,256,128]{2,1,0:T(8,128)S(1)} %shard_map.89.part, bf16[2,15,256,128]{3,2,1,0:T(8,128)(2,1)S(1)} %shard_map.87.before.weights, f32[256,128]{1,0:T(8,128)S(1)} %get-tuple-element.31.refs_0_), custom_call_target="tpu_custom_call" | custom-call | flops 10000000 | tf_op jit(solution)/shard_map/pallas_call | solution.py:433
  (14 shorter events, 0.1 us)
Async XLA Ops:
  2.3 9.3 %copy-start.1 = (bf16[2,16,4,128]{3,2,1,0:T(4,128)(2,1)S(1)}, bf16[2,16,4,128]{3,2,1,0:T(4,128)(2,1)}, u32[]{:S(2)}) copy-start(bf16[2,16,4,128]{3,2,1,0:T(4,128)(2,1)} %param.6) | copy-start | bytes 98308
  2.4 9.3 %copy-start.2 = (bf16[5,5,256,16]{2,3,1,0:T(8,128)(2,1)S(1)}, bf16[5,5,256,16]{2,3,1,0:T(8,128)(2,1)}, u32[]{:S(2)}) copy-start(bf16[5,5,256,16]{2,3,1,0:T(8,128)(2,1)} %param.9) | copy-start | bytes 614404
  2.4 9.3 %copy-start.4 = (f32[256]{0:T(256)S(1)}, f32[256]{0:T(256)}, u32[]{:S(2)}) copy-start(f32[256]{0:T(256)} %param.11) | copy-start | bytes 3076
  2.4 9.3 %copy-start = (bf16[5,5,256,256]{3,2,1,0:T(8,128)(2,1)S(1)}, bf16[5,5,256,256]{3,2,1,0:T(8,128)(2,1)}, u32[]{:S(2)}) copy-start(bf16[5,5,256,256]{3,2,1,0:T(8,128)(2,1)} %w.7) | copy-start | bytes 9830404
  2.4 7.0 %collective-permute-start = (f32[24,128]{1,0:T(8,128)S(1)}, f32[24,128]{1,0:T(8,128)S(1)}, u32[]{:S(2)}, u32[]{:S(2)}) collective-permute-start(f32[24,128]{1,0:T(8,128)S(1)} %get-tuple-element.18.to_right.refs_7_), channel_id=1, source_target_pairs={{0,4},{4,8},{8,12},{12,0},{1,5},{5,9},{9,13},{13,1},{2,6},{6,10},{... | collective-permute-start | bytes 36872 | tf_op jit(solution)/shard_map/ppermute | solution.py:470
  5.0 4.4 %collective-permute-start.1 = (f32[24,128]{1,0:T(8,128)S(1)}, f32[24,128]{1,0:T(8,128)S(1)}, u32[]{:S(2)}, u32[]{:S(2)}) collective-permute-start(f32[24,128]{1,0:T(8,128)S(1)} %get-tuple-element.19.to_left.refs_8_), channel_id=1, source_target_pairs={{4,0},{8,4},{12,8},{0,12},{5,1},{9,5},{13,9},{1,13},{6,2},{10,6},{... | collective-permute-start | bytes 36872 | tf_op jit(solution)/shard_map/ppermute | solution.py:471
  7.1 6.0 %collective-permute-start.7 = (bf16[256,128]{1,0:T(8,128)(2,1)S(1)}, bf16[256,128]{1,0:T(8,128)(2,1)S(1)}, u32[]{:S(2)}, u32[]{:S(2)}) collective-permute-start(bf16[256,128]{1,0:T(8,128)(2,1)S(1)} %shard_map.80.own), channel_id=1, source_target_pairs={{0,3},{1,2},{2,1},{3,0},{4,7},{5,6},{6,5},{7,4},{8,11},{9,10},{10,... | collective-permute-start | bytes 196616 | tf_op jit(solution)/shard_map/ppermute | solution.py:487
  8.2 5.0 %collective-permute-start.6 = (bf16[256,128]{1,0:T(8,128)(2,1)S(1)}, bf16[256,128]{1,0:T(8,128)(2,1)S(1)}, u32[]{:S(2)}, u32[]{:S(2)}) collective-permute-start(bf16[256,128]{1,0:T(8,128)(2,1)S(1)} %shard_map.80.own), channel_id=1, source_target_pairs={{0,2},{1,3},{2,0},{3,1},{4,6},{5,7},{6,4},{7,5},{8,10},{9,11},{10,... | collective-permute-start | bytes 196616 | tf_op jit(solution)/shard_map/ppermute | solution.py:487
  9.4 2.2 %collective-permute-start.5 = (bf16[256,128]{1,0:T(8,128)(2,1)S(1)}, bf16[256,128]{1,0:T(8,128)(2,1)S(1)}, u32[]{:S(2)}, u32[]{:S(2)}) collective-permute-start(bf16[256,128]{1,0:T(8,128)(2,1)S(1)} %shard_map.80.own), channel_id=1, source_target_pairs={{0,1},{1,0},{2,3},{3,2},{4,5},{5,4},{6,7},{7,6},{8,9},{9,8},{10,11... | collective-permute-start | bytes 196616 | tf_op jit(solution)/shard_map/ppermute | solution.py:487
  9.4 3.7 %copy-start.3 = (f32[64,4,128]{2,1,0:T(4,128)S(1)}, f32[64,4,128]{2,1,0:T(4,128)}, u32[]{:S(2)}) copy-start(f32[64,4,128]{2,1,0:T(4,128)} %param.8) | copy-start | bytes 393220
  9.4 4.8 %collective-permute-start.4 = (bf16[32,128]{1,0:T(8,128)(2,1)S(1)}, bf16[32,128]{1,0:T(8,128)(2,1)S(1)}, u32[]{:S(2)}, u32[]{:S(2)}) collective-permute-start(bf16[32,128]{1,0:T(8,128)(2,1)S(1)} %get-tuple-element.20.refs_0_), channel_id=1, source_target_pairs={{0,3},{1,2},{2,1},{3,0},{4,7},{5,6},{6,5},{7,4},{8,11},{9,10},{10,... | collective-permute-start | bytes 24584 | tf_op jit(solution)/shard_map/ppermute | solution.py:488
  10.9 3.7 %collective-permute-start.3 = (bf16[32,128]{1,0:T(8,128)(2,1)S(1)}, bf16[32,128]{1,0:T(8,128)(2,1)S(1)}, u32[]{:S(2)}, u32[]{:S(2)}) collective-permute-start(bf16[32,128]{1,0:T(8,128)(2,1)S(1)} %get-tuple-element.20.refs_0_), channel_id=1, source_target_pairs={{0,2},{1,3},{2,0},{3,1},{4,6},{5,7},{6,4},{7,5},{8,10},{9,11},{10,... | collective-permute-start | bytes 24584 | tf_op jit(solution)/shard_map/ppermute | solution.py:488
  11.6 2.9 %collective-permute-start.2 = (bf16[32,128]{1,0:T(8,128)(2,1)S(1)}, bf16[32,128]{1,0:T(8,128)(2,1)S(1)}, u32[]{:S(2)}, u32[]{:S(2)}) collective-permute-start(bf16[32,128]{1,0:T(8,128)(2,1)S(1)} %get-tuple-element.20.refs_0_), channel_id=1, source_target_pairs={{0,1},{1,0},{2,3},{3,2},{4,5},{5,4},{6,7},{7,6},{8,9},{9,8},{10,11... | collective-permute-start | bytes 24584 | tf_op jit(solution)/shard_map/ppermute | solution.py:488
  16.0 2.1 %collective-permute-start.9 = (bf16[272,128]{1,0:T(8,128)(2,1)S(1)}, bf16[272,128]{1,0:T(8,128)(2,1)S(1)}, u32[]{:S(2)}, u32[]{:S(2)}) collective-permute-start(bf16[272,128]{1,0:T(8,128)(2,1)S(1)} %get-tuple-element.30.before.own), channel_id=1, source_target_pairs={{0,1},{1,0},{2,3},{3,2},{4,5},{5,4},{6,7},{7,6},{8,9},{9,8},{10,11... | collective-permute-start | bytes 208904 | tf_op jit(solution)/shard_map/ppermute | solution.py:480
  16.3 4.3 %collective-permute-start.8 = (bf16[272,128]{1,0:T(8,128)(2,1)S(1)}, bf16[272,128]{1,0:T(8,128)(2,1)S(1)}, u32[]{:S(2)}, u32[]{:S(2)}) collective-permute-start(bf16[272,128]{1,0:T(8,128)(2,1)S(1)} %get-tuple-element.30.before.own), channel_id=1, source_target_pairs={{0,2},{1,3},{2,0},{3,1},{4,6},{5,7},{6,4},{7,5},{8,10},{9,11},{10,... | collective-permute-start | bytes 208904 | tf_op jit(solution)/shard_map/ppermute | solution.py:480
  20.7 1.3 %collective-permute-start.10 = (bf16[272,128]{1,0:T(8,128)(2,1)S(1)}, bf16[272,128]{1,0:T(8,128)(2,1)S(1)}, u32[]{:S(2)}, u32[]{:S(2)}) collective-permute-start(bf16[272,128]{1,0:T(8,128)(2,1)S(1)} %shard_map.88.shard), channel_id=1, source_target_pairs={{0,1},{1,0},{2,3},{3,2},{4,5},{5,4},{6,7},{7,6},{8,9},{9,8},{10,11... | collective-permute-start | bytes 208904 | tf_op jit(solution)/shard_map/ppermute | solution.py:484

commit v7 on v5

--- a/solution.py
+++ b/solution.py
@@ -322,7 +322,7 @@
         part[2 * pair + 1] = total[:, 128:256]
 
 
-def far_kernel(step, same, cross, part, cell, w, *refs):
+def far_kernel(step, cross, same, part, cell, w, *refs):
     ch = cell.shape[0] // 4
     hid_out, cell_out, xs, pre, hid32 = refs[-5:]
     at = first_channel(2 * ch, True)
@@ -396,7 +396,7 @@
     ch = cell.shape[0] // 4
     if len(blocks) == 4:
         first = lax.axis_index("chan") // 2 == 0
-        here, there = ordered(*blocks[:2]), ordered(*blocks[2:])
+        here, there = ordered(*blocks[:2]), ordered(*blocks[:1:-1])
         shards = [jnp.where(first, here[k], there[k]) for k in (0, 1)]
         shards += [jnp.where(first, there[k], here[k]) for k in (0, 1)]
     else:
@@ -500,7 +500,7 @@
         elif paired:
             field, cell = call(
                 functools.partial(far_kernel, step), outs, [windowed, pre, hid32],
-                same, cross, part, cell, w_hidden, *(rim or []), us=0.01,
+                cross, same, part, cell, w_hidden, *(rim or []), us=0.01,
             )
         else:
             gathered = lax.all_gather(field, "chan", axis=0)
@@ -511,7 +511,7 @@
         if not last:
             field, cell = call(
                 rim_kernel, [((4 * ch + FOLD, 128), BF16), ((4 * ch, 128), F32)], [((1, gate, 128), F32)],
-                *blocks, *rim, field, cell,
+                *blocks[:2], *blocks[:1:-1], *rim, field, cell,
                 to_right, to_left, from_right, from_left, w_hidden, us=0.01,
             )
             traveling = others(field) if paired else None

time: 23.6 us -> 23.7 us (level)
  starting transfers between devices: 10.7 us -> 11.1 us
  waiting for transfers between devices: 1.54 us -> 1.3 us
    ppermute x2, starting transfers between devices: 1.57 us -> 1.83 us  [others(): lax.ppermute(x, 'chan', [(i, i ^ k) for i in range(shards)])]
    ppermute x2, waiting for transfers between devices: 0.75 us -> 0.51 us  [others(): lax.ppermute(x, 'chan', [(i, i ^ k) for i in range(shards)])]
where the time goes in v7:
time: 23.7 us; the launch traced here: 23.5 us
  starting transfers between devices  11.1 us (47%)
  Pallas kernels  10.3 us (43%)
  waiting for transfers between devices  1.3 us (5%)
  between operations  0.81 us (3%)
    pallas_call x14, Pallas kernels, call(): pl.pallas_call(kernel, out_shape=[jax.ShapeDtypeStruct(s, d) for s, d in...  10.3 us
    ppermute x1, starting transfers between devices, shards(): lax.ppermute(to_right, 'lon', [(i, (i + 1) % n) for i in range(n)])  2.68 us
    ppermute x3, starting transfers between devices, shards(): lax.ppermute(field, 'chan', [(i, i ^ k) for i in range(shards)])  2.31 us
    ppermute x3, starting transfers between devices, shards(): lax.ppermute(strip, 'chan', [(i, i ^ k) for i in range(shards)])  2.21 us
    ppermute x1, starting transfers between devices, shards(): lax.ppermute(to_left, 'lon', [((i + 1) % n, i) for i in range(n)])  2.09 us
    ppermute x2, starting transfers between devices, others(): lax.ppermute(x, 'chan', [(i, i ^ k) for i in range(shards)])  1.83 us
    ppermute x2, waiting for transfers between devices, others(): lax.ppermute(x, 'chan', [(i, i ^ k) for i in range(shards)])  0.51 us
    ppermute x1, waiting for transfers between devices, onward(): lax.ppermute(same, 'chan', [(i, i ^ 1) for i in range(shards)])  0.51 us
  transfers between devices with their start and end apart: 11, of which 3 were waited for; matrix products, arithmetic and copies ran while one was open for 0% of the time, Pallas kernels for 24%

profile of v7, /device:TPU:0, one launch (start us, length us, event | category | flops | bytes accessed | tf_op | source)
XLA Modules:
  0.0 23.5 jit_solution(10946494964123530675)
XLA Ops:
  0.6 1.7 %shard_map.77 = (f32[24,128]{1,0:T(8,128)S(1)}, f32[24,128]{1,0:T(8,128)S(1)}, f32[256,128]{1,0:T(8,128)S(1)}, bf16[256,512]{1,0:T(8,128)(2,1)S(1)}, f32[4,256,128]{2,1,0:T(8,128)S(1)}) custom-call(bf16[256,128]{1,0:T(8,128)(2,1)} %bitcast.20, f32[256,128]{1,0:T(8,128)} %bitcast.15, bf16[128,128]{1,0:T(8,128)(2,1)} %bitcast.9, bf16[400,256]{1,0:T(8,128)(2,1)} %bitcast.13, ...), custom_call_target="tpu_custom_call" | custom-call | flops 20000000000 | tf_op jit(solution)/shard_map/pallas_call | solution.py:414
  2.3 0.0 copy-start.1
  2.3 0.0 copy-start.2
  2.3 0.0 copy-start.4
  2.4 0.0 copy-start
  2.4 2.7 %collective-permute-start = (f32[24,128]{1,0:T(8,128)S(1)}, f32[24,128]{1,0:T(8,128)S(1)}, u32[]{:S(2)}, u32[]{:S(2)}) collective-permute-start(f32[24,128]{1,0:T(8,128)S(1)} %get-tuple-element.18.to_right.refs_7_), channel_id=1, source_target_pairs={{0,4},{4,8},{8,12},{12,0},{1,5},{5,9},{9,13},{13,1},{2,6},{6,10},{... | collective-permute-start | bytes 36872 | tf_op jit(solution)/shard_map/ppermute | solution.py:450
  5.1 2.1 %collective-permute-start.1 = (f32[24,128]{1,0:T(8,128)S(1)}, f32[24,128]{1,0:T(8,128)S(1)}, u32[]{:S(2)}, u32[]{:S(2)}) collective-permute-start(f32[24,128]{1,0:T(8,128)S(1)} %get-tuple-element.19.to_left.refs_8_), channel_id=1, source_target_pairs={{4,0},{8,4},{12,8},{0,12},{5,1},{9,5},{13,9},{1,13},{6,2},{10,6},{... | collective-permute-start | bytes 36872 | tf_op jit(solution)/shard_map/ppermute | solution.py:451
  7.2 2.1 %collective-permute-start.7 = (bf16[256,128]{1,0:T(8,128)(2,1)S(1)}, bf16[256,128]{1,0:T(8,128)(2,1)S(1)}, u32[]{:S(2)}, u32[]{:S(2)}) collective-permute-start(bf16[256,128]{1,0:T(8,128)(2,1)S(1)} %shard_map.80.own), channel_id=1, source_target_pairs={{0,2},{1,3},{2,0},{3,1},{4,6},{5,7},{6,4},{7,5},{8,10},{9,11},{10,... | collective-permute-start | bytes 196616 | tf_op jit(solution)/shard_map/ppermute | solution.py:467
  9.3 0.0 collective-permute-start.6
  9.3 0.2 collective-permute-start.5
  9.5 0.0 collective-permute-done.came_left
  9.5 0.0 copy-start.3
  9.5 2.0 %collective-permute-start.4 = (bf16[32,128]{1,0:T(8,128)(2,1)S(1)}, bf16[32,128]{1,0:T(8,128)(2,1)S(1)}, u32[]{:S(2)}, u32[]{:S(2)}) collective-permute-start(bf16[32,128]{1,0:T(8,128)(2,1)S(1)} %get-tuple-element.20.refs_0_), channel_id=1, source_target_pairs={{0,2},{1,3},{2,0},{3,1},{4,6},{5,7},{6,4},{7,5},{8,10},{9,11},{10,... | collective-permute-start | bytes 24584 | tf_op jit(solution)/shard_map/ppermute | solution.py:468
  11.5 0.2 collective-permute-start.2
  11.7 1.0 %shard_map.81.refs_0_.part = f32[4,256,128]{2,1,0:T(8,128)S(1)} custom-call(bf16[256,128]{1,0:T(8,128)(2,1)S(1)} %shard_map.80.own, bf16[256,128]{1,0:T(8,128)(2,1)S(1)} %collective-permute-done.5.other, f32[4,256,128]{2,1,0:T(8,128)S(1)} %get-tuple-element.27.driven, bf16[5,5,256,256]{3,2,1,0:T(8,128)(2,1)S(1)} %copy-done), custom_call_target="tpu_custom_call" | custom-call | flops 10000000 | tf_op jit(solution)/shard_map/pallas_call | solution.py:414
  12.7 0.5 %shard_map.82.refs_0_.refs_4_ = f32[256,128]{1,0:T(8,128)S(1)} custom-call(f32[24,128]{1,0:T(8,128)S(1)} %get-tuple-element.21.from_right.refs_9_, f32[24,128]{1,0:T(8,128)S(1)} %get-tuple-element.22.from_left.refs_10_, bf16[128,128]{1,0:T(8,128)(2,1)S(1)} %bitcast.11, bf16[256,512]{1,0:T(8,128)(2,1)S(1)} %get-tuple-element.25.weights, ...), custom_call_target="tpu_custom_call" | custom-call | flops 10000000 | tf_op jit(solution)/shard_map/pallas_call | solution.py:414
  13.2 0.0 collective-permute-done.7.same
  13.2 1.1 %shard_map.83 = (bf16[256,128]{1,0:T(8,128)(2,1)S(1)}, f32[256,128]{1,0:T(8,128)S(1)}) custom-call(bf16[256,128]{1,0:T(8,128)(2,1)S(1)} %collective-permute-done.6.cross, bf16[256,128]{1,0:T(8,128)(2,1)S(1)} %collective-permute-done.7.same, f32[4,256,128]{2,1,0:T(8,128)S(1)} %shard_map.81.refs_0_.part, f32[256,128]{1,0:T(8,128)S(1)} %bitcast.16, ...), custom_call_target="tpu_custom_call" | custom-call | flops 10000000 | tf_op jit(solution)/shard_map/pallas_call | solution.py:414
  14.3 0.0 collective-permute-done.4.refs_3_
  14.3 0.3 %collective-permute-done.3.refs_2_ = bf16[32,128]{1,0:T(8,128)(2,1)S(1)} collective-permute-done((bf16[32,128]{1,0:T(8,128)(2,1)S(1)}, bf16[32,128]{1,0:T(8,128)(2,1)S(1)}, u32[]{:S(2)}, u32[]{:S(2)}) %collective-permute-start.3) | collective-permute-done | bytes 8224 | tf_op jit(solution)/shard_map/ppermute | solution.py:468
  14.6 1.5 %shard_map.84 = (bf16[272,128]{1,0:T(8,128)(2,1)S(1)}, f32[256,128]{1,0:T(8,128)S(1)}) custom-call(bf16[32,128]{1,0:T(8,128)(2,1)S(1)} %get-tuple-element.20.refs_0_, bf16[32,128]{1,0:T(8,128)(2,1)S(1)} %collective-permute-done.2.refs_1_, bf16[32,128]{1,0:T(8,128)(2,1)S(1)} %collective-permute-done.3.refs_2_, ...), custom_call_target="tpu_custom_call" | custom-call | flops 10000000 | tf_op jit(solution)/shard_map/pallas_call | solution.py:414
  16.1 0.1 collective-permute-start.9
  16.2 1.7 %collective-permute-start.8 = (bf16[272,128]{1,0:T(8,128)(2,1)S(1)}, bf16[272,128]{1,0:T(8,128)(2,1)S(1)}, u32[]{:S(2)}, u32[]{:S(2)}) collective-permute-start(bf16[272,128]{1,0:T(8,128)(2,1)S(1)} %get-tuple-element.30.before.own), channel_id=1, source_target_pairs={{0,2},{1,3},{2,0},{3,1},{4,6},{5,7},{6,4},{7,5},{8,10},{9,11},{10,... | collective-permute-start | bytes 208904 | tf_op jit(solution)/shard_map/ppermute | solution.py:460
  17.9 0.5 %shard_map.85.driven = f32[4,256,128]{2,1,0:T(8,128)S(1)} custom-call(f32[24,128]{1,0:T(8,128)S(1)} %get-tuple-element.21.from_right.refs_9_, f32[24,128]{1,0:T(8,128)S(1)} %get-tuple-element.22.from_left.refs_10_, bf16[128,128]{1,0:T(8,128)(2,1)S(1)} %bitcast.12, bf16[256,512]{1,0:T(8,128)(2,1)S(1)} %get-tuple-element.25.weights, ...), custom_call_target="tpu_custom_call" | custom-call | flops 10000000 | tf_op jit(solution)/shard_map/pallas_call | solution.py:414
  18.5 0.0 collective-permute-done.9.other
  18.5 1.1 %shard_map.86.before.part = f32[4,256,128]{2,1,0:T(8,128)S(1)} custom-call(bf16[272,128]{1,0:T(8,128)(2,1)S(1)} %get-tuple-element.30.before.own, bf16[272,128]{1,0:T(8,128)(2,1)S(1)} %collective-permute-done.9.other, f32[4,256,128]{2,1,0:T(8,128)S(1)} %shard_map.85.driven, bf16[5,5,256,256]{3,2,1,0:T(8,128)(2,1)S(1)} %copy-done), custom_call_target="tpu_custom_call" | custom-call | flops 10000000 | tf_op jit(solution)/shard_map/pallas_call | solution.py:414
  19.6 0.7 %shard_map.87.before.weights = bf16[2,15,256,128]{3,2,1,0:T(8,128)(2,1)S(1)} custom-call(bf16[5,5,256,256]{3,2,1,0:T(8,128)(2,1)S(1)} %copy-done, f32[4,256,128]{2,1,0:T(8,128)S(1)} %shard_map.86.before.part), custom_call_target="tpu_custom_call" | custom-call | flops 10000000 | tf_op jit(solution)/shard_map/pallas_call | solution.py:414
  20.3 0.5 %collective-permute-done.8.x = bf16[272,128]{1,0:T(8,128)(2,1)S(1)} collective-permute-done((bf16[272,128]{1,0:T(8,128)(2,1)S(1)}, bf16[272,128]{1,0:T(8,128)(2,1)S(1)}, u32[]{:S(2)}, u32[]{:S(2)}) %collective-permute-start.8) | collective-permute-done | bytes 69664 | tf_op jit(solution)/shard_map/ppermute | solution.py:460
  20.8 0.0 collective-permute-start.10
  20.8 0.7 %shard_map.89.part = f32[4,256,128]{2,1,0:T(8,128)S(1)} custom-call(bf16[272,128]{1,0:T(8,128)(2,1)S(1)} %shard_map.88.shard, f32[4,256,128]{2,1,0:T(8,128)S(1)} %shard_map.86.before.part, bf16[2,15,256,128]{3,2,1,0:T(8,128)(2,1)S(1)} %shard_map.87.before.weights), custom_call_target="tpu_custom_call" | custom-call | flops 10000000 | tf_op jit(solution)/shard_map/pallas_call | solution.py:414
  21.5 0.5 %collective-permute-done.10.shard = bf16[272,128]{1,0:T(8,128)(2,1)S(1)} collective-permute-done((bf16[272,128]{1,0:T(8,128)(2,1)S(1)}, bf16[272,128]{1,0:T(8,128)(2,1)S(1)}, u32[]{:S(2)}, u32[]{:S(2)}) %collective-permute-start.10) | collective-permute-done | bytes 69664 | tf_op jit(solution)/shard_map/ppermute | solution.py:464
  22.0 1.5 %shard_map.90 = (bf16[256,128]{1,0:T(8,128)(2,1)}, f32[256,128]{1,0:T(8,128)}) custom-call(bf16[272,128]{1,0:T(8,128)(2,1)S(1)} %collective-permute-done.10.shard, f32[4,256,128]{2,1,0:T(8,128)S(1)} %shard_map.89.part, bf16[2,15,256,128]{3,2,1,0:T(8,128)(2,1)S(1)} %shard_map.87.before.weights, f32[256,128]{1,0:T(8,128)S(1)} %get-tuple-element.31.refs_0_), custom_call_target="tpu_custom_call" | custom-call | flops 10000000 | tf_op jit(solution)/shard_map/pallas_call | solution.py:414
  (14 shorter events, 0.1 us)
Async XLA Ops:
  2.3 9.4 %copy-start.1 = (bf16[2,16,4,128]{3,2,1,0:T(4,128)(2,1)S(1)}, bf16[2,16,4,128]{3,2,1,0:T(4,128)(2,1)}, u32[]{:S(2)}) copy-start(bf16[2,16,4,128]{3,2,1,0:T(4,128)(2,1)} %param.6) | copy-start | bytes 98308
  2.3 9.4 %copy-start.2 = (bf16[5,5,256,16]{2,3,1,0:T(8,128)(2,1)S(1)}, bf16[5,5,256,16]{2,3,1,0:T(8,128)(2,1)}, u32[]{:S(2)}) copy-start(bf16[5,5,256,16]{2,3,1,0:T(8,128)(2,1)} %param.9) | copy-start | bytes 614404
  2.3 9.4 %copy-start.4 = (f32[256]{0:T(256)S(1)}, f32[256]{0:T(256)}, u32[]{:S(2)}) copy-start(f32[256]{0:T(256)} %param.11) | copy-start | bytes 3076
  2.4 9.4 %copy-start = (bf16[5,5,256,256]{3,2,1,0:T(8,128)(2,1)S(1)}, bf16[5,5,256,256]{3,2,1,0:T(8,128)(2,1)}, u32[]{:S(2)}) copy-start(bf16[5,5,256,256]{3,2,1,0:T(8,128)(2,1)} %w.7) | copy-start | bytes 9830404
  2.4 7.1 %collective-permute-start = (f32[24,128]{1,0:T(8,128)S(1)}, f32[24,128]{1,0:T(8,128)S(1)}, u32[]{:S(2)}, u32[]{:S(2)}) collective-permute-start(f32[24,128]{1,0:T(8,128)S(1)} %get-tuple-element.18.to_right.refs_7_), channel_id=1, source_target_pairs={{0,4},{4,8},{8,12},{12,0},{1,5},{5,9},{9,13},{13,1},{2,6},{6,10},{... | collective-permute-start | bytes 36872 | tf_op jit(solution)/shard_map/ppermute | solution.py:450
  5.1 4.4 %collective-permute-start.1 = (f32[24,128]{1,0:T(8,128)S(1)}, f32[24,128]{1,0:T(8,128)S(1)}, u32[]{:S(2)}, u32[]{:S(2)}) collective-permute-start(f32[24,128]{1,0:T(8,128)S(1)} %get-tuple-element.19.to_left.refs_8_), channel_id=1, source_target_pairs={{4,0},{8,4},{12,8},{0,12},{5,1},{9,5},{13,9},{1,13},{6,2},{10,6},{... | collective-permute-start | bytes 36872 | tf_op jit(solution)/shard_map/ppermute | solution.py:451
  7.2 6.0 %collective-permute-start.7 = (bf16[256,128]{1,0:T(8,128)(2,1)S(1)}, bf16[256,128]{1,0:T(8,128)(2,1)S(1)}, u32[]{:S(2)}, u32[]{:S(2)}) collective-permute-start(bf16[256,128]{1,0:T(8,128)(2,1)S(1)} %shard_map.80.own), channel_id=1, source_target_pairs={{0,2},{1,3},{2,0},{3,1},{4,6},{5,7},{6,4},{7,5},{8,10},{9,11},{10,... | collective-permute-start | bytes 196616 | tf_op jit(solution)/shard_map/ppermute | solution.py:467
  9.3 3.9 %collective-permute-start.6 = (bf16[256,128]{1,0:T(8,128)(2,1)S(1)}, bf16[256,128]{1,0:T(8,128)(2,1)S(1)}, u32[]{:S(2)}, u32[]{:S(2)}) collective-permute-start(bf16[256,128]{1,0:T(8,128)(2,1)S(1)} %shard_map.80.own), channel_id=1, source_target_pairs={{0,3},{1,2},{2,1},{3,0},{4,7},{5,6},{6,5},{7,4},{8,11},{9,10},{10,... | collective-permute-start | bytes 196616 | tf_op jit(solution)/shard_map/ppermute | solution.py:467
  9.3 2.2 %collective-permute-start.5 = (bf16[256,128]{1,0:T(8,128)(2,1)S(1)}, bf16[256,128]{1,0:T(8,128)(2,1)S(1)}, u32[]{:S(2)}, u32[]{:S(2)}) collective-permute-start(bf16[256,128]{1,0:T(8,128)(2,1)S(1)} %shard_map.80.own), channel_id=1, source_target_pairs={{0,1},{1,0},{2,3},{3,2},{4,5},{5,4},{6,7},{7,6},{8,9},{9,8},{10,11... | collective-permute-start | bytes 196616 | tf_op jit(solution)/shard_map/ppermute | solution.py:467
  9.5 3.7 %copy-start.3 = (f32[64,4,128]{2,1,0:T(4,128)S(1)}, f32[64,4,128]{2,1,0:T(4,128)}, u32[]{:S(2)}) copy-start(f32[64,4,128]{2,1,0:T(4,128)} %param.8) | copy-start | bytes 393220
  9.5 4.8 %collective-permute-start.4 = (bf16[32,128]{1,0:T(8,128)(2,1)S(1)}, bf16[32,128]{1,0:T(8,128)(2,1)S(1)}, u32[]{:S(2)}, u32[]{:S(2)}) collective-permute-start(bf16[32,128]{1,0:T(8,128)(2,1)S(1)} %get-tuple-element.20.refs_0_), channel_id=1, source_target_pairs={{0,2},{1,3},{2,0},{3,1},{4,6},{5,7},{6,4},{7,5},{8,10},{9,11},{10,... | collective-permute-start | bytes 24584 | tf_op jit(solution)/shard_map/ppermute | solution.py:468
  11.5 3.1 %collective-permute-start.3 = (bf16[32,128]{1,0:T(8,128)(2,1)S(1)}, bf16[32,128]{1,0:T(8,128)(2,1)S(1)}, u32[]{:S(2)}, u32[]{:S(2)}) collective-permute-start(bf16[32,128]{1,0:T(8,128)(2,1)S(1)} %get-tuple-element.20.refs_0_), channel_id=1, source_target_pairs={{0,3},{1,2},{2,1},{3,0},{4,7},{5,6},{6,5},{7,4},{8,11},{9,10},{10,... | collective-permute-start | bytes 24584 | tf_op jit(solution)/shard_map/ppermute | solution.py:468
  11.5 3.1 %collective-permute-start.2 = (bf16[32,128]{1,0:T(8,128)(2,1)S(1)}, bf16[32,128]{1,0:T(8,128)(2,1)S(1)}, u32[]{:S(2)}, u32[]{:S(2)}) collective-permute-start(bf16[32,128]{1,0:T(8,128)(2,1)S(1)} %get-tuple-element.20.refs_0_), channel_id=1, source_target_pairs={{0,1},{1,0},{2,3},{3,2},{4,5},{5,4},{6,7},{7,6},{8,9},{9,8},{10,11... | collective-permute-start | bytes 24584 | tf_op jit(solution)/shard_map/ppermute | solution.py:468
  16.1 2.4 %collective-permute-start.9 = (bf16[272,128]{1,0:T(8,128)(2,1)S(1)}, bf16[272,128]{1,0:T(8,128)(2,1)S(1)}, u32[]{:S(2)}, u32[]{:S(2)}) collective-permute-start(bf16[272,128]{1,0:T(8,128)(2,1)S(1)} %get-tuple-element.30.before.own), channel_id=1, source_target_pairs={{0,1},{1,0},{2,3},{3,2},{4,5},{5,4},{6,7},{7,6},{8,9},{9,8},{10,11... | collective-permute-start | bytes 208904 | tf_op jit(solution)/shard_map/ppermute | solution.py:460
  16.2 4.5 %collective-permute-start.8 = (bf16[272,128]{1,0:T(8,128)(2,1)S(1)}, bf16[272,128]{1,0:T(8,128)(2,1)S(1)}, u32[]{:S(2)}, u32[]{:S(2)}) collective-permute-start(bf16[272,128]{1,0:T(8,128)(2,1)S(1)} %get-tuple-element.30.before.own), channel_id=1, source_target_pairs={{0,2},{1,3},{2,0},{3,1},{4,6},{5,7},{6,4},{7,5},{8,10},{9,11},{10,... | collective-permute-start | bytes 208904 | tf_op jit(solution)/shard_map/ppermute | solution.py:460
  20.8 1.3 %collective-permute-start.10 = (bf16[272,128]{1,0:T(8,128)(2,1)S(1)}, bf16[272,128]{1,0:T(8,128)(2,1)S(1)}, u32[]{:S(2)}, u32[]{:S(2)}) collective-permute-start(bf16[272,128]{1,0:T(8,128)(2,1)S(1)} %shard_map.88.shard), channel_id=1, source_target_pairs={{0,1},{1,0},{2,3},{3,2},{4,5},{5,4},{6,7},{7,6},{8,9},{9,8},{10,11... | collective-permute-start | bytes 208904 | tf_op jit(solution)/shard_map/ppermute | solution.py:464
